TPU v7x, 32 devices: a whole 2x2x4 slice. The times are simulated.
32 devices in a mesh: prow: 4 (over y, core), pcol: 8 (over z, x).
Axes of the slice: x: 2, y: 2, z: 4, core: 2. Of those that a mesh axis runs over, the one named last changes fastest.
Arguments:
- assembly: float32 [4, 256, 2, 128, 128], P('prow', 'pcol'), may hold values from -6 to 6
- slot_tile: int32 [4, 256], P('prow', 'pcol'), may hold values from 0 to 255, as said below
- pivots: int32 [2, 128], replicated, may hold values from 0 to 8191, as said below
- inverses: float32 [2, 2, 128, 128], replicated, may hold values from -0.046875 to 0.046875
Outputs:
- factored: float32 [2, 8192, 2048], P(None, 'prow', 'pcol')
Inputs may be any that keep to these rules, and one draw needn't show every extreme that they name: `slot_tile`: row p lists tile ids t = i*16 + b, i the row tile among those of prow p and b the column tile; each of prow p's tiles appears in exactly one slot. A device's 32 slots hold at most 5 tiles whose column owner b % 8 is one index, and every device holds exactly 5 for some owner. `pivots`: entry j of panel k is either k*128 + j (no swap) or a row at or past 2*128; the rows named in one panel differ.
All inputs are finite; a program needn't handle non-finite values.
Results may differ from a plain program's by a relative error of at most 0.00013.
Values sent between devices are 32-bit elements; how exact they have to be, the bound alone decides.
No kernel may reach another device: no remote copies, remote signals or barrier semaphores. Data moves between devices by JAX's collectives and lax.ppermute only.
A program may use at most 128 MiB of HBM per device.

v0:
```python
import jax
import jax.numpy as jnp
from jax import lax
from jax.sharding import PartitionSpec as P

CBLK = 2


def spread(x, axis, root):
    mine = lax.axis_index(axis) == root
    return lax.psum(jnp.where(mine, x, jnp.zeros_like(x)), axis)


def product(left, right):
    return jnp.dot(left, right, precision=lax.Precision.HIGHEST, preferred_element_type=jnp.float32)


def complex_product(left, right):
    real = product(left[0], right[0]) - product(left[1], right[1])
    imag = product(left[0], right[1]) + product(left[1], right[0])
    return jnp.stack([real, imag])


def per_device(assembly, slot_tile, pivots, inverses):
    cols_n = lax.axis_size("pcol")
    rows_n = lax.axis_size("prow")
    my_col = lax.axis_index("pcol")
    my_row = lax.axis_index("prow")
    tiles = assembly[0]
    slot_count = tiles.shape[0]
    block = tiles.shape[-1]
    width_tiles = CBLK * cols_n
    capacity = (slot_count + cols_n - 1) // cols_n + 1
    ident = slot_tile[0]
    column_tile = ident % width_tiles
    target = column_tile % cols_n
    local_id = ident // width_tiles * CBLK + column_tile // cols_n
    onehot = (target[:, None] == jnp.arange(cols_n, dtype=jnp.int32)[None, :]).astype(jnp.int32)
    before = jnp.cumsum(onehot, axis=0) - onehot
    rank = jnp.sum(before * onehot, axis=1)
    position = target * capacity + rank
    outgoing = (
        jnp.zeros((cols_n * capacity,) + tiles.shape[1:], jnp.float32).at[position].set(tiles)
    )
    labels = jnp.full((cols_n * capacity,), float(slot_count), jnp.float32)
    labels = labels.at[position].set(local_id.astype(jnp.float32))
    arrived, arrived_ids = (
        lax.all_to_all(outgoing, "pcol", split_axis=0, concat_axis=0, tiled=True),
        lax.all_to_all(labels, "pcol", split_axis=0, concat_axis=0, tiled=True),
    )
    placed = jnp.zeros_like(tiles).at[arrived_ids.astype(jnp.int32)].set(arrived, mode="drop")
    row_tiles = slot_count // CBLK
    row_total = row_tiles * block
    matrix = placed.reshape(row_tiles, CBLK, 2, block, block).transpose(2, 0, 3, 1, 4)
    matrix = matrix.reshape(2, row_total, CBLK * block)
    row_global = jnp.arange(row_total, dtype=jnp.int32) // block * rows_n + my_row
    col_global = jnp.arange(CBLK * block, dtype=jnp.int32) // block * cols_n + my_col
    for panel in range(2):
        chosen = pivots[panel]
        owner = chosen // block % rows_n
        where_local = chosen // block // rows_n * block + chosen % block
        mine = owner == my_row
        moved = chosen != panel * block + jnp.arange(block, dtype=jnp.int32)
        picked = jnp.where(
            mine[None, :, None], matrix[:, jnp.clip(where_local, 0, row_total - 1), :], 0.0
        )
        own_top = matrix[:, :block, :]
        old_top = spread(own_top, "prow", panel)
        new_top = lax.psum(picked, "prow")
        target_rows = jnp.where(mine & moved, where_local, row_total)
        matrix = matrix.at[:, target_rows, :].set(old_top, mode="drop")
        matrix = matrix.at[:, :block, :].set(
            jnp.where(my_row == panel, new_top, matrix[:, :block, :])
        )
        factor_block = inverses[panel]
        lower = row_global > panel
        right = col_global > panel
        panel_cols = matrix[:, :, :block]
        factor_rows = spread(complex_product(panel_cols, factor_block), "pcol", panel)
        update = complex_product(factor_rows, new_top)
        keep = lower[:, None] & right[None, :]
        matrix = matrix - jnp.where(keep[None], update, 0.0)
        stored = jnp.where(
            lower[None, :, None] & (my_col == panel), factor_rows, matrix[:, :, :block]
        )
        matrix = matrix.at[:, :, :block].set(stored)
    return matrix


def solution(mesh):
    in_specs = (P("prow", "pcol", None, None, None), P("prow", "pcol"), P(), P())
    out_specs = P(None, "prow", "pcol")
    return jax.shard_map(
        per_device, mesh=mesh, in_specs=in_specs, out_specs=out_specs, check_vma=False
    )
```

profile of v0, /device:TPU:29, one launch (start us, length us, event | category | flops | bytes accessed | tf_op | source)
XLA Modules:
  0.0 557.2 jit_solution(16355667242996151915)
XLA Ops:
  9.6 5.5 all-to-all-start
  15.0 3.0 broadcast_in_dim.82
  18.0 8.4 %scatter_fusion = f32[40,2,128,128]{3,2,1,0:T(8,128)} fusion(f32[40,2,128,128]{3,2,1,0:T(8,128)} %broadcast_in_dim.82, s32[32]{0:T(128)S(1)} %fusion.60, f32[32,2,128,128]{3,2,1,0:T(8,128)} %bitcast.194), kind=kCustom, calls=%fused_computation.3 | custom fusion | bytes 12583040 | tf_op jit(solution)/shard_map/scatter | solution.py:43
  26.4 5.6 all-to-all-start.1
  32.2 114.7 %all-to-all-done.1 = f32[40,2,128,128]{3,2,1,0:T(8,128)} async-done(((f32[40,2,128,128]{3,2,1,0:T(8,128)}), f32[40,2,128,128]{3,2,1,0:T(8,128)}, u32[]{:S(2)}, u32[]{:S(2)}) %all-to-all-start.1) | async-done | bytes 5242912 | tf_op jit(solution)/shard_map/all_to_all | solution.py:48
  146.9 2.5 broadcast_in_dim.80
  149.4 11.0 %scatter_fusion.1 = f32[32,2,128,128]{3,2,1,0:T(8,128)} fusion(f32[32,2,128,128]{3,2,1,0:T(8,128)} %broadcast_in_dim.80, s32[40]{0:T(128)S(1)} %fusion.61, f32[40,2,128,128]{3,2,1,0:T(8,128)} %all-to-all-done.1), kind=kCustom, calls=%fused_computation.4 | custom fusion | bytes 15728800 | tf_op jit(solution)/shard_map/scatter | solution.py:51
  160.5 7.5 %copy.27 = f32[2,16,128,2,128]{4,3,2,1,0:T(2,128)} copy(f32[2,16,128,2,128]{4,2,0,3,1:T(8,128)} %bitcast.193) | data formatting | bytes 8388608 | tf_op jit(solution)/shard_map/transpose | solution.py:54
  168.0 6.4 %reshape.911 = f32[2,2048,256]{2,1,0:T(8,128)} reshape(f32[2,16,128,2,128]{4,3,2,1,0:T(2,128)} %copy.27) | data formatting | bytes 8388608 | tf_op jit(solution)/shard_map/reshape | solution.py:55
  174.4 8.7 %copy.28 = f32[2,2048,256]{2,0,1:T(2,128)} copy(f32[2,2048,256]{2,1,0:T(8,128)} %reshape.911) | data formatting | bytes 8388608 | tf_op jit(solution)/shard_map/reshape | solution.py:55
  184.8 3.1 gather_fusion
  189.0 31.1 %all-reduce.13.cloned.1.call-done = (f32[2,128,256]{2,1,0:T(8,128)}, f32[2,128,256]{2,1,0:T(8,128)}) async-done(((f32[2,128,256]{2,1,0:T(8,128)}, f32[2,128,256]{2,1,0:T(8,128)}), (f32[2,128,256]{2,1,0:T(8,128)}, f32[2,128,256]{2,1,0:T(8,128)})) %all-reduce.13.cloned.1.call-update) | async-done | bytes 524304 | tf_op jit(solution)/shard_map/psum | solution.py:11
  221.3 15.1 %scatter_fusion.2 = f32[2,2048,256]{2,0,1:T(2,128)} fusion(f32[2,2048,256]{2,0,1:T(2,128)} %copy.28, s32[128]{0:T(128)S(1)} %fusion.62, f32[128,2,256]{2,1,0:T(2,128)S(1)} %copy.29), kind=kCustom, calls=%fused_computation.5 | custom fusion | bytes 786944 | tf_op jit(solution)/shard_map/scatter | solution.py:71
  236.3 2.6 copy.33
  245.0 102.3 %all-reduce.7.cloned.1.call-done = f32[2,2048,128]{2,1,0:T(8,128)} async-done(((f32[2,2048,128]{2,1,0:T(8,128)}), f32[2,2048,128]{2,1,0:T(8,128)}) %all-reduce.7.cloned.1.call-update) | async-done | bytes 2097168 | tf_op jit(solution)/shard_map/psum | solution.py:11
  347.3 3.2 fusion.15
  350.5 3.0 fusion.14
  353.6 1.8 fusion.5
  355.4 1.8 fusion.4
  358.6 12.2 %copy.34 = f32[2,2048,256]{2,0,1:T(2,128)} copy(f32[2,2048,256]{2,1,0:T(8,128)S(1)} %fusion.11) | data formatting | bytes 8388608 | tf_op jit(solution)/shard_map/scatter | solution.py:86
  371.5 3.1 gather_fusion.1
  375.4 9.9 %all-reduce.9.cloned.1.call-start = ((), (), s32[]{:S(2)}) async-start(), calls=%async_computation.3 | async-start | bytes 4194304 | tf_op jit(solution)/shard_map/psum | solution.py:11
  385.3 22.5 %all-reduce.11.cloned.1.call-done = (f32[2,128,256]{2,1,0:T(8,128)}, f32[2,128,256]{2,1,0:T(8,128)}) async-done(((f32[2,128,256]{2,1,0:T(8,128)}, f32[2,128,256]{2,1,0:T(8,128)}), (f32[2,128,256]{2,1,0:T(8,128)}, f32[2,128,256]{2,1,0:T(8,128)})) %all-reduce.11.cloned.1.call-update) | async-done | bytes 524304 | tf_op jit(solution)/shard_map/psum | solution.py:11
  409.0 15.1 %scatter_fusion.3 = f32[2,2048,256]{2,0,1:T(2,128)} fusion(f32[2,2048,256]{2,0,1:T(2,128)} %copy.34, s32[128]{0:T(128)S(1)} %get-tuple-element.67, f32[128,2,256]{2,1,0:T(2,128)S(1)} %copy.35), kind=kCustom, calls=%fused_computation.6 | custom fusion | bytes 786944 | tf_op jit(solution)/shard_map/scatter | solution.py:71
  424.0 2.6 copy.39
  432.6 102.5 %all-reduce.9.cloned.1.call-done = f32[2,2048,128]{2,1,0:T(8,128)} async-done(((f32[2,2048,128]{2,1,0:T(8,128)}), f32[2,2048,128]{2,1,0:T(8,128)}) %all-reduce.9.cloned.1.call-update) | async-done | bytes 2097168 | tf_op jit(solution)/shard_map/psum | solution.py:11
  535.1 3.2 fusion.19
  538.3 3.0 fusion.18
  541.4 1.8 fusion.3
  543.2 1.8 fusion.2
  545.1 2.7 fusion.1
  547.7 2.8 fusion.10
  (73 shorter events, 23.1 us)
Async XLA Ops:
  9.6 16.8 %all-to-all-start = ((f32[8,5,1]{1,2,0:T(1,128)}), f32[8,5,1]{1,2,0:T(1,128)S(1)}, u32[]{:S(2)}, u32[]{:S(2)}) async-start(f32[8,5,1]{1,2,0:T(1,128)} %bitcast.4), calls=%async_computation | async-start | bytes 8192 | tf_op jit(solution)/shard_map/all_to_all | solution.py:49
  26.4 5.6 %copy-start.9 = (s32[2,128]{1,0:T(2,128)S(1)}, s32[2,128]{1,0:T(2,128)}, u32[]{:S(2)}) copy-start(s32[2,128]{1,0:T(2,128)} %param.14) | copy-start | bytes 3076
  26.4 120.5 %all-to-all-start.1 = ((f32[40,2,128,128]{3,2,1,0:T(8,128)}), f32[40,2,128,128]{3,2,1,0:T(8,128)}, u32[]{:S(2)}, u32[]{:S(2)}) async-start(f32[40,2,128,128]{3,2,1,0:T(8,128)} %scatter_fusion), calls=%async_computation.1 | async-start | bytes 10485760 | tf_op jit(solution)/shard_map/all_to_all | solution.py:48
  32.0 188.1 %all-reduce.13.cloned.1.call-start = ((), (), s32[]{:S(2)}) async-start(), calls=%async_computation.5 | async-start | bytes 1048576 | tf_op jit(solution)/shard_map/psum | solution.py:11
  188.7 158.6 %all-reduce.7.cloned.1.call-start = ((), (), s32[]{:S(2)}) async-start(), calls=%async_computation.2 | async-start | bytes 4194304 | tf_op jit(solution)/shard_map/psum | solution.py:11
  236.3 2.6 copy-start.6
  236.3 2.7 copy-start.8
  239.0 4.0 copy-start
  244.5 163.4 %all-reduce.11.cloned.1.call-start = ((), (), s32[]{:S(2)}) async-start(), calls=%async_computation.4 | async-start | bytes 1048576 | tf_op jit(solution)/shard_map/psum | solution.py:11
  347.3 6.3 %copy-start.4 = (f32[2,2048,128]{2,1,0:T(8,128)S(1)}, f32[2,2048,128]{2,1,0:T(8,128)}, u32[]{:S(2)}) copy-start(f32[2,2048,128]{2,1,0:T(8,128)} %all-reduce.7.cloned.1.call-done) | copy-start | bytes 6291460
  353.6 3.7 copy-start.1
  375.4 159.7 %all-reduce.9.cloned.1.call-start = ((), (), s32[]{:S(2)}) async-start(), calls=%async_computation.3 | async-start | bytes 4194304 | tf_op jit(solution)/shard_map/psum | solution.py:11
  424.0 2.6 copy-start.7
  426.7 4.0 copy-start.2
  535.1 6.3 %copy-start.5 = (f32[2,2048,128]{2,1,0:T(8,128)S(1)}, f32[2,2048,128]{2,1,0:T(8,128)}, u32[]{:S(2)}) copy-start(f32[2,2048,128]{2,1,0:T(8,128)} %all-reduce.9.cloned.1.call-done) | copy-start | bytes 6291460
  541.4 3.7 copy-start.3
Sparse Core Ops, SparseCore 0:
  188.8 31.2 all-reduce.12
  244.6 102.6 all-reduce.6
  375.5 32.2 all-reduce.10
  432.3 102.8 all-reduce.8
where the time goes:
time: 569 us; the launch traced here: 557 us
  waiting for transfers between devices  373 us (66%)
  local copies, waits for them, and re-layouts  105 us (18%)
  matrix products  27.6 us (5%)
  starting transfers between devices  21.2 us (4%)
  other arithmetic  16.5 us (3%)
  between operations  13.7 us (2%)
    psum x4, waiting for transfers between devices, spread(): return lax.psum(jnp.where(mine, x, jnp.zeros_like(x)), axis)  258 us
    all_to_all x1, waiting for transfers between devices, per_device(): lax.all_to_all(outgoing, 'pcol', split_axis=0, concat_axis=0, tiled=True)  115 us
    scatter x4, local copies, waits for them, and re-layouts, per_device(): matrix = matrix.at[:, target_rows, :].set(old_top, mode='drop')  35.3 us
    dot_general x16, matrix products, product(): jnp.dot(left, right, precision=lax.Precision.HIGHEST, preferred_element_t...  27.6 us
    reshape x2, local copies, waits for them, and re-layouts, per_device(): matrix = matrix.reshape(2, row_total, CBLK * block)  15.2 us
    scatter x1, local copies, waits for them, and re-layouts, per_device(): matrix = matrix.at[:, :, :block].set(stored)  12.2 us
  transfers between devices with their start and end apart: 6, of which 5 were waited for; matrix products, arithmetic and copies ran while one was open for 2% of the time, Pallas kernels for 0%

commit v1 on v0

v1 whole, which is shorter than its diff:
```python
import functools

import jax
import jax.numpy as jnp
from jax import lax
from jax.experimental import pallas as pl
from jax.experimental.pallas import tpu as pltpu
from jax.sharding import PartitionSpec as P

CBLK = 2
LINES = 2
F32 = jnp.float32
BF16 = jnp.bfloat16
VMEM_LIMIT = 48 * 1024 * 1024

ANY = pl.BlockSpec(memory_space=pl.ANY)
SMEM = pl.BlockSpec(memory_space=pltpu.SMEM)
VMEM = pl.BlockSpec(memory_space=pltpu.VMEM)


def params():
    return pltpu.CompilerParams(vmem_limit_bytes=VMEM_LIMIT)


def list_slots(ids_ref, pos, cnt, slots, cols_n, base):
    for o in range(cols_n + 1):
        cnt[o] = 0
    pos[cols_n * (base + 1)] = 0

    def one(j, carry):
        owner = lax.rem(ids_ref[j], cols_n)
        r = cnt[owner]
        cnt[owner] = r + 1
        pos[owner * (base + 1) + r] = j

        @pl.when(r >= base)
        def _():
            e = cnt[cols_n]

            @pl.when(e == 0)
            def _():
                pos[cols_n * (base + 1)] = j

            cnt[cols_n] = e + 1

        return carry

    lax.fori_loop(0, slots, one, 0)


def copy_listed(moves, sems):
    for n, (cond, src, dst) in enumerate(moves):

        @pl.when(cond)
        def _(n=n, src=src, dst=dst):
            pltpu.make_async_copy(src, dst, sems.at[n]).start()

    for n, (cond, src, dst) in enumerate(moves):

        @pl.when(cond)
        def _(n=n, src=src, dst=dst):
            pltpu.make_async_copy(src, dst, sems.at[n]).wait()


def pack_streams(tiles, ids, me, cols_n, base):
    slots = tiles.shape[0]
    one = tiles.shape[1:]

    def kernel(ids_ref, me_ref, tiles_ref, mine_ref, other_ref, extra_ref, pos, cnt, sems):
        list_slots(ids_ref, pos, cnt, slots, cols_n, base)
        line = lax.rem(me_ref[0], LINES)
        moves = []
        for ref, owner in ((mine_ref, line), (other_ref, LINES - 1 - line)):
            for r in range(base):
                moves.append((r < cnt[owner], tiles_ref.at[pos[owner * (base + 1) + r]], ref.at[r]))
        moves.append((cnt[cols_n] > 0, tiles_ref.at[pos[cols_n * (base + 1)]], extra_ref.at[0]))
        copy_listed(moves, sems)

    return pl.pallas_call(
        kernel,
        out_shape=(
            jax.ShapeDtypeStruct((base,) + one, F32),
            jax.ShapeDtypeStruct((base,) + one, F32),
            jax.ShapeDtypeStruct((1,) + one, F32),
        ),
        in_specs=[SMEM, SMEM, ANY],
        out_specs=(ANY, ANY, ANY),
        scratch_shapes=[
            pltpu.SMEM((cols_n * (base + 1) + 1,), jnp.int32),
            pltpu.SMEM((cols_n + 1,), jnp.int32),
            pltpu.SemaphoreType.DMA((2 * base + 1,)),
        ],
        compiler_params=params(),
        name="pack_streams",
    )(ids, me, tiles)


def pack_shifts(tiles, ids, me, cols_n, base):
    slots = tiles.shape[0]
    one = tiles.shape[1:]

    def kernel(ids_ref, me_ref, tiles_ref, *rest):
        outs, (pos, cnt, sems) = rest[: cols_n - 1], rest[cols_n - 1 :]
        list_slots(ids_ref, pos, cnt, slots, cols_n, base)
        moves = []
        for k in range(1, cols_n):
            owner = lax.rem(me_ref[0] + k, cols_n)
            for r in range(base):
                moves.append(
                    (
                        (r < cnt[owner]) & (owner >= LINES),
                        tiles_ref.at[pos[owner * (base + 1) + r]],
                        outs[k - 1].at[r],
                    )
                )
        copy_listed(moves, sems)

    return pl.pallas_call(
        kernel,
        out_shape=tuple(jax.ShapeDtypeStruct((base,) + one, F32) for _ in range(1, cols_n)),
        in_specs=[SMEM, SMEM, ANY],
        out_specs=tuple(ANY for _ in range(1, cols_n)),
        scratch_shapes=[
            pltpu.SMEM((cols_n * (base + 1) + 1,), jnp.int32),
            pltpu.SMEM((cols_n + 1,), jnp.int32),
            pltpu.SemaphoreType.DMA(((cols_n - 1) * base,)),
        ],
        compiler_params=params(),
        name="pack_shifts",
    )(ids, me, tiles)


def place(parts, tables, outs_n, name):
    one = parts[0].shape[1:]
    counts = [p.shape[0] for p in parts]
    table = jnp.concatenate(tables)
    total = sum(counts)
    size = outs_n[1]
    n_out = outs_n[0]

    def kernel(table_ref, *rest):
        ins, outs, sems = rest[: len(parts)], rest[len(parts) : -1], rest[-1]
        moves = []
        at = 0
        for part, count in zip(ins, counts):
            for n in range(count):
                where = table_ref[at]
                for o in range(n_out):
                    inside = (where >= o * size) & (where < (o + 1) * size)
                    moves.append((inside, part.at[n], outs[o].at[where - o * size], at))
                at += 1
        for cond, src, dst, s in moves:

            @pl.when(cond)
            def _(src=src, dst=dst, s=s):
                pltpu.make_async_copy(src, dst, sems.at[s]).start()

        for cond, src, dst, s in moves:

            @pl.when(cond)
            def _(src=src, dst=dst, s=s):
                pltpu.make_async_copy(src, dst, sems.at[s]).wait()

    return pl.pallas_call(
        kernel,
        out_shape=tuple(jax.ShapeDtypeStruct((size,) + one, F32) for _ in range(n_out)),
        in_specs=[SMEM] + [ANY] * len(parts),
        out_specs=tuple(ANY for _ in range(n_out)),
        scratch_shapes=[pltpu.SemaphoreType.DMA((total,))],
        compiler_params=params(),
        name=name,
    )(table, *parts)


def extract(parts, tables, source_rows, tiles_n, name):
    block = parts[0].shape[-1]
    counts = [p.shape[0] for p in parts]
    table = jnp.concatenate(tables)
    total = sum(counts)
    picks = source_rows.shape[0]

    def kernel(table_ref, rows_ref, *rest):
        ins, (held, picked, sems) = rest[: len(parts)], rest[len(parts) :]
        moves = []
        at = 0
        for part, count in zip(ins, counts):
            for n in range(count):
                where = table_ref[at]
                moves.append((where >= 0, part.at[n], held.at[where]))
                at += 1
        for n, (cond, src, dst) in enumerate(moves):

            @pl.when(cond)
            def _(n=n, src=src, dst=dst):
                pltpu.make_async_copy(src, dst, sems.at[n]).start()

        picked[...] = jnp.zeros_like(picked)
        for n, (cond, src, dst) in enumerate(moves):

            @pl.when(cond)
            def _(n=n, src=src, dst=dst):
                pltpu.make_async_copy(src, dst, sems.at[n]).wait()

        def one(j, carry):
            row = rows_ref[j]

            @pl.when(row >= 0)
            def _():
                tile, inner = row // block, lax.rem(row, block)
                for m in range(CBLK):
                    for c in range(2):
                        picked[2 * m + c, pl.ds(j, 1), :] = held[
                            tile * CBLK + m, c, pl.ds(inner, 1), :
                        ]

            return carry

        lax.fori_loop(0, picks, one, 0)

    return pl.pallas_call(
        kernel,
        out_shape=(
            jax.ShapeDtypeStruct((tiles_n, 2, block, block), F32),
            jax.ShapeDtypeStruct((2 * CBLK, picks, block), F32),
        ),
        in_specs=[SMEM, SMEM] + [ANY] * len(parts),
        out_specs=(VMEM, VMEM),
        scratch_shapes=[pltpu.SemaphoreType.DMA((total,))],
        compiler_params=params(),
        name=name,
    )(table, source_rows, *parts)


def exchange(picked, top, my_row, rows_n):
    total = picked
    step = 1
    while step < rows_n:
        total = total + lax.ppermute(total, "prow", [(p, p ^ step) for p in range(rows_n)])
        step *= 2
    held = top
    step = 2
    while step < rows_n:
        got = lax.ppermute(held, "prow", [(p, p + step) for p in range(step)])
        held = jnp.where((my_row >= step) & (my_row < 2 * step), got, held)
        step *= 2
    other = lax.ppermute(held, "prow", [(p, p ^ 1) for p in range(rows_n)])
    even = my_row % 2 == 0
    old = jnp.stack([jnp.where(even, held, other), jnp.where(even, other, held)])
    return total, old


def replace_rows(targets_ref, old_ref, held, block, picks):
    def one(j, carry):
        row = targets_ref[j]

        @pl.when(row >= 0)
        def _():
            tile, inner = row // block, lax.rem(row, block)
            half, at = j // block, lax.rem(j, block)
            for m in range(CBLK):
                for c in range(2):
                    held[tile * CBLK + m, c, pl.ds(inner, 1), :] = old_ref[
                        half, m, c, pl.ds(at, 1), :
                    ]

        return carry

    lax.fori_loop(0, picks, one, 0)


def split(x):
    high = x.astype(BF16)
    return high, (x - high.astype(F32)).astype(BF16)


def dot3(x, w_high, w_low):
    high, low = split(x)
    return (
        jnp.dot(high, w_high, preferred_element_type=F32)
        + jnp.dot(high, w_low, preferred_element_type=F32)
        + jnp.dot(low, w_high, preferred_element_type=F32)
    )


def store_complex(high_ref, low_ref, row, col, re, im):
    k, n = re.shape
    for r, c, value in ((0, 0, re), (0, 1, im), (1, 0, -im), (1, 1, re)):
        high, low = split(value)
        rows, cols = pl.ds(row + r * k, k), pl.ds(col + c * n, n)
        high_ref[rows, cols] = high
        low_ref[rows, cols] = low


def panel_factors(held, new, old, inverses, targets, my_row):
    block = held.shape[-1]
    row_tiles = held.shape[0] // CBLK
    picks = targets.shape[0]

    def kernel(tgt, row_ref, held_in, new_ref, old_ref, inv_ref, out_ref, top_ref, held_ref, *w):
        held_ref[...] = held_in[...]
        replace_rows(tgt, old_ref, held_ref, block, picks)
        i0h, i0l, i1h, i1l, uh, ul = w
        store_complex(i0h, i0l, 0, 0, inv_ref[0, 0], inv_ref[0, 1])
        store_complex(i1h, i1l, 0, 0, inv_ref[1, 0], inv_ref[1, 1])
        store_complex(uh, ul, 0, 0, new_ref[2, :block], new_ref[3, :block])

        @pl.when(row_ref[0] == 1)
        def _():
            for m in range(CBLK):
                for c in range(2):
                    held_ref[m, c] = new_ref[2 * m + c, block:]

        lower = dot3(
            jnp.concatenate([new_ref[0, block:], new_ref[1, block:]], axis=1), i0h[...], i0l[...]
        )
        top_ref[0], top_ref[1] = lower[:, :block], lower[:, block:]

        def one(i, carry):
            x0 = jnp.concatenate([held_ref[i * CBLK, 0], held_ref[i * CBLK, 1]], axis=1)
            x1 = jnp.concatenate([held_ref[i * CBLK + 1, 0], held_ref[i * CBLK + 1, 1]], axis=1)
            l0 = dot3(x0, i0h[...], i0l[...])
            l1 = dot3(x1 - dot3(l0, uh[...], ul[...]), i1h[...], i1l[...])
            out_ref[i, 0], out_ref[i, 1] = l0[:, :block], l0[:, block:]
            out_ref[i, 2], out_ref[i, 3] = l1[:, :block], l1[:, block:]
            return carry

        lax.fori_loop(0, row_tiles, one, 0)

    wide = pltpu.VMEM((2 * block, 2 * block), BF16)
    return pl.pallas_call(
        kernel,
        out_shape=(
            jax.ShapeDtypeStruct((row_tiles, 4, block, block), F32),
            jax.ShapeDtypeStruct((2, block, block), F32),
        ),
        in_specs=[SMEM, SMEM, VMEM, VMEM, VMEM, VMEM],
        out_specs=(VMEM, VMEM),
        scratch_shapes=[pltpu.VMEM(held.shape, F32)] + [wide] * 6,
        compiler_params=params(),
        name="panel_factors",
    )(targets, my_row, held, new, old, inverses)


def update(held, new, old, lower, lower_top, targets, my_row, my_col, rows_n):
    block = held.shape[-1]
    row_tiles = held.shape[0] // CBLK
    picks = targets.shape[0]

    def kernel(tgt, row_ref, col_ref, held_in, new_ref, old_ref, low_ref, top_ref, out_ref, held_ref, wh, wl):
        held_ref[...] = held_in[...]
        replace_rows(tgt, old_ref, held_ref, block, picks)
        for m in range(CBLK):
            store_complex(wh, wl, 0, 2 * m * block, new_ref[2 * m, :block], new_ref[2 * m + 1, :block])
        top = jnp.concatenate([top_ref[0], top_ref[1]], axis=1)
        first = dot3(top, wh[: 2 * block, :], wl[: 2 * block, :])
        for m in range(CBLK):
            re = new_ref[2 * m, block:] - first[:, 2 * m * block : (2 * m + 1) * block]
            im = new_ref[2 * m + 1, block:] - first[:, (2 * m + 1) * block : (2 * m + 2) * block]
            store_complex(wh, wl, 2 * block, 2 * m * block, re, im)

            @pl.when(row_ref[0] == 1)
            def _(m=m, re=re, im=im):
                out_ref[0, :block, m * block : (m + 1) * block] = re
                out_ref[1, :block, m * block : (m + 1) * block] = im

            @pl.when(row_ref[0] == 0)
            def _(m=m):
                for c in range(2):
                    out_ref[c, :block, m * block : (m + 1) * block] = new_ref[2 * m + c, :block]

        def one(i, carry):
            row_tile = i * rows_n + row_ref[0]

            @pl.when(row_tile >= 2)
            def _():
                x = jnp.concatenate([low_ref[i, n] for n in range(4)], axis=1)
                y = dot3(x, wh[...], wl[...])
                rows = pl.ds(pl.multiple_of(i * block, block), block)
                for m in range(CBLK):
                    for c in range(2):
                        at = (2 * m + c) * block
                        out_ref[c, rows, m * block : (m + 1) * block] = (
                            held_ref[i * CBLK + m, c] - y[:, at : at + block]
                        )

            for panel in range(2):

                @pl.when((col_ref[0] == panel) & (row_tile > panel))
                def _(panel=panel):
                    rows = pl.ds(pl.multiple_of(i * block, block), block)
                    for c in range(2):
                        out_ref[c, rows, :block] = low_ref[i, 2 * panel + c]

            return carry

        lax.fori_loop(0, row_tiles, one, 0)

    return pl.pallas_call(
        kernel,
        out_shape=jax.ShapeDtypeStruct((2, row_tiles * block, CBLK * block), F32),
        in_specs=[SMEM] * 3 + [VMEM] * 5,
        out_specs=VMEM,
        scratch_shapes=[
            pltpu.VMEM(held.shape, F32),
            pltpu.VMEM((4 * block, 4 * block), BF16),
            pltpu.VMEM((4 * block, 4 * block), BF16),
        ],
        compiler_params=params(),
        name="update",
    )(targets, my_row, my_col, held, new, old, lower, lower_top)


def per_device(assembly, slot_tile, pivots, inverses):
    cols_n = lax.axis_size("pcol")
    rows_n = lax.axis_size("prow")
    my_col = lax.axis_index("pcol")
    my_row = lax.axis_index("prow")
    tiles = assembly[0]
    slots = tiles.shape[0]
    block = tiles.shape[-1]
    width = CBLK * cols_n
    row_tiles = slots // CBLK
    base = (slots + cols_n - 1) // cols_n
    excess_max = slots // (base + 1)
    depth = cols_n // LINES
    line, level = my_col % LINES, my_col // LINES
    me = my_col.astype(jnp.int32).reshape(1)
    me_row = my_row.astype(jnp.int32).reshape(1)
    ids = slot_tile[0]

    def shift(x, k, keep=lambda d: True):
        pairs = [(i, (i + k) % cols_n) for i in range(cols_n)]
        return lax.ppermute(x, "pcol", [(a, b) for a, b in pairs if keep(b)])

    def swap(x):
        return lax.ppermute(x, "pcol", [(i, i ^ 1) for i in range(cols_n)])

    def chain(x):
        ups, downs = [], []
        up = down = x
        for t in range(1, depth):
            up = lax.ppermute(
                up, "pcol", [(i, i + LINES) for i in range((t - 1) * LINES, cols_n - LINES)]
            )
            down = lax.ppermute(
                down, "pcol", [(i, i - LINES) for i in range(LINES, cols_n - (t - 1) * LINES)]
            )
            ups.append(up)
            downs.append(down)
        return ups, downs

    mine, other, extra = pack_streams(tiles, ids, me, cols_n, base)
    partner = swap(other)
    ups_m, downs_m = chain(mine)
    ups_e, downs_e = chain(extra)
    ups_p, downs_p = chain(partner)
    shifted = pack_shifts(tiles, ids, me, cols_n, base)
    arrived = [shift(shifted[k - 1], k, lambda d: d >= LINES) for k in range(1, cols_n)]

    near = [ids] + [shift(ids, k) for k in range(1, cols_n)]
    order = jnp.arange(cols_n, dtype=jnp.int32)
    sources = (my_col - order) % cols_n
    all_ids = jnp.stack(near)
    all_ids = jnp.sum(
        jnp.where(order[:, None, None] == sources[None, :, None], all_ids[None], 0), axis=1
    )
    owner = all_ids % cols_n
    slot_order = jnp.arange(slots, dtype=jnp.int32)
    earlier = slot_order[None, :] < slot_order[:, None]
    rank = jnp.sum(((owner[:, :, None] == owner[:, None, :]) & earlier[None]).astype(jnp.int32), axis=2)
    over = rank >= base
    over_rank = jnp.sum((over[:, None, :] & earlier[None]).astype(jnp.int32), axis=2)
    local_id = all_ids // width * CBLK + all_ids % width // cols_n
    most = jnp.max(jnp.sum(over.astype(jnp.int32), axis=1))
    step = 1
    most = jnp.broadcast_to(most, (8, 128))
    while step < rows_n:
        most = jnp.maximum(most, lax.ppermute(most, "prow", [(p, p ^ step) for p in range(rows_n)]))
        step *= 2

    def stream_table(stream):
        hit = (
            (owner[:, None, :] == stream)
            & ~over[:, None, :]
            & (rank[:, None, :] == jnp.arange(base, dtype=jnp.int32)[None, :, None])
        )
        return jnp.sum(jnp.where(hit, local_id[:, None, :] + 1, 0), axis=2) - 1

    def excess_table(stream):
        hit = (
            (owner[:, None, :] == stream)
            & over[:, None, :]
            & (over_rank[:, None, :] == jnp.arange(excess_max, dtype=jnp.int32)[None, :, None])
        )
        return jnp.sum(jnp.where(hit, local_id[:, None, :] + 1, 0), axis=2) - 1

    def at_source(table, source, valid):
        row = jnp.sum(jnp.where(order[:, None] == source, table, 0), axis=0)
        return jnp.where(valid, row, -1)

    line_extra = jnp.concatenate(ups_e[::-1] + [extra] + downs_e)
    line_extra = lax.dynamic_slice_in_dim(line_extra, depth - 1 - level, depth, axis=0)
    cross_extra = swap(line_extra)

    def gather_rest():
        def nth(e):
            hit = (order[:, None] == my_col) & over & (over_rank == e)
            return jnp.sum(jnp.where(hit, slot_order[None, :], 0))

        rest = jnp.stack([lax.dynamic_index_in_dim(tiles, nth(e), 0, False) for e in range(1, excess_max)])
        return lax.all_gather(rest, "pcol").reshape((-1,) + tiles.shape[1:])

    def no_rest():
        return jnp.zeros((cols_n * (excess_max - 1),) + tiles.shape[1:], F32)

    rest = lax.cond(most[0, 0] > 1, gather_rest, no_rest)

    def by_column(table):
        return jnp.where(table >= 0, table % CBLK * row_tiles + table // CBLK, -1)

    line_table = by_column(stream_table(line))
    line_over = by_column(excess_table(line))
    other_line = LINES - 1 - line
    parts, tables = [mine, partner], [
        at_source(line_table, my_col, True),
        at_source(line_table, level * LINES + other_line, True),
    ]
    for t in range(1, depth):
        for got, source_level in ((ups_m, level - t), (downs_m, level + t)):
            parts.append(got[t - 1])
            valid = (source_level >= 0) & (source_level < depth)
            tables.append(at_source(line_table, source_level * LINES + line, valid))
        for got, source_level in ((ups_p, level - t), (downs_p, level + t)):
            parts.append(got[t - 1])
            valid = (source_level >= 0) & (source_level < depth)
            tables.append(at_source(line_table, source_level * LINES + other_line, valid))
    levels = jnp.arange(depth, dtype=jnp.int32)

    def firsts(table, which):
        return jnp.sum(
            jnp.where(order[None, :] == (levels * LINES + which)[:, None], table[None, :, 0], 0), axis=1
        )

    parts += [line_extra, cross_extra, rest]
    tables += [firsts(line_over, line), firsts(line_over, other_line), line_over[:, 1:].reshape(-1)]
    panel_mine, column_rest = place(parts, tables, (CBLK, row_tiles), "place_streams")
    panel_other = swap(panel_mine)

    picks = jnp.arange(2 * block, dtype=jnp.int32)
    first, second = pivots[0], pivots[1]
    same = (second[:, None] == first[None, :]) & (first[None, :] >= 2 * block)
    chained = jnp.sum(jnp.where(same, picks[None, :block], 0), axis=1)
    second_source = jnp.where(jnp.any(same, axis=1), chained, second)
    wanted = jnp.concatenate([first, second_source])
    named = jnp.concatenate([first, second])

    def local_row(row, keep):
        ours = (row // block % rows_n == my_row) & keep
        return jnp.where(ours, row // block // rows_n * block + row % block, -1)

    source_rows = local_row(wanted, True)
    targets = local_row(named, named != picks)

    tile_order = jnp.arange(row_tiles, dtype=jnp.int32) * CBLK
    held_p, picked_p = extract(
        [panel_mine, panel_other], [tile_order + line, tile_order + other_line], source_rows, slots, "panel_rows"
    )
    new_p, old_p = exchange(picked_p, held_p[:CBLK], my_row, rows_n)
    lower, lower_top = panel_factors(held_p, new_p, old_p, inverses, targets, me_row)

    own_table, own_over = stream_table(my_col), excess_table(my_col)
    gathered = my_col < LINES
    here = (owner == my_col) & (order[:, None] == my_col)
    self_table = jnp.max(jnp.where(here, local_id, -1), axis=0)
    parts, tables = [tiles], [jnp.where(gathered, -1, self_table)]
    for k in range(1, cols_n):
        parts.append(arrived[k - 1])
        tables.append(at_source(own_table, (my_col - k) % cols_n, ~gathered))
    foreign = ~gathered & (order[:, None] != my_col)
    own_over = jnp.where(foreign, own_over, -1)
    parts += [line_extra, cross_extra, rest, panel_mine, column_rest]
    tables += [firsts(own_over, line), firsts(own_over, other_line), own_over[:, 1:].reshape(-1)]
    tables += [jnp.where(gathered, tile_order, -1), jnp.where(gathered, tile_order + 1, -1)]
    held, picked = extract(parts, tables, source_rows, slots, "own_rows")
    new, old = exchange(picked, held[:CBLK], my_row, rows_n)
    return update(held, new, old, lower, lower_top, targets, me_row, me, rows_n)


def solution(mesh):
    in_specs = (P("prow", "pcol", None, None, None), P("prow", "pcol"), P(), P())
    out_specs = P(None, "prow", "pcol")
    return jax.shard_map(
        per_device, mesh=mesh, in_specs=in_specs, out_specs=out_specs, check_vma=False
    )
```

time: 569 us -> 366 us (0.64); the launches traced: 557 us -> 363 us
  waiting for transfers between devices: 373 us -> 109 us
  Pallas kernels: 0 us -> 127 us
  local copies, waits for them, and re-layouts: 105 us -> 22.8 us
  starting transfers between devices: 21.2 us -> 78.4 us
  matrix products: 27.6 us -> 0 us
  other arithmetic: 16.5 us -> 10.1 us
    psum x4 -> x0, waiting for transfers between devices: 258 us -> none  [spread(): return lax.psum(jnp.where(mine, x, jnp.zeros_like(x)), axis)]
    pallas_call x0 -> x7, Pallas kernels: none -> 127 us  [the longest x1 66.3 us: place(): pl.pallas_call(kernel, out_shape=tuple((jax.ShapeDtypeStruct((size,) + on...]
    all_to_all x2 -> x0, waiting for transfers between devices: 115 us -> none  [the longest x1 115 us: per_device(): lax.all_to_all(outgoing, 'pcol', split_axis=0, concat_axis=0, tiled=True)]
    ppermute x0 -> x45, waiting for transfers between devices: none -> 109 us  [the longest x14 55.7 us: shift(): return lax.ppermute(x, 'pcol', [(a, b) for a, b in pairs if keep(b)])]
    ppermute x0 -> x45, starting transfers between devices: none -> 78.4 us  [the longest x9 23.5 us: chain(): lax.ppermute(down, 'pcol', [(i, i - LINES) for i in range(LINES, cols_n -...]
    scatter x8 -> x0, local copies, waits for them, and re-layouts: 67.6 us -> none  [the longest x4 35.3 us: per_device(): matrix = matrix.at[:, target_rows, :].set(old_top, mode='drop')]
    dot_general x16 -> x0, matrix products: 27.6 us -> none  [product(): jnp.dot(left, right, precision=lax.Precision.HIGHEST, preferred_element_t...]
    unnamed x20 -> x60, local copies, waits for them, and re-layouts: 0.05 us -> 15.4 us
  transfers between devices with their start and end apart: 6 -> 45, of which waited for: 5 -> 14; matrix products, arithmetic and copies ran while one was open for 2% -> 5% of each run, Pallas kernels for 0% -> 26%
where the time goes in v1:
time: 366 us; the launch traced here: 363 us
  Pallas kernels  127 us (35%)
  waiting for transfers between devices  109 us (30%)
  starting transfers between devices  78.4 us (21%)
  local copies, waits for them, and re-layouts  22.8 us (6%)
  between operations  15.4 us (4%)
  other arithmetic  10.1 us (3%)
    pallas_call x1, Pallas kernels, place(): pl.pallas_call(kernel, out_shape=tuple((jax.ShapeDtypeStruct((size,) + on...  66.3 us
    ppermute x14, waiting for transfers between devices, shift(): return lax.ppermute(x, 'pcol', [(a, b) for a, b in pairs if keep(b)])  55.7 us
    ppermute x9, waiting for transfers between devices, chain(): lax.ppermute(up, 'pcol', [(i, i + LINES) for i in range((t - 1) * LINES,...  24.7 us
    ppermute x9, starting transfers between devices, chain(): lax.ppermute(down, 'pcol', [(i, i - LINES) for i in range(LINES, cols_n -...  23.5 us
    pallas_call x2, Pallas kernels, extract(): pl.pallas_call(kernel, out_shape=(jax.ShapeDtypeStruct((tiles_n, 2, block...  23.1 us
    ppermute x14, starting transfers between devices, shift(): return lax.ppermute(x, 'pcol', [(a, b) for a, b in pairs if keep(b)])  22.9 us
    ppermute x4, waiting for transfers between devices, exchange(): lax.ppermute(total, 'prow', [(p, p ^ step) for p in range(rows_n)])  18.9 us
    pallas_call x1, Pallas kernels, panel_factors(): pl.pallas_call(kernel, out_shape=(jax.ShapeDtypeStruct((row_tiles, 4, blo...  16.5 us
  transfers between devices with their start and end apart: 45, of which 14 were waited for; matrix products, arithmetic and copies ran while one was open for 5% of the time, Pallas kernels for 26%

profile of v1, /device:TPU:29, one launch (start us, length us, event | category | flops | bytes accessed | tf_op | source)
XLA Modules:
  0.0 363.1 jit_solution(14854208754606187131)
XLA Ops:
  7.7 2.2 collective-permute-start.2
  10.1 2.2 collective-permute-start.4
  14.6 3.2 pack_shifts.1
  23.6 2.9 pack_streams.1
  29.7 4.0 %collective-permute-start.17 = (f32[1,2,128,128]{3,2,1,0:T(8,128)S(1)}, f32[1,2,128,128]{3,2,1,0:T(8,128)S(1)}, u32[]{:S(2)}, u32[]{:S(2)}) collective-permute-start(f32[1,2,128,128]{3,2,1,0:T(8,128)S(1)} %get-tuple-element.59), channel_id=1, source_target_pairs={{2,0},{3,1},{4,2},{5,3},{6,4},{7,5},{10,8},{11,9},{12,10},{13,11},... | collective-permute-start | bytes 393224 | tf_op jit(solution)/shard_map/ppermute | solution.py:445
  37.9 3.4 collective-permute-start.21
  44.2 7.6 %collective-permute-start.25 = (f32[4,2,128,128]{3,2,1,0:T(8,128)S(1)}, f32[4,2,128,128]{3,2,1,0:T(8,128)S(1)}, u32[]{:S(2)}, u32[]{:S(2)}) collective-permute-start(f32[4,2,128,128]{3,2,1,0:T(8,128)S(1)} %get-tuple-element.60.rest_0_), channel_id=1, source_target_pairs={{2,0},{3,1},{4,2},{5,3},{6,4},{7,5},{10,8},{11,9},{12,10},{13,11},... | collective-permute-start | bytes 1572872 | tf_op jit(solution)/shard_map/ppermute | solution.py:445
  54.5 4.7 %collective-permute-start.27 = (f32[4,2,128,128]{3,2,1,0:T(8,128)S(1)}, f32[4,2,128,128]{3,2,1,0:T(8,128)S(1)}, u32[]{:S(2)}, u32[]{:S(2)}) collective-permute-start(f32[4,2,128,128]{3,2,1,0:T(8,128)S(1)} %collective-permute-done.23.rest_1_), channel_id=1, source_target_pairs={{2,0},{3,1},{4,2},{5,3},{6,4},{7,5},{10,8},{11,9},{12,10},{13,11},... | collective-permute-start | bytes 1572872 | tf_op jit(solution)/shard_map/ppermute | solution.py:445
  64.0 5.7 %collective-permute-done.26.rest_4_ = f32[4,2,128,128]{3,2,1,0:T(8,128)S(1)} collective-permute-done((f32[4,2,128,128]{3,2,1,0:T(8,128)S(1)}, f32[4,2,128,128]{3,2,1,0:T(8,128)S(1)}, u32[]{:S(2)}, u32[]{:S(2)}) %collective-permute-start.26) | collective-permute-done | bytes 524320 | tf_op jit(solution)/shard_map/ppermute | solution.py:442
  70.9 2.8 collective-permute-done.27.rest_5_
  75.8 2.4 collective-permute-done.22
  83.8 8.5 %collective-permute-done.30.rest_8_ = f32[4,2,128,128]{3,2,1,0:T(8,128)} collective-permute-done((f32[4,2,128,128]{3,2,1,0:T(8,128)S(1)}, f32[4,2,128,128]{3,2,1,0:T(8,128)}, u32[]{:S(2)}, u32[]{:S(2)}) %collective-permute-start.30) | collective-permute-done | bytes 524320 | tf_op jit(solution)/shard_map/ppermute | solution.py:442
  97.1 3.0 conditional.1
  97.2 3.0 broadcast.507
  100.1 3.1 collective-permute-start.7
  106.0 8.6 %collective-permute-done.34.rest_12_ = f32[4,2,128,128]{3,2,1,0:T(8,128)} collective-permute-done((f32[4,2,128,128]{3,2,1,0:T(8,128)}, f32[4,2,128,128]{3,2,1,0:T(8,128)}, u32[]{:S(2)}, u32[]{:S(2)}) %collective-permute-start.34) | collective-permute-done | bytes 524320 | tf_op jit(solution)/shard_map/ppermute | solution.py:442
  114.7 4.4 %collective-permute-start.10 = (f32[4,2,128,128]{3,2,1,0:T(8,128)}, f32[4,2,128,128]{3,2,1,0:T(8,128)}, u32[]{:S(2)}, u32[]{:S(2)}) collective-permute-start(f32[4,2,128,128]{3,2,1,0:T(8,128)} %copy-done.21), channel_id=1, source_target_pairs={{0,4},{1,5},{2,6},{3,7},{6,2},{7,3},{8,12},{9,13},{10,14},{11,15},... | collective-permute-start | bytes 1572872 | tf_op jit(solution)/shard_map/ppermute | solution.py:433
  122.3 66.3 %place_streams.1 = (f32[16,2,128,128]{3,2,1,0:T(8,128)}, f32[16,2,128,128]{3,2,1,0:T(8,128)}) custom-call(s32[104]{0:T(128)S(1)} %concatenate.22.table_ref, f32[4,2,128,128]{3,2,1,0:T(8,128)S(1)} %get-tuple-element.60.rest_0_, f32[4,2,128,128]{3,2,1,0:T(8,128)S(1)} %collective-permute-done.23.rest_1_, ...), custom_call_target="tpu_custom_call" | custom-call | tf_op jit(solution)/shard_map/place_streams/pallas_call | solution.py:164
  192.4 1.9 collective-permute-start.12
  194.3 1.9 collective-permute-start.13
  196.5 15.5 %collective-permute-done.11.rest_5_ = f32[4,2,128,128]{3,2,1,0:T(8,128)S(1)} collective-permute-done((f32[4,2,128,128]{3,2,1,0:T(8,128)}, f32[4,2,128,128]{3,2,1,0:T(8,128)S(1)}, u32[]{:S(2)}, u32[]{:S(2)}) %collective-permute-start.11) | collective-permute-done | bytes 524320 | tf_op jit(solution)/shard_map/ppermute | solution.py:433
  212.8 13.4 %collective-permute-done.12.rest_6_ = f32[4,2,128,128]{3,2,1,0:T(8,128)} collective-permute-done((f32[4,2,128,128]{3,2,1,0:T(8,128)}, f32[4,2,128,128]{3,2,1,0:T(8,128)}, u32[]{:S(2)}, u32[]{:S(2)}) %collective-permute-start.12) | collective-permute-done | bytes 524320 | tf_op jit(solution)/shard_map/ppermute | solution.py:433
  226.2 26.8 %collective-permute-done.13.rest_7_ = f32[4,2,128,128]{3,2,1,0:T(8,128)} collective-permute-done((f32[4,2,128,128]{3,2,1,0:T(8,128)}, f32[4,2,128,128]{3,2,1,0:T(8,128)}, u32[]{:S(2)}, u32[]{:S(2)}) %collective-permute-start.13) | collective-permute-done | bytes 524320 | tf_op jit(solution)/shard_map/ppermute | solution.py:433
  256.1 10.6 %own_rows.1 = (f32[32,2,128,128]{3,2,1,0:T(8,128)}, f32[4,256,128]{2,1,0:T(8,128)S(1)}) custom-call(s32[140]{0:T(256)S(1)} %concatenate.19.table_ref, s32[256]{0:T(256)S(1)} %get-tuple-element.123.rows_ref, f32[32,2,128,128]{3,2,1,0:T(8,128)} %bitcast.43, f32[4,2,128,128]{3,2,1,0:T(8,128)S(1)} %collective-permute-done.7.rest_1_, ...), custom_call_target="tpu_custom_call" | custom-call | tf_op jit(solution)/shard_map/own_rows/pallas_call | solution.py:220
  266.7 6.3 %collective-permute-start.36 = (f32[4,256,128]{2,1,0:T(8,128)S(1)}, f32[4,256,128]{2,1,0:T(8,128)}, u32[]{:S(2)}, u32[]{:S(2)}) collective-permute-start(f32[4,256,128]{2,1,0:T(8,128)S(1)} %get-tuple-element.65), channel_id=1, source_target_pairs={{0,8},{8,0},{16,24},{24,16},{1,9},{9,1},{17,25},{25,17},{2,10},{10... | collective-permute-start | bytes 1572872 | tf_op jit(solution)/shard_map/ppermute | solution.py:238
  275.4 12.5 %panel_rows.1 = (f32[32,2,128,128]{3,2,1,0:T(8,128)}, f32[4,256,128]{2,1,0:T(8,128)S(1)}) custom-call(s32[32]{0:T(128)S(1)} %pad_add_fusion.2.table_ref, s32[256]{0:T(256)S(1)} %get-tuple-element.123.rows_ref, f32[16,2,128,128]{3,2,1,0:T(8,128)S(1)} %copy-done, f32[16,2,128,128]{3,2,1,0:T(8,128)S(1)} %collective-permute-done.40.rest_1_), custom_call_target="tpu_custom_call" | custom-call | tf_op jit(solution)/shard_map/panel_rows/pallas_call | solution.py:220
  293.0 3.0 collective-permute-start.37
  296.0 4.1 %collective-permute-done.43 = f32[2,2,128,128]{3,2,1,0:T(8,128)S(1)} collective-permute-done((f32[2,2,128,128]{3,2,1,0:T(8,128)S(1)}, f32[2,2,128,128]{3,2,1,0:T(8,128)S(1)}, u32[]{:S(2)}, u32[]{:S(2)}) %collective-permute-start.43) | collective-permute-done | bytes 262176 | tf_op jit(solution)/shard_map/ppermute | solution.py:243
  303.5 7.9 %collective-permute-done.37 = f32[4,256,128]{2,1,0:T(8,128)S(1)} collective-permute-done((f32[4,256,128]{2,1,0:T(8,128)S(1)}, f32[4,256,128]{2,1,0:T(8,128)S(1)}, u32[]{:S(2)}, u32[]{:S(2)}) %collective-permute-start.37) | collective-permute-done | bytes 524320 | tf_op jit(solution)/shard_map/ppermute | solution.py:238
  311.5 11.1 %collective-permute-done.42 = f32[4,256,128]{2,1,0:T(8,128)S(1)} collective-permute-done((f32[4,256,128]{2,1,0:T(8,128)S(1)}, f32[4,256,128]{2,1,0:T(8,128)S(1)}, u32[]{:S(2)}, u32[]{:S(2)}) %collective-permute-start.42) | collective-permute-done | bytes 524320 | tf_op jit(solution)/shard_map/ppermute | solution.py:238
  322.7 16.5 %panel_factors.1 = (f32[16,4,128,128]{3,2,1,0:T(8,128)S(1)}, f32[2,128,128]{2,1,0:T(8,128)S(1)}) custom-call(s32[256]{0:T(256)S(1)} %get-tuple-element.124.tgt, s32[1]{0:T(128)} %bitcast.2.row_ref, f32[32,2,128,128]{3,2,1,0:T(8,128)} %get-tuple-element.66.held_in, f32[4,256,128]{2,1,0:T(8,128)S(1)} %add.339.new_ref, ...), custom_call_target="tpu_custom_call" | custom-call | tf_op jit(solution)/shard_map/panel_factors/pallas_call | solution.py:330
  341.0 15.2 %update.1 = f32[2,2048,256]{2,1,0:T(8,128)} custom-call(s32[256]{0:T(256)S(1)} %get-tuple-element.124.tgt, s32[1]{0:T(128)} %bitcast.2.row_ref, s32[1]{0:T(128)} %bitcast.3.me_ref.col_ref, f32[32,2,128,128]{3,2,1,0:T(8,128)S(1)} %copy-done.1, f32[4,256,128]{2,1,0:T(8,128)S(1)} %add.332.new_ref, f32[2,2,2,128,128]{4,3,2,1,0:T(8,128)S(1)} %pad_maximum_fusion.old_ref, ...), custom_call_target="tpu_custom_call" | custom-call | tf_op jit(solution)/shard_map/update/pallas_call | solution.py:398
  (221 shorter events, 66.1 us)
Async XLA Ops:
  6.5 20.5 %collective-permute-start = (s32[32]{0:T(128)}, s32[32]{0:T(128)S(1)}, u32[]{:S(2)}, u32[]{:S(2)}) collective-permute-start(s32[32]{0:T(128)} %bitcast.32), channel_id=1, source_target_pairs={{0,1},{1,2},{2,3},{3,4},{4,5},{5,6},{6,7},{7,0},{8,9},{9,10},{10,1... | collective-permute-start | bytes 392 | tf_op jit(solution)/shard_map/ppermute | solution.py:433
  7.7 19.6 %collective-permute-start.1 = (s32[32]{0:T(128)}, s32[32]{0:T(128)S(1)}, u32[]{:S(2)}, u32[]{:S(2)}) collective-permute-start(s32[32]{0:T(128)} %bitcast.33), channel_id=1, source_target_pairs={{0,2},{1,3},{2,4},{3,5},{4,6},{5,7},{6,0},{7,1},{8,10},{9,11},{10,... | collective-permute-start | bytes 392 | tf_op jit(solution)/shard_map/ppermute | solution.py:433
  7.7 20.6 %collective-permute-start.2 = (s32[32]{0:T(128)}, s32[32]{0:T(128)S(1)}, u32[]{:S(2)}, u32[]{:S(2)}) collective-permute-start(s32[32]{0:T(128)} %bitcast.34), channel_id=1, source_target_pairs={{0,3},{1,4},{2,5},{3,6},{4,7},{5,0},{6,1},{7,2},{8,11},{9,12},{10,... | collective-permute-start | bytes 392 | tf_op jit(solution)/shard_map/ppermute | solution.py:433
  10.0 19.7 %collective-permute-start.3 = (s32[32]{0:T(128)}, s32[32]{0:T(128)S(1)}, u32[]{:S(2)}, u32[]{:S(2)}) collective-permute-start(s32[32]{0:T(128)} %bitcast.35), channel_id=1, source_target_pairs={{0,4},{1,5},{2,6},{3,7},{4,0},{5,1},{6,2},{7,3},{8,12},{9,13},{10,... | collective-permute-start | bytes 392 | tf_op jit(solution)/shard_map/ppermute | solution.py:433
  10.1 23.6 %collective-permute-start.4 = (s32[32]{0:T(128)}, s32[32]{0:T(128)S(1)}, u32[]{:S(2)}, u32[]{:S(2)}) collective-permute-start(s32[32]{0:T(128)} %bitcast.36), channel_id=1, source_target_pairs={{0,5},{1,6},{2,7},{3,0},{4,1},{5,2},{6,3},{7,4},{8,13},{9,14},{10,... | collective-permute-start | bytes 392 | tf_op jit(solution)/shard_map/ppermute | solution.py:433
  33.7 19.5 %collective-permute-start.23 = (f32[4,2,128,128]{3,2,1,0:T(8,128)S(1)}, f32[4,2,128,128]{3,2,1,0:T(8,128)S(1)}, u32[]{:S(2)}, u32[]{:S(2)}) collective-permute-start(f32[4,2,128,128]{3,2,1,0:T(8,128)S(1)} %get-tuple-element.61), channel_id=1, source_target_pairs={{0,1},{1,0},{2,3},{3,2},{4,5},{5,4},{6,7},{7,6},{8,9},{9,8},{10,11... | collective-permute-start | bytes 1572872 | tf_op jit(solution)/shard_map/ppermute | solution.py:436
  34.2 26.4 %collective-permute-start.24 = (f32[4,2,128,128]{3,2,1,0:T(8,128)S(1)}, f32[4,2,128,128]{3,2,1,0:T(8,128)S(1)}, u32[]{:S(2)}, u32[]{:S(2)}) collective-permute-start(f32[4,2,128,128]{3,2,1,0:T(8,128)S(1)} %get-tuple-element.60.rest_0_), channel_id=1, source_target_pairs={{0,2},{1,3},{2,4},{3,5},{4,6},{5,7},{8,10},{9,11},{10,12},{11,13},... | collective-permute-start | bytes 1572872 | tf_op jit(solution)/shard_map/ppermute | solution.py:442
  44.2 18.3 %collective-permute-start.25 = (f32[4,2,128,128]{3,2,1,0:T(8,128)S(1)}, f32[4,2,128,128]{3,2,1,0:T(8,128)S(1)}, u32[]{:S(2)}, u32[]{:S(2)}) collective-permute-start(f32[4,2,128,128]{3,2,1,0:T(8,128)S(1)} %get-tuple-element.60.rest_0_), channel_id=1, source_target_pairs={{2,0},{3,1},{4,2},{5,3},{6,4},{7,5},{10,8},{11,9},{12,10},{13,11},... | collective-permute-start | bytes 1572872 | tf_op jit(solution)/shard_map/ppermute | solution.py:445
  53.2 16.5 %collective-permute-start.26 = (f32[4,2,128,128]{3,2,1,0:T(8,128)S(1)}, f32[4,2,128,128]{3,2,1,0:T(8,128)S(1)}, u32[]{:S(2)}, u32[]{:S(2)}) collective-permute-start(f32[4,2,128,128]{3,2,1,0:T(8,128)S(1)} %collective-permute-done.23.rest_1_), channel_id=1, source_target_pairs={{0,2},{1,3},{2,4},{3,5},{4,6},{5,7},{8,10},{9,11},{10,12},{11,13},... | collective-permute-start | bytes 1572872 | tf_op jit(solution)/shard_map/ppermute | solution.py:442
  54.5 19.2 %collective-permute-start.27 = (f32[4,2,128,128]{3,2,1,0:T(8,128)S(1)}, f32[4,2,128,128]{3,2,1,0:T(8,128)S(1)}, u32[]{:S(2)}, u32[]{:S(2)}) collective-permute-start(f32[4,2,128,128]{3,2,1,0:T(8,128)S(1)} %collective-permute-done.23.rest_1_), channel_id=1, source_target_pairs={{2,0},{3,1},{4,2},{5,3},{6,4},{7,5},{10,8},{11,9},{12,10},{13,11},... | collective-permute-start | bytes 1572872 | tf_op jit(solution)/shard_map/ppermute | solution.py:445
  59.8 15.4 %collective-permute-start.19 = (f32[1,2,128,128]{3,2,1,0:T(8,128)S(1)}, f32[1,2,128,128]{3,2,1,0:T(8,128)S(1)}, u32[]{:S(2)}, u32[]{:S(2)}) collective-permute-start(f32[1,2,128,128]{3,2,1,0:T(8,128)S(1)} %collective-permute-done.18), channel_id=1, source_target_pairs={{2,0},{3,1},{10,8},{11,9},{18,16},{19,17},{26,24},{27,25}} | collective-permute-start | bytes 393224 | tf_op jit(solution)/shard_map/ppermute | solution.py:445
  60.6 20.4 %collective-permute-start.28 = (f32[4,2,128,128]{3,2,1,0:T(8,128)S(1)}, f32[4,2,128,128]{3,2,1,0:T(8,128)}, u32[]{:S(2)}, u32[]{:S(2)}) collective-permute-start(f32[4,2,128,128]{3,2,1,0:T(8,128)S(1)} %collective-permute-done.24.rest_2_), channel_id=1, source_target_pairs={{2,4},{3,5},{4,6},{5,7},{10,12},{11,13},{12,14},{13,15},{18,20},{1... | collective-permute-start | bytes 1572872 | tf_op jit(solution)/shard_map/ppermute | solution.py:442
  62.5 19.8 %collective-permute-start.29 = (f32[4,2,128,128]{3,2,1,0:T(8,128)S(1)}, f32[4,2,128,128]{3,2,1,0:T(8,128)}, u32[]{:S(2)}, u32[]{:S(2)}) collective-permute-start(f32[4,2,128,128]{3,2,1,0:T(8,128)S(1)} %collective-permute-done.25.rest_3_), channel_id=1, source_target_pairs={{2,0},{3,1},{4,2},{5,3},{10,8},{11,9},{12,10},{13,11},{18,16},{19,... | collective-permute-start | bytes 1572872 | tf_op jit(solution)/shard_map/ppermute | solution.py:445
  69.6 22.6 %collective-permute-start.30 = (f32[4,2,128,128]{3,2,1,0:T(8,128)S(1)}, f32[4,2,128,128]{3,2,1,0:T(8,128)}, u32[]{:S(2)}, u32[]{:S(2)}) collective-permute-start(f32[4,2,128,128]{3,2,1,0:T(8,128)S(1)} %collective-permute-done.26.rest_4_), channel_id=1, source_target_pairs={{2,4},{3,5},{4,6},{5,7},{10,12},{11,13},{12,14},{13,15},{18,20},{1... | collective-permute-start | bytes 1572872 | tf_op jit(solution)/shard_map/ppermute | solution.py:442
  73.7 19.8 %collective-permute-start.31 = (f32[4,2,128,128]{3,2,1,0:T(8,128)S(1)}, f32[4,2,128,128]{3,2,1,0:T(8,128)}, u32[]{:S(2)}, u32[]{:S(2)}) collective-permute-start(f32[4,2,128,128]{3,2,1,0:T(8,128)S(1)} %collective-permute-done.27.rest_5_), channel_id=1, source_target_pairs={{2,0},{3,1},{4,2},{5,3},{10,8},{11,9},{12,10},{13,11},{18,16},{19,... | collective-permute-start | bytes 1572872 | tf_op jit(solution)/shard_map/ppermute | solution.py:445
  78.2 21.9 %collective-permute-start.20 = (f32[4,2,128,128]{3,2,1,0:T(8,128)S(1)}, f32[4,2,128,128]{3,2,1,0:T(8,128)S(1)}, u32[]{:S(2)}, u32[]{:S(2)}) collective-permute-start(f32[4,2,128,128]{3,2,1,0:T(8,128)S(1)} %constant_dynamic-slice_fusion.rest_14_.rest_8_), channel_id=1, source_target_pairs={{0,1},{1,0},{2,3},{3,2},{4,5},{5,4},{6,7},{7,6},{8,9},{9,8},{10,11... | collective-permute-start | bytes 1572872 | tf_op jit(solution)/shard_map/ppermute | solution.py:436
  81.0 22.5 %collective-permute-start.32 = (f32[4,2,128,128]{3,2,1,0:T(8,128)}, f32[4,2,128,128]{3,2,1,0:T(8,128)}, u32[]{:S(2)}, u32[]{:S(2)}) collective-permute-start(f32[4,2,128,128]{3,2,1,0:T(8,128)} %collective-permute-done.28.rest_6_), channel_id=1, source_target_pairs={{4,6},{5,7},{12,14},{13,15},{20,22},{21,23},{28,30},{29,31}} | collective-permute-start | bytes 1572872 | tf_op jit(solution)/shard_map/ppermute | solution.py:442
  82.3 22.4 %collective-permute-start.33 = (f32[4,2,128,128]{3,2,1,0:T(8,128)}, f32[4,2,128,128]{3,2,1,0:T(8,128)}, u32[]{:S(2)}, u32[]{:S(2)}) collective-permute-start(f32[4,2,128,128]{3,2,1,0:T(8,128)} %collective-permute-done.29.rest_7_), channel_id=1, source_target_pairs={{2,0},{3,1},{10,8},{11,9},{18,16},{19,17},{26,24},{27,25}} | collective-permute-start | bytes 1572872 | tf_op jit(solution)/shard_map/ppermute | solution.py:445
  92.2 22.5 %collective-permute-start.34 = (f32[4,2,128,128]{3,2,1,0:T(8,128)}, f32[4,2,128,128]{3,2,1,0:T(8,128)}, u32[]{:S(2)}, u32[]{:S(2)}) collective-permute-start(f32[4,2,128,128]{3,2,1,0:T(8,128)} %collective-permute-done.30.rest_8_), channel_id=1, source_target_pairs={{4,6},{5,7},{12,14},{13,15},{20,22},{21,23},{28,30},{29,31}} | collective-permute-start | bytes 1572872 | tf_op jit(solution)/shard_map/ppermute | solution.py:442
  93.5 25.6 %collective-permute-start.35 = (f32[4,2,128,128]{3,2,1,0:T(8,128)}, f32[4,2,128,128]{3,2,1,0:T(8,128)}, u32[]{:S(2)}, u32[]{:S(2)}) collective-permute-start(f32[4,2,128,128]{3,2,1,0:T(8,128)} %collective-permute-done.31.rest_9_), channel_id=1, source_target_pairs={{2,0},{3,1},{10,8},{11,9},{18,16},{19,17},{26,24},{27,25}} | collective-permute-start | bytes 1572872 | tf_op jit(solution)/shard_map/ppermute | solution.py:445
  100.1 90.3 %collective-permute-start.7 = (f32[4,2,128,128]{3,2,1,0:T(8,128)}, f32[4,2,128,128]{3,2,1,0:T(8,128)S(1)}, u32[]{:S(2)}, u32[]{:S(2)}) collective-permute-start(f32[4,2,128,128]{3,2,1,0:T(8,128)} %copy-done.24), channel_id=1, source_target_pairs={{1,2},{2,3},{3,4},{4,5},{5,6},{6,7},{9,10},{10,11},{11,12},{12,13}... | collective-permute-start | bytes 1572872 | tf_op jit(solution)/shard_map/ppermute | solution.py:433
  103.5 88.9 %collective-permute-start.8 = (f32[4,2,128,128]{3,2,1,0:T(8,128)}, f32[4,2,128,128]{3,2,1,0:T(8,128)}, u32[]{:S(2)}, u32[]{:S(2)}) collective-permute-start(f32[4,2,128,128]{3,2,1,0:T(8,128)} %copy-done.23), channel_id=1, source_target_pairs={{0,2},{1,3},{2,4},{3,5},{4,6},{5,7},{8,10},{9,11},{10,12},{11,13},... | collective-permute-start | bytes 1572872 | tf_op jit(solution)/shard_map/ppermute | solution.py:433
  104.7 89.5 %collective-permute-start.9 = (f32[4,2,128,128]{3,2,1,0:T(8,128)}, f32[4,2,128,128]{3,2,1,0:T(8,128)}, u32[]{:S(2)}, u32[]{:S(2)}) collective-permute-start(f32[4,2,128,128]{3,2,1,0:T(8,128)} %copy-done.22), channel_id=1, source_target_pairs={{0,3},{1,4},{2,5},{3,6},{4,7},{7,2},{8,11},{9,12},{10,13},{11,14},... | collective-permute-start | bytes 1572872 | tf_op jit(solution)/shard_map/ppermute | solution.py:433
  114.7 81.8 %collective-permute-start.10 = (f32[4,2,128,128]{3,2,1,0:T(8,128)}, f32[4,2,128,128]{3,2,1,0:T(8,128)}, u32[]{:S(2)}, u32[]{:S(2)}) collective-permute-start(f32[4,2,128,128]{3,2,1,0:T(8,128)} %copy-done.21), channel_id=1, source_target_pairs={{0,4},{1,5},{2,6},{3,7},{6,2},{7,3},{8,12},{9,13},{10,14},{11,15},... | collective-permute-start | bytes 1572872 | tf_op jit(solution)/shard_map/ppermute | solution.py:433
  188.6 86.9 %collective-permute-start.40 = (f32[16,2,128,128]{3,2,1,0:T(8,128)}, f32[16,2,128,128]{3,2,1,0:T(8,128)S(1)}, u32[]{:S(2)}, u32[]{:S(2)}) collective-permute-start(f32[16,2,128,128]{3,2,1,0:T(8,128)} %get-tuple-element.62.rest_11_.rest_0_), channel_id=1, source_target_pairs={{0,1},{1,0},{2,3},{3,2},{4,5},{5,4},{6,7},{7,6},{8,9},{9,8},{10,11... | collective-permute-start | bytes 6291464 | tf_op jit(solution)/shard_map/ppermute | solution.py:436
  190.4 21.6 %collective-permute-start.11 = (f32[4,2,128,128]{3,2,1,0:T(8,128)}, f32[4,2,128,128]{3,2,1,0:T(8,128)S(1)}, u32[]{:S(2)}, u32[]{:S(2)}) collective-permute-start(f32[4,2,128,128]{3,2,1,0:T(8,128)} %copy-done.20), channel_id=1, source_target_pairs={{0,5},{1,6},{2,7},{5,2},{6,3},{7,4},{8,13},{9,14},{10,15},{13,10},... | collective-permute-start | bytes 1572872 | tf_op jit(solution)/shard_map/ppermute | solution.py:433
  192.4 33.8 %collective-permute-start.12 = (f32[4,2,128,128]{3,2,1,0:T(8,128)}, f32[4,2,128,128]{3,2,1,0:T(8,128)}, u32[]{:S(2)}, u32[]{:S(2)}) collective-permute-start(f32[4,2,128,128]{3,2,1,0:T(8,128)} %copy-done.19), channel_id=1, source_target_pairs={{0,6},{1,7},{4,2},{5,3},{6,4},{7,5},{8,14},{9,15},{12,10},{13,11},... | collective-permute-start | bytes 1572872 | tf_op jit(solution)/shard_map/ppermute | solution.py:433
  194.3 58.7 %collective-permute-start.13 = (f32[4,2,128,128]{3,2,1,0:T(8,128)}, f32[4,2,128,128]{3,2,1,0:T(8,128)}, u32[]{:S(2)}, u32[]{:S(2)}) collective-permute-start(f32[4,2,128,128]{3,2,1,0:T(8,128)} %copy-done.18), channel_id=1, source_target_pairs={{0,7},{3,2},{4,3},{5,4},{6,5},{7,6},{8,15},{11,10},{12,11},{13,12}... | collective-permute-start | bytes 1572872 | tf_op jit(solution)/shard_map/ppermute | solution.py:433
  266.7 25.2 %collective-permute-start.36 = (f32[4,256,128]{2,1,0:T(8,128)S(1)}, f32[4,256,128]{2,1,0:T(8,128)}, u32[]{:S(2)}, u32[]{:S(2)}) collective-permute-start(f32[4,256,128]{2,1,0:T(8,128)S(1)} %get-tuple-element.65), channel_id=1, source_target_pairs={{0,8},{8,0},{16,24},{24,16},{1,9},{9,1},{17,25},{25,17},{2,10},{10... | collective-permute-start | bytes 1572872 | tf_op jit(solution)/shard_map/ppermute | solution.py:238
  274.0 16.2 %collective-permute-start.38 = (f32[2,2,128,128]{3,2,1,0:T(8,128)S(1)}, f32[2,2,128,128]{3,2,1,0:T(8,128)}, u32[]{:S(2)}, u32[]{:S(2)}) collective-permute-start(f32[2,2,128,128]{3,2,1,0:T(8,128)S(1)} %slice.40), channel_id=1, source_target_pairs={{0,16},{8,24},{1,17},{9,25},{2,18},{10,26},{3,19},{11,27},{4,20},{... | collective-permute-start | bytes 786440 | tf_op jit(solution)/shard_map/ppermute | solution.py:243
  293.0 18.3 %collective-permute-start.37 = (f32[4,256,128]{2,1,0:T(8,128)S(1)}, f32[4,256,128]{2,1,0:T(8,128)S(1)}, u32[]{:S(2)}, u32[]{:S(2)}) collective-permute-start(f32[4,256,128]{2,1,0:T(8,128)S(1)} %add.331), channel_id=1, source_target_pairs={{0,16},{8,24},{16,0},{24,8},{1,17},{9,25},{17,1},{25,9},{2,18},{10... | collective-permute-start | bytes 1572872 | tf_op jit(solution)/shard_map/ppermute | solution.py:238
  303.3 19.3 %collective-permute-start.42 = (f32[4,256,128]{2,1,0:T(8,128)S(1)}, f32[4,256,128]{2,1,0:T(8,128)S(1)}, u32[]{:S(2)}, u32[]{:S(2)}) collective-permute-start(f32[4,256,128]{2,1,0:T(8,128)S(1)} %add.338), channel_id=1, source_target_pairs={{0,16},{8,24},{16,0},{24,8},{1,17},{9,25},{17,1},{25,9},{2,18},{10... | collective-permute-start | bytes 1572872 | tf_op jit(solution)/shard_map/ppermute | solution.py:238
  (40 other events, 422.8 us)

commit v2 on v0

v2 whole, which is shorter than its diff:
```python
import jax
import jax.numpy as jnp
from jax import lax
from jax.experimental import pallas as pl
from jax.experimental.pallas import tpu as pltpu
from jax.sharding import PartitionSpec as P

CBLK = 2
LINES = 2
F32 = jnp.float32
BF16 = jnp.bfloat16
MIB = 1024 * 1024

ANY = pl.BlockSpec(memory_space=pl.ANY)
SMEM = pl.BlockSpec(memory_space=pltpu.SMEM)
VMEM = pl.BlockSpec(memory_space=pltpu.VMEM)


def call(kernel, mib, **kw):
    return pl.pallas_call(
        kernel,
        compiler_params=pltpu.CompilerParams(vmem_limit_bytes=mib * MIB),
        cost_estimate=pl.CostEstimate(flops=0, bytes_accessed=0, transcendentals=0),
        **kw,
    )


def list_slots(ids_ref, pos, cnt, slots, cols_n, base):
    for o in range(cols_n + 1):
        cnt[o] = 0
    pos[cols_n * (base + 1)] = 0

    def one(j, carry):
        owner = lax.rem(ids_ref[j], cols_n)
        r = cnt[owner]
        cnt[owner] = r + 1
        pos[owner * (base + 1) + r] = j

        @pl.when(r >= base)
        def _():
            e = cnt[cols_n]

            @pl.when(e == 0)
            def _():
                pos[cols_n * (base + 1)] = j

            cnt[cols_n] = e + 1

        return carry

    lax.fori_loop(0, slots, one, 0)


def copy_listed(moves, sems):
    for n, (cond, src, dst) in enumerate(moves):

        @pl.when(cond)
        def _(n=n, src=src, dst=dst):
            pltpu.make_async_copy(src, dst, sems.at[n]).start()

    for n, (cond, src, dst) in enumerate(moves):

        @pl.when(cond)
        def _(n=n, src=src, dst=dst):
            pltpu.make_async_copy(src, dst, sems.at[n]).wait()


def pack_streams(tiles, ids, cols_n, base):
    slots = tiles.shape[0]
    count = LINES * base + 1

    def kernel(ids_ref, tiles_ref, out_ref, pos, cnt, sems):
        list_slots(ids_ref, pos, cnt, slots, cols_n, base)
        moves = []
        for o in range(LINES):
            for r in range(base):
                moves.append((r < cnt[o], tiles_ref.at[pos[o * (base + 1) + r]], out_ref.at[o * base + r]))
        moves.append((cnt[cols_n] > 0, tiles_ref.at[pos[cols_n * (base + 1)]], out_ref.at[LINES * base]))
        copy_listed(moves, sems)

    return call(
        kernel,
        2,
        out_shape=jax.ShapeDtypeStruct((count,) + tiles.shape[1:], F32),
        in_specs=[SMEM, ANY],
        out_specs=ANY,
        scratch_shapes=[
            pltpu.SMEM((cols_n * (base + 1) + 1,), jnp.int32),
            pltpu.SMEM((cols_n + 1,), jnp.int32),
            pltpu.SemaphoreType.DMA((count,)),
        ],
        name="pack_streams",
    )(ids, tiles)


def pack_shifts(tiles, ids, me, cols_n, base):
    slots = tiles.shape[0]

    def kernel(ids_ref, me_ref, tiles_ref, *rest):
        outs, (pos, cnt, sems) = rest[: cols_n - 1], rest[cols_n - 1 :]
        list_slots(ids_ref, pos, cnt, slots, cols_n, base)
        moves = []
        for k in range(1, cols_n):
            owner = lax.rem(me_ref[0] + k, cols_n)
            for r in range(base):
                moves.append(
                    (
                        (r < cnt[owner]) & (owner >= LINES),
                        tiles_ref.at[pos[owner * (base + 1) + r]],
                        outs[k - 1].at[r],
                    )
                )
        copy_listed(moves, sems)

    return call(
        kernel,
        2,
        out_shape=tuple(jax.ShapeDtypeStruct((base,) + tiles.shape[1:], F32) for _ in range(1, cols_n)),
        in_specs=[SMEM, SMEM, ANY],
        out_specs=tuple(ANY for _ in range(1, cols_n)),
        scratch_shapes=[
            pltpu.SMEM((cols_n * (base + 1) + 1,), jnp.int32),
            pltpu.SMEM((cols_n + 1,), jnp.int32),
            pltpu.SemaphoreType.DMA(((cols_n - 1) * base,)),
        ],
        name="pack_shifts",
    )(ids, me, tiles)


def unwritten(shape):
    def kernel(out_ref):
        pass

    return call(kernel, 2, out_shape=jax.ShapeDtypeStruct(shape, F32), out_specs=ANY, name="unwritten")()


def extract(parts, tables, source_rows, odd, tiles_n, name):
    block = parts[0].shape[-1]
    bits = block.bit_length() - 1
    counts = [p.shape[0] for p in parts]
    table = jnp.concatenate(tables)
    wide = 2 * CBLK

    def kernel(table_ref, rows_ref, odd_ref, *rest):
        ins, (held, keep, send, top, sem) = rest[: len(parts)], rest[len(parts) :]
        at = 0
        for part, count in zip(ins, counts):
            for n in range(count):
                where = table_ref[at]

                @pl.when(where >= 0)
                def _(part=part, n=n, where=where):
                    pltpu.make_async_copy(part.at[n], held.at[where], sem).start()

                at += 1
        keep[...] = jnp.zeros_like(keep)
        send[...] = jnp.zeros_like(send)
        pltpu.make_async_copy(held, held, sem).wait()
        for m in range(CBLK):
            for c in range(2):
                top[2 * m + c] = held[m, c]
        for out, half in ((keep, odd_ref[0]), (send, 1 - odd_ref[0])):

            def one(j, carry, out=out, half=half):
                row = rows_ref[half * block + j]

                @pl.when(row >= 0)
                def _():
                    tile = lax.shift_right_logical(row, bits) * CBLK
                    inner = row & (block - 1)
                    for m in range(CBLK):
                        for c in range(2):
                            out[2 * m + c, pl.ds(j, 1), :] = held[tile + m, c, pl.ds(inner, 1), :]

                return carry

            lax.fori_loop(0, block, one, 0, unroll=4)

    part_rows = jax.ShapeDtypeStruct((wide, block, block), F32)
    return call(
        kernel,
        12,
        out_shape=(jax.ShapeDtypeStruct((tiles_n, 2, block, block), F32), part_rows, part_rows, part_rows),
        in_specs=[SMEM, SMEM, SMEM] + [ANY] * len(parts),
        out_specs=(VMEM, VMEM, VMEM, VMEM),
        scratch_shapes=[pltpu.SemaphoreType.DMA],
        name=name,
    )(table, source_rows, odd, *parts)


def exchange(keep, send, top, my_row, rows_n):
    def cross(x, step):
        return lax.ppermute(x, "prow", [(p, p ^ step) for p in range(rows_n)])

    held = top
    step = 2
    while step < rows_n:
        got = lax.ppermute(held, "prow", [(p, p + step) for p in range(step)])
        held = jnp.where((my_row >= step) & (my_row < 2 * step), got, held)
        step *= 2
    total = keep + cross(send, 1)
    step = 2
    while step < rows_n:
        total = total + cross(total, step)
        step *= 2
    return (total, cross(total, 1)), (held, cross(held, 1))


def replace_rows(targets_ref, odd, old_refs, held, block):
    bits = block.bit_length() - 1

    for ref, half in ((old_refs[0], odd), (old_refs[1], 1 - odd)):

        def one(j, carry, ref=ref, half=half):
            row = targets_ref[half * block + j]

            @pl.when(row >= 0)
            def _():
                tile = lax.shift_right_logical(row, bits) * CBLK
                inner = row & (block - 1)
                for m in range(CBLK):
                    for c in range(2):
                        held[tile + m, c, pl.ds(inner, 1), :] = ref[2 * m + c, pl.ds(j, 1), :]

            return carry

        lax.fori_loop(0, block, one, 0, unroll=4)


def split(x):
    high = x.astype(BF16)
    return high, (x - high.astype(F32)).astype(BF16)


def dot3(high, low, w_high, w_low):
    return (
        jnp.dot(high, w_high, preferred_element_type=F32)
        + jnp.dot(high, w_low, preferred_element_type=F32)
        + jnp.dot(low, w_high, preferred_element_type=F32)
    )


def store_complex(high_ref, low_ref, row, col, re, im):
    k, n = re.shape
    for r, c, value in ((0, 0, re), (0, 1, im), (1, 0, -im), (1, 1, re)):
        high, low = split(value)
        rows, cols = pl.ds(row + r * k, k), pl.ds(col + c * n, n)
        high_ref[rows, cols] = high
        low_ref[rows, cols] = low


def panel_factors(held, new, old, inverses, targets, my_row, group):
    block = held.shape[-1]
    row_tiles = held.shape[0] // CBLK
    rows = row_tiles * block

    def kernel(tgt, row_ref, held_in, new_a, new_b, old_a, old_b, inv_ref, high_ref, low_ref, top_ref, *rest):
        held_ref, new_ref, i0h, i0l, i1h, i1l, uh, ul, sem = rest
        odd = lax.rem(row_ref[0], 2)
        copy = pltpu.make_async_copy(held_in, held_ref, sem)
        copy.start()
        new_ref[odd] = new_a[...]
        new_ref[1 - odd] = new_b[...]
        store_complex(i0h, i0l, 0, 0, inv_ref[0, 0], inv_ref[0, 1])
        store_complex(i1h, i1l, 0, 0, inv_ref[1, 0], inv_ref[1, 1])
        store_complex(uh, ul, 0, 0, new_ref[0, 2], new_ref[0, 3])
        lower = dot3(
            *split(jnp.concatenate([new_ref[1, 0], new_ref[1, 1]], axis=1)), i0h[...], i0l[...]
        )
        top_ref[...] = lower
        copy.wait()
        replace_rows(tgt, odd, (old_a, old_b), held_ref, block)

        @pl.when(row_ref[0] == 1)
        def _():
            for m in range(CBLK):
                for c in range(2):
                    held_ref[m, c] = new_ref[1, 2 * m + c]

        def one(g, carry):
            x = [
                jnp.concatenate(
                    [
                        jnp.concatenate(
                            [held_ref[(g * group + t) * CBLK + m, 0], held_ref[(g * group + t) * CBLK + m, 1]], axis=1
                        )
                        for t in range(group)
                    ],
                    axis=0,
                )
                for m in range(CBLK)
            ]
            at = pl.ds(pl.multiple_of(g * (group * block), group * block), group * block)
            l0h, l0l = split(dot3(*split(x[0]), i0h[...], i0l[...]))
            high_ref[at, : 2 * block] = l0h
            low_ref[at, : 2 * block] = l0l
            y = x[1] - dot3(l0h, l0l, uh[...], ul[...])
            l1h, l1l = split(dot3(*split(y), i1h[...], i1l[...]))
            high_ref[at, 2 * block :] = l1h
            low_ref[at, 2 * block :] = l1l
            return carry

        lax.fori_loop(0, row_tiles // group, one, 0)

    wide = pltpu.VMEM((2 * block, 2 * block), BF16)
    return call(
        kernel,
        20,
        out_shape=(
            jax.ShapeDtypeStruct((rows, 4 * block), BF16),
            jax.ShapeDtypeStruct((rows, 4 * block), BF16),
            jax.ShapeDtypeStruct((block, 2 * block), F32),
        ),
        in_specs=[SMEM, SMEM, ANY] + [VMEM] * 5,
        out_specs=(VMEM, VMEM, VMEM),
        scratch_shapes=[pltpu.VMEM(held.shape, F32), pltpu.VMEM((2, 2 * CBLK, block, block), F32)]
        + [wide] * 6
        + [pltpu.SemaphoreType.DMA],
        name="panel_factors",
    )(targets, my_row, held, *new, *old, inverses)


def update(held, new, old, high, low, lower_top, targets, my_row, my_col, rows_n, group):
    block = held.shape[-1]
    row_tiles = held.shape[0] // CBLK
    rows = row_tiles * block
    steps = row_tiles // group
    span = group * block

    def kernel(tgt, row_ref, col_ref, held_in, new_a, new_b, old_a, old_b, high_in, low_in, top_ref, out_ref, *rest):
        held_ref, new_ref, high_ref, low_ref, res_ref, wh, wl, sem, in_sems, out_sems = rest
        odd = lax.rem(row_ref[0], 2)
        copies = [pltpu.make_async_copy(held_in, held_ref, sem)]
        copies[0].start()
        for g in range(steps):
            at = pl.ds(g * span, span)
            for n, (src, dst) in enumerate(((high_in, high_ref), (low_in, low_ref))):
                pltpu.make_async_copy(src.at[at], dst.at[at], in_sems.at[2 * g + n]).start()
        new_ref[odd] = new_a[...]
        new_ref[1 - odd] = new_b[...]
        for m in range(CBLK):
            store_complex(wh, wl, 0, 2 * m * block, new_ref[0, 2 * m], new_ref[0, 2 * m + 1])
        first = dot3(*split(top_ref[...]), wh[: 2 * block, :], wl[: 2 * block, :])
        second = []
        for n in range(2 * CBLK):
            second.append(new_ref[1, n] - first[:, n * block : (n + 1) * block])
            new_ref[1, n] = second[n]
        for m in range(CBLK):
            store_complex(wh, wl, 2 * block, 2 * m * block, second[2 * m], second[2 * m + 1])
        copies[0].wait()
        replace_rows(tgt, odd, (old_a, old_b), held_ref, block)
        for g in range(steps):
            at = pl.ds(g * span, span)
            for n, (src, dst) in enumerate(((high_in, high_ref), (low_in, low_ref))):
                pltpu.make_async_copy(src.at[at], dst.at[at], in_sems.at[2 * g + n]).wait()
            y = dot3(high_ref[at, :], low_ref[at, :], wh[...], wl[...])
            for t in range(group):
                tile = g * group + t
                for m in range(CBLK):
                    for c in range(2):
                        n = 2 * m + c
                        res_ref[c, tile * block : (tile + 1) * block, m * block : (m + 1) * block] = (
                            held_ref[tile * CBLK + m, c]
                            - y[t * block : (t + 1) * block, n * block : (n + 1) * block]
                        )
            for panel in range(2):

                @pl.when(col_ref[0] == panel)
                def _(panel=panel, at=at):
                    for c in range(2):
                        cols = slice((2 * panel + c) * block, (2 * panel + c + 1) * block)
                        res_ref[c, at, :block] = high_ref[at, cols].astype(F32) + low_ref[at, cols].astype(F32)

            if g == 0:
                for p in range(2):

                    @pl.when(row_ref[0] == p)
                    def _(p=p):
                        for c in range(2):
                            for m in range(CBLK):
                                res_ref[c, :block, m * block : (m + 1) * block] = new_ref[p, 2 * m + c]

                @pl.when((row_ref[0] == 1) & (col_ref[0] == 0))
                def _():
                    for c in range(2):
                        res_ref[c, :block, :block] = top_ref[:, c * block : (c + 1) * block]

            for c in range(2):
                pltpu.make_async_copy(res_ref.at[c, at], out_ref.at[c, at], out_sems.at[2 * g + c]).start()
        for g in range(steps):
            at = pl.ds(g * span, span)
            for c in range(2):
                pltpu.make_async_copy(res_ref.at[c, at], out_ref.at[c, at], out_sems.at[2 * g + c]).wait()

    return call(
        kernel,
        24,
        out_shape=jax.ShapeDtypeStruct((2, rows, CBLK * block), F32),
        in_specs=[SMEM] * 3 + [ANY] + [VMEM] * 4 + [ANY] * 2 + [VMEM],
        out_specs=ANY,
        scratch_shapes=[
            pltpu.VMEM(held.shape, F32),
            pltpu.VMEM((2, 2 * CBLK, block, block), F32),
            pltpu.VMEM((rows, 4 * block), BF16),
            pltpu.VMEM((rows, 4 * block), BF16),
            pltpu.VMEM((2, rows, CBLK * block), F32),
            pltpu.VMEM((4 * block, 4 * block), BF16),
            pltpu.VMEM((4 * block, 4 * block), BF16),
            pltpu.SemaphoreType.DMA,
            pltpu.SemaphoreType.DMA((2 * steps,)),
            pltpu.SemaphoreType.DMA((2 * steps,)),
        ],
        name="update",
    )(targets, my_row, my_col, held, *new, *old, high, low, lower_top)


def per_device(assembly, slot_tile, pivots, inverses):
    cols_n = lax.axis_size("pcol")
    rows_n = lax.axis_size("prow")
    my_col = lax.axis_index("pcol")
    my_row = lax.axis_index("prow")
    tiles = assembly[0]
    slots = tiles.shape[0]
    block = tiles.shape[-1]
    width = CBLK * cols_n
    row_tiles = slots // CBLK
    base = (slots + cols_n - 1) // cols_n
    excess_max = slots // (base + 1)
    depth = cols_n // LINES
    group = 4 if row_tiles % 4 == 0 else 1
    line, level = my_col % LINES, my_col // LINES
    me = my_col.astype(jnp.int32).reshape(1)
    me_row = my_row.astype(jnp.int32).reshape(1)
    odd = me_row % 2
    ids = slot_tile[0]

    def swap(x, low=0, high=depth):
        return lax.ppermute(x, "pcol", [(i, i ^ 1) for i in range(low * LINES, high * LINES)])

    packed = pack_streams(tiles, ids, cols_n, base)
    parts, sources = [packed, swap(packed)], [(level, line), (level, 1 - line)]
    up = down = packed
    for t in range(1, depth):
        up = lax.ppermute(up, "pcol", [(i, i + LINES) for i in range((t - 1) * LINES, cols_n - LINES)])
        down = lax.ppermute(down, "pcol", [(i, i - LINES) for i in range(LINES, cols_n - (t - 1) * LINES)])
        parts += [up, down, swap(up, t, depth), swap(down, 0, depth - t)]
        sources += [(level - t, line), (level + t, line), (level - t, 1 - line), (level + t, 1 - line)]

    shifted = pack_shifts(tiles, ids, me, cols_n, base)
    arrived = []
    for k in range(1, cols_n):
        pairs = [(i, (i + k) % cols_n) for i in range(cols_n)]
        arrived.append(lax.ppermute(shifted[k - 1], "pcol", [(a, b) for a, b in pairs if b >= LINES]))

    near = lax.optimization_barrier((ids, packed))[0][None]
    step = 1
    while step < cols_n:
        near = jnp.concatenate([near, lax.ppermute(near, "pcol", [(i, i ^ step) for i in range(cols_n)])])
        step *= 2
    order = jnp.arange(cols_n, dtype=jnp.int32)
    all_ids = jnp.sum(
        jnp.where((order[:, None] == (order[None, :] ^ my_col))[:, :, None], near[:, None, :], 0), axis=0
    )
    owner = all_ids % cols_n
    slot_order = jnp.arange(slots, dtype=jnp.int32)
    earlier = slot_order[None, :] < slot_order[:, None]
    rank = jnp.sum(((owner[:, :, None] == owner[:, None, :]) & earlier[None]).astype(jnp.int32), axis=2)
    over = rank >= base
    over_rank = jnp.sum((over[:, None, :] & earlier[None]).astype(jnp.int32), axis=2)
    most = jnp.broadcast_to(jnp.max(jnp.sum(over.astype(jnp.int32), axis=1)), (8, 128))
    step = 1
    while step < rows_n:
        most = jnp.maximum(most, lax.ppermute(most, "prow", [(p, p ^ step) for p in range(rows_n)]))
        step *= 2

    def ids_where(hit):
        return jnp.sum(jnp.where(hit, all_ids[:, None, :] + 1, 0), axis=2) - 1

    ranks = jnp.arange(base, dtype=jnp.int32)[None, :, None]
    over_ranks = jnp.arange(excess_max, dtype=jnp.int32)[None, :, None]

    def ranked(stream):
        return ids_where((owner[:, None, :] == stream) & ~over[:, None, :] & (rank[:, None, :] == ranks))

    excess = ids_where(over[:, None, :] & (over_rank[:, None, :] == over_ranks))
    sent = jnp.concatenate([ranked(o) for o in range(LINES)] + [excess[:, :1]], axis=1)
    later = excess[:, 1:].reshape(-1)

    def panel_place(t):
        return jnp.where((t >= 0) & (t % width < LINES), t // width * CBLK + t % width, -1)

    def own_place(t):
        return jnp.where((t >= 0) & (t % cols_n == my_col), t // width * CBLK + t % width // cols_n, -1)

    def by_part(table):
        source = jnp.stack([jnp.where((a >= 0) & (a < depth), a * LINES + b, -1) for a, b in sources])
        hit = source[:, None, None] == order[None, :, None]
        return (jnp.sum(jnp.where(hit, table[None] + 1, 0), axis=1) - 1).reshape(-1)

    def gather_rest():
        def nth(e):
            hit = (order[:, None] == my_col) & over & (over_rank == e)
            return jnp.sum(jnp.where(hit, slot_order[None, :], 0))

        rest = jnp.stack([lax.dynamic_index_in_dim(tiles, nth(e), 0, False) for e in range(1, excess_max)])
        return lax.all_gather(rest, "pcol").reshape((-1,) + tiles.shape[1:])

    def no_rest():
        return unwritten((cols_n * (excess_max - 1),) + tiles.shape[1:])

    rest = lax.cond(most[0, 0] > 1, gather_rest, no_rest)

    picks = jnp.arange(2 * block, dtype=jnp.int32)
    first, second = pivots[0], pivots[1]
    same = (second[:, None] == first[None, :]) & (first[None, :] >= 2 * block)
    chained = jnp.sum(jnp.where(same, picks[None, :block], 0), axis=1)
    second_source = jnp.where(jnp.any(same, axis=1), chained, second)
    replaced = jnp.any(same, axis=0)
    wanted = jnp.concatenate([first, second_source])
    named = jnp.concatenate([first, second])
    moved = (named != picks) & ~jnp.concatenate([replaced, jnp.zeros_like(replaced)])

    def local_row(row, keep):
        ours = (row // block % rows_n == my_row) & keep
        return jnp.where(ours, row // block // rows_n * block + row % block, -1)

    source_rows = local_row(wanted, True)
    targets = local_row(named, moved)

    tables = [by_part(panel_place(sent)), panel_place(later)]
    held_p, keep_p, send_p, top_p = extract(parts + [rest], tables, source_rows, odd, slots, "panel_rows")
    new_p, old_p = exchange(keep_p, send_p, top_p, my_row, rows_n)
    high, low, lower_top = panel_factors(held_p, new_p, old_p, inverses, targets, me_row, group)

    gathered = my_col < LINES
    mine = order[:, None] == my_col
    here = jnp.max(jnp.where(mine, own_place(all_ids), -1), axis=0)
    tables = [jnp.where(gathered, -1, here)]
    own_sent = own_place(ranked(my_col))
    for k in range(1, cols_n):
        row = jnp.sum(jnp.where(order[:, None] == (my_col - k) % cols_n, own_sent, 0), axis=0)
        tables.append(jnp.where(gathered, -1, row))
    use = gathered | ~mine
    tables += [by_part(jnp.where(use, own_place(sent), -1))]
    tables += [jnp.where(jnp.repeat(use[:, 0], excess_max - 1), own_place(later), -1)]
    held, keep, send, top = extract(
        [tiles] + arrived + parts + [rest], tables, source_rows, odd, slots, "own_rows"
    )
    new, old = exchange(keep, send, top, my_row, rows_n)
    return update(held, new, old, high, low, lower_top, targets, me_row, me, rows_n, group)


def solution(mesh):
    in_specs = (P("prow", "pcol", None, None, None), P("prow", "pcol"), P(), P())
    out_specs = P(None, "prow", "pcol")
    return jax.shard_map(
        per_device, mesh=mesh, in_specs=in_specs, out_specs=out_specs, check_vma=False
    )
```

time: 569 us -> 322 us (0.57); the launches traced: 557 us -> 318 us
  waiting for transfers between devices: 373 us -> 98.2 us
  local copies, waits for them, and re-layouts: 105 us -> 25.9 us
  starting transfers between devices: 21.2 us -> 88.7 us
  Pallas kernels: 0 us -> 54.3 us
  matrix products: 27.6 us -> 0 us
  other arithmetic: 16.5 us -> 36.2 us
    psum x4 -> x0, waiting for transfers between devices: 258 us -> none  [spread(): return lax.psum(jnp.where(mine, x, jnp.zeros_like(x)), axis)]
    all_to_all x2 -> x0, waiting for transfers between devices: 115 us -> none  [the longest x1 115 us: per_device(): lax.all_to_all(outgoing, 'pcol', split_axis=0, concat_axis=0, tiled=True)]
    ppermute x0 -> x35, waiting for transfers between devices: none -> 98.2 us  [the longest x7 44.8 us: swap(): lax.ppermute(x, 'pcol', [(i, i ^ 1) for i in range(low * LINES, high * LI...]
    ppermute x0 -> x35, starting transfers between devices: none -> 88.7 us  [the longest x7 31.3 us: per_device(): lax.ppermute(shifted[k - 1], 'pcol', [(a, b) for a, b in pairs if b >= LI...]
    scatter x8 -> x0, local copies, waits for them, and re-layouts: 67.6 us -> none  [the longest x4 35.3 us: per_device(): matrix = matrix.at[:, target_rows, :].set(old_top, mode='drop')]
    pallas_call x0 -> x7, Pallas kernels: none -> 54.3 us  [the longest x1 18.8 us: pack_shifts(): call(kernel, 2, out_shape=tuple((jax.ShapeDtypeStruct((base,) + tiles.sha...]
    dot_general x16 -> x0, matrix products: 27.6 us -> none  [product(): jnp.dot(left, right, precision=lax.Precision.HIGHEST, preferred_element_t...]
    unnamed x20 -> x44, local copies, waits for them, and re-layouts: 0.05 us -> 14.3 us
  transfers between devices with their start and end apart: 6 -> 35, of which waited for: 5 -> 10; matrix products, arithmetic and copies ran while one was open for 2% -> 15% of each run, Pallas kernels for 0% -> 13%
where the time goes in v2:
time: 322 us; the launch traced here: 318 us
  waiting for transfers between devices  98.2 us (30%)
  starting transfers between devices  88.7 us (28%)
  Pallas kernels  54.3 us (17%)
  other arithmetic  36.2 us (11%)
  local copies, waits for them, and re-layouts  25.9 us (8%)
  between operations  14.7 us (5%)
    ppermute x7, waiting for transfers between devices, swap(): lax.ppermute(x, 'pcol', [(i, i ^ 1) for i in range(low * LINES, high * LI...  44.8 us
    ppermute x7, starting transfers between devices, per_device(): lax.ppermute(shifted[k - 1], 'pcol', [(a, b) for a, b in pairs if b >= LI...  31.3 us
    ppermute x7, waiting for transfers between devices, per_device(): lax.ppermute(shifted[k - 1], 'pcol', [(a, b) for a, b in pairs if b >= LI...  28.8 us
    ppermute x8, starting transfers between devices, cross(): return lax.ppermute(x, 'prow', [(p, p ^ step) for p in range(rows_n)])  22.4 us
    pallas_call x1, Pallas kernels, pack_shifts(): call(kernel, 2, out_shape=tuple((jax.ShapeDtypeStruct((base,) + tiles.sha...  18.8 us
    pallas_call x2, Pallas kernels, extract(): call(kernel, 12, out_shape=(jax.ShapeDtypeStruct((tiles_n, 2, block, bloc...  14.6 us
    ppermute x7, starting transfers between devices, swap(): lax.ppermute(x, 'pcol', [(i, i ^ 1) for i in range(low * LINES, high * LI...  14.5 us
    unnamed x44, local copies, waits for them, and re-layouts  14.3 us
  transfers between devices with their start and end apart: 35, of which 10 were waited for; matrix products, arithmetic and copies ran while one was open for 15% of the time, Pallas kernels for 13%

profile of v2, /device:TPU:29, one launch (start us, length us, event | category | flops | bytes accessed | tf_op | source)
XLA Modules:
  0.0 318.0 jit_solution(12538027281376866352)
XLA Ops:
  6.5 2.8 pack_streams.1.rest_8_.rest_0_
  9.3 2.1 collective-permute-start.12
  14.3 18.8 %pack_shifts.1 = (f32[4,2,128,128]{3,2,1,0:T(8,128)}, f32[4,2,128,128]{3,2,1,0:T(8,128)S(1)}, f32[4,2,128,128]{3,2,1,0:T(8,128)S(1)}, f32[4,2,128,128]{3,2,1,0:T...) custom-call(s32[32]{0:T(128)} %bitcast.5.ids_ref, ...), custom_call_target="tpu_custom_call" | custom-call | tf_op jit(solution)/shard_map/pack_shifts/pallas_call | solution.py:115
  37.9 1.9 collective-permute-start.3
  49.1 3.3 %collective-permute-start.1 = (s32[2,32]{1,0:T(2,128)S(1)}, s32[2,32]{1,0:T(2,128)S(1)}, u32[]{:S(2)}, u32[]{:S(2)}) collective-permute-start(s32[2,32]{1,0:T(2,128)S(1)} %pad_add_fusion.5), channel_id=1, source_target_pairs={{0,2},{1,3},{2,0},{3,1},{4,6},{5,7},{6,4},{7,5},{8,10},{9,11},{10,... | collective-permute-start | bytes 776 | tf_op jit(solution)/shard_map/ppermute | solution.py:458
  61.0 1.7 collective-permute-start.16
  68.6 3.5 %collective-permute-start.23 = (s32[8,128]{1,0:T(8,128)S(1)}, s32[8,128]{1,0:T(8,128)S(1)}, u32[]{:S(2)}, u32[]{:S(2)}) collective-permute-start(s32[8,128]{1,0:T(8,128)S(1)} %broadcast_in_dim.311), channel_id=1, source_target_pairs={{0,8},{8,0},{16,24},{24,16},{1,9},{9,1},{17,25},{25,17},{2,10},{10... | collective-permute-start | bytes 12296 | tf_op jit(solution)/shard_map/ppermute | solution.py:473
  75.2 2.8 collective-permute-done.24
  81.5 7.8 %collective-permute-done.15.rest_14_.rest_6_ = f32[9,2,128,128]{3,2,1,0:T(8,128)} collective-permute-done((f32[9,2,128,128]{3,2,1,0:T(8,128)S(1)}, f32[9,2,128,128]{3,2,1,0:T(8,128)}, u32[]{:S(2)}, u32[]{:S(2)}) %collective-permute-start.15) | collective-permute-done | bytes 1179680 | tf_op jit(solution)/shard_map/ppermute | solution.py:444
  96.4 28.8 %collective-permute-done.4.rest_2_ = f32[4,2,128,128]{3,2,1,0:T(8,128)S(1)} collective-permute-done((f32[4,2,128,128]{3,2,1,0:T(8,128)}, f32[4,2,128,128]{3,2,1,0:T(8,128)S(1)}, u32[]{:S(2)}, u32[]{:S(2)}) %collective-permute-start.4) | collective-permute-done | bytes 524320 | tf_op jit(solution)/shard_map/ppermute | solution.py:453
  126.0 2.9 collective-permute-start.13
  134.4 2.4 collective-permute-start.17
  138.5 2.9 collective-permute-start.21
  153.0 21.0 %collective-permute-start.6 = (f32[4,2,128,128]{3,2,1,0:T(8,128)}, f32[4,2,128,128]{3,2,1,0:T(8,128)}, u32[]{:S(2)}, u32[]{:S(2)}) collective-permute-start(f32[4,2,128,128]{3,2,1,0:T(8,128)} %copy-done.13), channel_id=1, source_target_pairs={{0,4},{1,5},{2,6},{3,7},{6,2},{7,3},{8,12},{9,13},{10,14},{11,15},... | collective-permute-start | bytes 1572872 | tf_op jit(solution)/shard_map/ppermute | solution.py:453
  174.0 10.8 %collective-permute-done.17.rest_16_.rest_8_ = f32[9,2,128,128]{3,2,1,0:T(8,128)} collective-permute-done((f32[9,2,128,128]{3,2,1,0:T(8,128)}, f32[9,2,128,128]{3,2,1,0:T(8,128)}, u32[]{:S(2)}, u32[]{:S(2)}) %collective-permute-start.17) | collective-permute-done | bytes 1179680 | tf_op jit(solution)/shard_map/ppermute | solution.py:438
  184.8 1.9 collective-permute-start.7
  186.7 2.0 collective-permute-start.8
  188.8 33.9 %collective-permute-done.21.rest_20_.rest_12_ = f32[9,2,128,128]{3,2,1,0:T(8,128)} collective-permute-done((f32[9,2,128,128]{3,2,1,0:T(8,128)}, f32[9,2,128,128]{3,2,1,0:T(8,128)}, u32[]{:S(2)}, u32[]{:S(2)}) %collective-permute-start.21) | collective-permute-done | bytes 1179680 | tf_op jit(solution)/shard_map/ppermute | solution.py:438
  222.7 1.9 collective-permute-start.9
  227.9 7.9 %panel_rows.1 = (f32[32,2,128,128]{3,2,1,0:T(8,128)S(1)}, f32[4,128,128]{2,1,0:T(8,128)S(1)}, f32[4,128,128]{2,1,0:T(8,128)}, f32[4,128,128]{2,1,0:T(8,128)}) custom-call(s32[166]{0:T(256)S(1)} %pad_add_fusion.6.table_ref, s32[256]{0:T(256)S(1)} %get-tuple-element.105.rows_ref, s32[1]{0:T(128)S(6)} %select_n.531.odd_ref, ...), custom_call_target="tpu_custom_call" | custom-call | tf_op jit(solution)/shard_map/panel_rows/pallas_call | solution.py:180
  235.8 2.0 copy-done
  238.5 8.2 %collective-permute-start.30 = (f32[4,128,128]{2,1,0:T(8,128)}, f32[4,128,128]{2,1,0:T(8,128)}, u32[]{:S(2)}, u32[]{:S(2)}) collective-permute-start(f32[4,128,128]{2,1,0:T(8,128)} %get-tuple-element.67), channel_id=1, source_target_pairs={{0,8},{8,0},{16,24},{24,16},{1,9},{9,1},{17,25},{25,17},{2,10},{10... | collective-permute-start | bytes 786440 | tf_op jit(solution)/shard_map/ppermute | solution.py:193
  250.4 6.7 %own_rows.1 = (f32[32,2,128,128]{3,2,1,0:T(8,128)S(1)}, f32[4,128,128]{2,1,0:T(8,128)S(1)}, f32[4,128,128]{2,1,0:T(8,128)}, f32[4,128,128]{2,1,0:T(8,128)}) custom-call(s32[226]{0:T(256)S(1)} %concatenate.86.table_ref, s32[256]{0:T(256)S(1)} %get-tuple-element.105.rows_ref, s32[1]{0:T(128)S(6)} %select_n.531.odd_ref, f32[32,2,128,128]{3,2,1,0:T(8,128)} %bitcast.31, ...), custom_call_target="tpu_custom_call" | custom-call | tf_op jit(solution)/shard_map/own_rows/pallas_call | solution.py:180
  257.2 2.0 copy-done.2
  261.5 6.0 %collective-permute-start.31 = (f32[4,128,128]{2,1,0:T(8,128)S(1)}, f32[4,128,128]{2,1,0:T(8,128)S(1)}, u32[]{:S(2)}, u32[]{:S(2)}) collective-permute-start(f32[4,128,128]{2,1,0:T(8,128)S(1)} %add.401), channel_id=1, source_target_pairs={{0,16},{8,24},{16,0},{24,8},{1,17},{9,25},{17,1},{25,9},{2,18},{10... | collective-permute-start | bytes 786440 | tf_op jit(solution)/shard_map/ppermute | solution.py:193
  269.8 2.2 collective-permute-start.26
  274.5 3.9 %collective-permute-done.31 = f32[4,128,128]{2,1,0:T(8,128)S(1)} collective-permute-done((f32[4,128,128]{2,1,0:T(8,128)S(1)}, f32[4,128,128]{2,1,0:T(8,128)S(1)}, u32[]{:S(2)}, u32[]{:S(2)}) %collective-permute-start.31) | collective-permute-done | bytes 262176 | tf_op jit(solution)/shard_map/ppermute | solution.py:193
  280.1 3.9 %collective-permute-done.28 = f32[4,128,128]{2,1,0:T(8,128)S(1)} collective-permute-done((f32[4,128,128]{2,1,0:T(8,128)}, f32[4,128,128]{2,1,0:T(8,128)S(1)}, u32[]{:S(2)}, u32[]{:S(2)}) %collective-permute-start.28) | collective-permute-done | bytes 262176 | tf_op jit(solution)/shard_map/ppermute | solution.py:198
  285.7 3.9 %collective-permute-done.26 = f32[4,128,128]{2,1,0:T(8,128)S(1)} collective-permute-done((f32[4,128,128]{2,1,0:T(8,128)S(1)}, f32[4,128,128]{2,1,0:T(8,128)S(1)}, u32[]{:S(2)}, u32[]{:S(2)}) %collective-permute-start.26) | collective-permute-done | bytes 262176 | tf_op jit(solution)/shard_map/ppermute | solution.py:193
  290.8 2.2 copy-done.1
  293.0 8.7 %panel_factors.1 = (bf16[2048,512]{1,0:T(8,128)(2,1)S(1)}, bf16[2048,512]{1,0:T(8,128)(2,1)S(1)}, f32[128,256]{1,0:T(8,128)S(1)}) custom-call(s32[256]{0:T(256)S(1)} %get-tuple-element.106.tgt, s32[1]{0:T(128)} %bitcast.3.row_ref, f32[32,2,128,128]{3,2,1,0:T(8,128)S(1)} %copy-done.1, f32[4,128,128]{2,1,0:T(8,128)S(1)} %add.402.new_a, ...), custom_call_target="tpu_custom_call" | custom-call | tf_op jit(solution)/shard_map/panel_factors/pallas_call | solution.py:306
  301.7 9.5 %update.1 = f32[2,2048,256]{2,1,0:T(8,128)} custom-call(s32[256]{0:T(256)S(1)} %get-tuple-element.106.tgt, s32[1]{0:T(128)} %bitcast.3.row_ref, s32[1]{0:T(128)} %bitcast.4.me_ref.col_ref, f32[32,2,128,128]{3,2,1,0:T(8,128)S(1)} %copy-done.3, f32[4,128,128]{2,1,0:T(8,128)S(1)} %add.397.new_a, f32[4,128,128]{2,1,0:T(8,128)S(1)} %collective-permute-done.27.new_b, ...), custom_call_target="tpu_custom_call" | custom-call | tf_op jit(solution)/shard_map/update/pallas_call | solution.py:395
  (162 shorter events, 83.1 us)
Async XLA Ops:
  9.3 51.7 %collective-permute-start.12 = (f32[9,2,128,128]{3,2,1,0:T(8,128)S(1)}, f32[9,2,128,128]{3,2,1,0:T(8,128)S(1)}, u32[]{:S(2)}, u32[]{:S(2)}) collective-permute-start(f32[9,2,128,128]{3,2,1,0:T(8,128)S(1)} %pack_streams.1.rest_8_.rest_0_), channel_id=1, source_target_pairs={{2,0},{3,1},{4,2},{5,3},{6,4},{7,5},{10,8},{11,9},{12,10},{13,11},... | collective-permute-start | bytes 3538952 | tf_op jit(solution)/shard_map/ppermute | solution.py:445
  11.4 51.3 %collective-permute-start.11 = (f32[9,2,128,128]{3,2,1,0:T(8,128)S(1)}, f32[9,2,128,128]{3,2,1,0:T(8,128)S(1)}, u32[]{:S(2)}, u32[]{:S(2)}) collective-permute-start(f32[9,2,128,128]{3,2,1,0:T(8,128)S(1)} %pack_streams.1.rest_8_.rest_0_), channel_id=1, source_target_pairs={{0,2},{1,3},{2,4},{3,5},{4,6},{5,7},{8,10},{9,11},{10,12},{11,13},... | collective-permute-start | bytes 3538952 | tf_op jit(solution)/shard_map/ppermute | solution.py:444
  12.7 120.0 %collective-permute-start.10 = (f32[9,2,128,128]{3,2,1,0:T(8,128)S(1)}, f32[9,2,128,128]{3,2,1,0:T(8,128)}, u32[]{:S(2)}, u32[]{:S(2)}) collective-permute-start(f32[9,2,128,128]{3,2,1,0:T(8,128)S(1)} %pack_streams.1.rest_8_.rest_0_), channel_id=1, source_target_pairs={{0,1},{1,0},{2,3},{3,2},{4,5},{5,4},{6,7},{7,6},{8,9},{9,8},{10,11... | collective-permute-start | bytes 3538952 | tf_op jit(solution)/shard_map/ppermute | solution.py:438
  14.0 34.4 %collective-permute-start = (s32[1,32]{1,0:T(1,128)}, s32[1,32]{1,0:T(1,128)}, u32[]{:S(2)}, u32[]{:S(2)}) collective-permute-start(s32[1,32]{1,0:T(1,128)} %bitcast.7), channel_id=1, source_target_pairs={{0,1},{1,0},{2,3},{3,2},{4,5},{5,4},{6,7},{7,6},{8,9},{9,8},{10,11... | collective-permute-start | bytes 392 | tf_op jit(solution)/shard_map/ppermute | solution.py:458
  37.9 55.2 %collective-permute-start.3 = (f32[4,2,128,128]{3,2,1,0:T(8,128)}, f32[4,2,128,128]{3,2,1,0:T(8,128)}, u32[]{:S(2)}, u32[]{:S(2)}) collective-permute-start(f32[4,2,128,128]{3,2,1,0:T(8,128)} %get-tuple-element.54), channel_id=1, source_target_pairs={{1,2},{2,3},{3,4},{4,5},{5,6},{6,7},{9,10},{10,11},{11,12},{12,13}... | collective-permute-start | bytes 1572872 | tf_op jit(solution)/shard_map/ppermute | solution.py:453
  61.0 18.8 %collective-permute-start.16 = (f32[9,2,128,128]{3,2,1,0:T(8,128)S(1)}, f32[9,2,128,128]{3,2,1,0:T(8,128)}, u32[]{:S(2)}, u32[]{:S(2)}) collective-permute-start(f32[9,2,128,128]{3,2,1,0:T(8,128)S(1)} %collective-permute-done.12.rest_11_.rest_3_), channel_id=1, source_target_pairs={{2,0},{3,1},{4,2},{5,3},{10,8},{11,9},{12,10},{13,11},{18,16},{19,... | collective-permute-start | bytes 3538952 | tf_op jit(solution)/shard_map/ppermute | solution.py:445
  62.7 26.6 %collective-permute-start.15 = (f32[9,2,128,128]{3,2,1,0:T(8,128)S(1)}, f32[9,2,128,128]{3,2,1,0:T(8,128)}, u32[]{:S(2)}, u32[]{:S(2)}) collective-permute-start(f32[9,2,128,128]{3,2,1,0:T(8,128)S(1)} %collective-permute-done.11.rest_10_.rest_2_), channel_id=1, source_target_pairs={{2,4},{3,5},{4,6},{5,7},{10,12},{11,13},{12,14},{13,15},{18,20},{1... | collective-permute-start | bytes 3538952 | tf_op jit(solution)/shard_map/ppermute | solution.py:444
  68.6 5.8 %collective-permute-start.23 = (s32[8,128]{1,0:T(8,128)S(1)}, s32[8,128]{1,0:T(8,128)S(1)}, u32[]{:S(2)}, u32[]{:S(2)}) collective-permute-start(s32[8,128]{1,0:T(8,128)S(1)} %broadcast_in_dim.311), channel_id=1, source_target_pairs={{0,8},{8,0},{16,24},{24,16},{1,9},{9,1},{17,25},{25,17},{2,10},{10... | collective-permute-start | bytes 12296 | tf_op jit(solution)/shard_map/ppermute | solution.py:473
  78.0 56.4 %collective-permute-start.14 = (f32[9,2,128,128]{3,2,1,0:T(8,128)S(1)}, f32[9,2,128,128]{3,2,1,0:T(8,128)}, u32[]{:S(2)}, u32[]{:S(2)}) collective-permute-start(f32[9,2,128,128]{3,2,1,0:T(8,128)S(1)} %collective-permute-done.12.rest_11_.rest_3_), channel_id=1, source_target_pairs={{0,1},{1,0},{2,3},{3,2},{4,5},{5,4},{8,9},{9,8},{10,11},{11,10},{1... | collective-permute-start | bytes 3538952 | tf_op jit(solution)/shard_map/ppermute | solution.py:438
  79.7 57.1 %collective-permute-start.20 = (f32[9,2,128,128]{3,2,1,0:T(8,128)}, f32[9,2,128,128]{3,2,1,0:T(8,128)}, u32[]{:S(2)}, u32[]{:S(2)}) collective-permute-start(f32[9,2,128,128]{3,2,1,0:T(8,128)} %collective-permute-done.16.rest_15_.rest_7_), channel_id=1, source_target_pairs={{2,0},{3,1},{10,8},{11,9},{18,16},{19,17},{26,24},{27,25}} | collective-permute-start | bytes 3538952 | tf_op jit(solution)/shard_map/ppermute | solution.py:445
  89.3 49.3 %collective-permute-start.19 = (f32[9,2,128,128]{3,2,1,0:T(8,128)}, f32[9,2,128,128]{3,2,1,0:T(8,128)}, u32[]{:S(2)}, u32[]{:S(2)}) collective-permute-start(f32[9,2,128,128]{3,2,1,0:T(8,128)} %collective-permute-done.15.rest_14_.rest_6_), channel_id=1, source_target_pairs={{4,6},{5,7},{12,14},{13,15},{20,22},{21,23},{28,30},{29,31}} | collective-permute-start | bytes 3538952 | tf_op jit(solution)/shard_map/ppermute | solution.py:444
  93.1 32.1 %collective-permute-start.4 = (f32[4,2,128,128]{3,2,1,0:T(8,128)}, f32[4,2,128,128]{3,2,1,0:T(8,128)S(1)}, u32[]{:S(2)}, u32[]{:S(2)}) collective-permute-start(f32[4,2,128,128]{3,2,1,0:T(8,128)} %copy-done.15), channel_id=1, source_target_pairs={{0,2},{1,3},{2,4},{3,5},{4,6},{5,7},{8,10},{9,11},{10,12},{11,13},... | collective-permute-start | bytes 1572872 | tf_op jit(solution)/shard_map/ppermute | solution.py:453
  126.0 24.4 %collective-permute-start.13 = (f32[9,2,128,128]{3,2,1,0:T(8,128)S(1)}, f32[9,2,128,128]{3,2,1,0:T(8,128)}, u32[]{:S(2)}, u32[]{:S(2)}) collective-permute-start(f32[9,2,128,128]{3,2,1,0:T(8,128)S(1)} %collective-permute-done.11.rest_10_.rest_2_), channel_id=1, source_target_pairs={{2,3},{3,2},{4,5},{5,4},{6,7},{7,6},{10,11},{11,10},{12,13},{13,12... | collective-permute-start | bytes 3538952 | tf_op jit(solution)/shard_map/ppermute | solution.py:438
  132.7 20.2 %collective-permute-start.18 = (f32[9,2,128,128]{3,2,1,0:T(8,128)}, f32[9,2,128,128]{3,2,1,0:T(8,128)}, u32[]{:S(2)}, u32[]{:S(2)}) collective-permute-start(f32[9,2,128,128]{3,2,1,0:T(8,128)} %collective-permute-done.16.rest_15_.rest_7_), channel_id=1, source_target_pairs={{0,1},{1,0},{2,3},{3,2},{8,9},{9,8},{10,11},{11,10},{16,17},{17,16... | collective-permute-start | bytes 3538952 | tf_op jit(solution)/shard_map/ppermute | solution.py:438
  134.4 50.4 %collective-permute-start.17 = (f32[9,2,128,128]{3,2,1,0:T(8,128)}, f32[9,2,128,128]{3,2,1,0:T(8,128)}, u32[]{:S(2)}, u32[]{:S(2)}) collective-permute-start(f32[9,2,128,128]{3,2,1,0:T(8,128)} %collective-permute-done.15.rest_14_.rest_6_), channel_id=1, source_target_pairs={{4,5},{5,4},{6,7},{7,6},{12,13},{13,12},{14,15},{15,14},{20,21},{2... | collective-permute-start | bytes 3538952 | tf_op jit(solution)/shard_map/ppermute | solution.py:438
  136.8 49.9 %collective-permute-start.22 = (f32[9,2,128,128]{3,2,1,0:T(8,128)}, f32[9,2,128,128]{3,2,1,0:T(8,128)}, u32[]{:S(2)}, u32[]{:S(2)}) collective-permute-start(f32[9,2,128,128]{3,2,1,0:T(8,128)} %collective-permute-done.20.rest_19_.rest_11_), channel_id=1, source_target_pairs={{0,1},{1,0},{8,9},{9,8},{16,17},{17,16},{24,25},{25,24}} | collective-permute-start | bytes 3538952 | tf_op jit(solution)/shard_map/ppermute | solution.py:438
  138.5 84.2 %collective-permute-start.21 = (f32[9,2,128,128]{3,2,1,0:T(8,128)}, f32[9,2,128,128]{3,2,1,0:T(8,128)}, u32[]{:S(2)}, u32[]{:S(2)}) collective-permute-start(f32[9,2,128,128]{3,2,1,0:T(8,128)} %collective-permute-done.19.rest_18_.rest_10_), channel_id=1, source_target_pairs={{6,7},{7,6},{14,15},{15,14},{22,23},{23,22},{30,31},{31,30}} | collective-permute-start | bytes 3538952 | tf_op jit(solution)/shard_map/ppermute | solution.py:438
  150.5 88.0 %collective-permute-start.5 = (f32[4,2,128,128]{3,2,1,0:T(8,128)}, f32[4,2,128,128]{3,2,1,0:T(8,128)}, u32[]{:S(2)}, u32[]{:S(2)}) collective-permute-start(f32[4,2,128,128]{3,2,1,0:T(8,128)} %copy-done.14), channel_id=1, source_target_pairs={{0,3},{1,4},{2,5},{3,6},{4,7},{7,2},{8,11},{9,12},{10,13},{11,14},... | collective-permute-start | bytes 1572872 | tf_op jit(solution)/shard_map/ppermute | solution.py:453
  153.0 96.4 %collective-permute-start.6 = (f32[4,2,128,128]{3,2,1,0:T(8,128)}, f32[4,2,128,128]{3,2,1,0:T(8,128)}, u32[]{:S(2)}, u32[]{:S(2)}) collective-permute-start(f32[4,2,128,128]{3,2,1,0:T(8,128)} %copy-done.13), channel_id=1, source_target_pairs={{0,4},{1,5},{2,6},{3,7},{6,2},{7,3},{8,12},{9,13},{10,14},{11,15},... | collective-permute-start | bytes 1572872 | tf_op jit(solution)/shard_map/ppermute | solution.py:453
  184.8 64.5 %collective-permute-start.7 = (f32[4,2,128,128]{3,2,1,0:T(8,128)}, f32[4,2,128,128]{3,2,1,0:T(8,128)}, u32[]{:S(2)}, u32[]{:S(2)}) collective-permute-start(f32[4,2,128,128]{3,2,1,0:T(8,128)} %copy-done.12), channel_id=1, source_target_pairs={{0,5},{1,6},{2,7},{5,2},{6,3},{7,4},{8,13},{9,14},{10,15},{13,10},... | collective-permute-start | bytes 1572872 | tf_op jit(solution)/shard_map/ppermute | solution.py:453
  186.7 62.6 %collective-permute-start.8 = (f32[4,2,128,128]{3,2,1,0:T(8,128)}, f32[4,2,128,128]{3,2,1,0:T(8,128)}, u32[]{:S(2)}, u32[]{:S(2)}) collective-permute-start(f32[4,2,128,128]{3,2,1,0:T(8,128)} %copy-done.11), channel_id=1, source_target_pairs={{0,6},{1,7},{4,2},{5,3},{6,4},{7,5},{8,14},{9,15},{12,10},{13,11},... | collective-permute-start | bytes 1572872 | tf_op jit(solution)/shard_map/ppermute | solution.py:453
  222.7 26.7 %collective-permute-start.9 = (f32[4,2,128,128]{3,2,1,0:T(8,128)}, f32[4,2,128,128]{3,2,1,0:T(8,128)}, u32[]{:S(2)}, u32[]{:S(2)}) collective-permute-start(f32[4,2,128,128]{3,2,1,0:T(8,128)} %copy-done.10), channel_id=1, source_target_pairs={{0,7},{3,2},{4,3},{5,4},{6,5},{7,6},{8,15},{11,10},{12,11},{13,12}... | collective-permute-start | bytes 1572872 | tf_op jit(solution)/shard_map/ppermute | solution.py:453
  238.5 22.0 %collective-permute-start.30 = (f32[4,128,128]{2,1,0:T(8,128)}, f32[4,128,128]{2,1,0:T(8,128)}, u32[]{:S(2)}, u32[]{:S(2)}) collective-permute-start(f32[4,128,128]{2,1,0:T(8,128)} %get-tuple-element.67), channel_id=1, source_target_pairs={{0,8},{8,0},{16,24},{24,16},{1,9},{9,1},{17,25},{25,17},{2,10},{10... | collective-permute-start | bytes 786440 | tf_op jit(solution)/shard_map/ppermute | solution.py:193
  259.2 9.6 %collective-permute-start.25 = (f32[4,128,128]{2,1,0:T(8,128)}, f32[4,128,128]{2,1,0:T(8,128)S(1)}, u32[]{:S(2)}, u32[]{:S(2)}) collective-permute-start(f32[4,128,128]{2,1,0:T(8,128)} %get-tuple-element.63), channel_id=1, source_target_pairs={{0,8},{8,0},{16,24},{24,16},{1,9},{9,1},{17,25},{25,17},{2,10},{10... | collective-permute-start | bytes 786440 | tf_op jit(solution)/shard_map/ppermute | solution.py:193
  259.2 13.6 %collective-permute-start.33 = (f32[4,128,128]{2,1,0:T(8,128)}, f32[4,128,128]{2,1,0:T(8,128)S(1)}, u32[]{:S(2)}, u32[]{:S(2)}) collective-permute-start(f32[4,128,128]{2,1,0:T(8,128)} %get-tuple-element.68), channel_id=1, source_target_pairs={{0,16},{8,24},{1,17},{9,25},{2,18},{10,26},{3,19},{11,27},{4,20},{... | collective-permute-start | bytes 786440 | tf_op jit(solution)/shard_map/ppermute | solution.py:198
  261.5 16.9 %collective-permute-start.31 = (f32[4,128,128]{2,1,0:T(8,128)S(1)}, f32[4,128,128]{2,1,0:T(8,128)S(1)}, u32[]{:S(2)}, u32[]{:S(2)}) collective-permute-start(f32[4,128,128]{2,1,0:T(8,128)S(1)} %add.401), channel_id=1, source_target_pairs={{0,16},{8,24},{16,0},{24,8},{1,17},{9,25},{17,1},{25,9},{2,18},{10... | collective-permute-start | bytes 786440 | tf_op jit(solution)/shard_map/ppermute | solution.py:193
  267.5 16.6 %collective-permute-start.28 = (f32[4,128,128]{2,1,0:T(8,128)}, f32[4,128,128]{2,1,0:T(8,128)S(1)}, u32[]{:S(2)}, u32[]{:S(2)}) collective-permute-start(f32[4,128,128]{2,1,0:T(8,128)} %get-tuple-element.64), channel_id=1, source_target_pairs={{0,16},{8,24},{1,17},{9,25},{2,18},{10,26},{3,19},{11,27},{4,20},{... | collective-permute-start | bytes 786440 | tf_op jit(solution)/shard_map/ppermute | solution.py:198
  269.8 19.9 %collective-permute-start.26 = (f32[4,128,128]{2,1,0:T(8,128)S(1)}, f32[4,128,128]{2,1,0:T(8,128)S(1)}, u32[]{:S(2)}, u32[]{:S(2)}) collective-permute-start(f32[4,128,128]{2,1,0:T(8,128)S(1)} %add.396), channel_id=1, source_target_pairs={{0,16},{8,24},{16,0},{24,8},{1,17},{9,25},{17,1},{25,9},{2,18},{10... | collective-permute-start | bytes 786440 | tf_op jit(solution)/shard_map/ppermute | solution.py:193
  272.8 17.9 %collective-permute-start.34 = (f32[4,128,128]{2,1,0:T(8,128)S(1)}, f32[4,128,128]{2,1,0:T(8,128)S(1)}, u32[]{:S(2)}, u32[]{:S(2)}) collective-permute-start(f32[4,128,128]{2,1,0:T(8,128)S(1)} %broadcast_select_fusion.old_a), channel_id=1, source_target_pairs={{0,8},{8,0},{16,24},{24,16},{1,9},{9,1},{17,25},{25,17},{2,10},{10... | collective-permute-start | bytes 786440 | tf_op jit(solution)/shard_map/ppermute | solution.py:193
  278.4 12.3 %collective-permute-start.32 = (f32[4,128,128]{2,1,0:T(8,128)S(1)}, f32[4,128,128]{2,1,0:T(8,128)S(1)}, u32[]{:S(2)}, u32[]{:S(2)}) collective-permute-start(f32[4,128,128]{2,1,0:T(8,128)S(1)} %add.402.new_a), channel_id=1, source_target_pairs={{0,8},{8,0},{16,24},{24,16},{1,9},{9,1},{17,25},{25,17},{2,10},{10... | collective-permute-start | bytes 786440 | tf_op jit(solution)/shard_map/ppermute | solution.py:193
  284.1 17.6 %collective-permute-start.29 = (f32[4,128,128]{2,1,0:T(8,128)S(1)}, f32[4,128,128]{2,1,0:T(8,128)S(1)}, u32[]{:S(2)}, u32[]{:S(2)}) collective-permute-start(f32[4,128,128]{2,1,0:T(8,128)S(1)} %broadcast_select_fusion.1.old_a), channel_id=1, source_target_pairs={{0,8},{8,0},{16,24},{24,16},{1,9},{9,1},{17,25},{25,17},{2,10},{10... | collective-permute-start | bytes 786440 | tf_op jit(solution)/shard_map/ppermute | solution.py:193
  289.7 12.0 %collective-permute-start.27 = (f32[4,128,128]{2,1,0:T(8,128)S(1)}, f32[4,128,128]{2,1,0:T(8,128)S(1)}, u32[]{:S(2)}, u32[]{:S(2)}) collective-permute-start(f32[4,128,128]{2,1,0:T(8,128)S(1)} %add.397.new_a), channel_id=1, source_target_pairs={{0,8},{8,0},{16,24},{24,16},{1,9},{9,1},{17,25},{25,17},{2,10},{10... | collective-permute-start | bytes 786440 | tf_op jit(solution)/shard_map/ppermute | solution.py:193
  (25 other events, 170.6 us)

commit v3 on v2

v3 whole, which is shorter than its diff:
```python
import functools

import jax
import jax.numpy as jnp
from jax import lax
from jax.experimental import pallas as pl
from jax.experimental.pallas import tpu as pltpu
from jax.sharding import PartitionSpec as P

CBLK = 2
LINES = 2
F32 = jnp.float32
BF16 = jnp.bfloat16
MIB = 1024 * 1024
META = 128

ANY = pl.BlockSpec(memory_space=pl.ANY)
SMEM = pl.BlockSpec(memory_space=pltpu.SMEM)
VMEM = pl.BlockSpec(memory_space=pltpu.VMEM)
HBM = pl.BlockSpec(memory_space=pltpu.HBM)


def call(kernel, mib, **kw):
    return pl.pallas_call(
        kernel,
        compiler_params=pltpu.CompilerParams(vmem_limit_bytes=mib * MIB),
        cost_estimate=pl.CostEstimate(flops=0, bytes_accessed=0, transcendentals=0),
        **kw,
    )


def list_slots(ids_ref, pos, meta, slots, cols_n, base, excess_max):
    first = cols_n * base
    for n in range(first + excess_max):
        meta[n] = -1
        pos[n] = 0
    for o in range(cols_n + 1):
        pos[first + excess_max + o] = 0

    def one(j, carry):
        t = ids_ref[j]
        owner = t & (cols_n - 1)
        r = pos[first + excess_max + owner]
        pos[first + excess_max + owner] = r + 1
        e = pos[first + excess_max + cols_n]
        over = (r >= base).astype(jnp.int32)
        pos[first + excess_max + cols_n] = e + over
        at = jnp.where(r >= base, first + e, owner * base + r)
        pos[at] = j
        meta[at] = t
        return carry

    lax.fori_loop(0, slots, one, 0)
    meta[first + excess_max] = pos[first + excess_max + cols_n]


def pack(tiles, ids, me, cols_n, base, excess_max):
    slots = tiles.shape[0]
    count = LINES * base + 1
    first = cols_n * base

    def kernel(ids_ref, me_ref, tiles_ref, stream_ref, *rest):
        outs, (meta, held, pos, sems) = rest[: cols_n - 1], rest[cols_n - 1 :]
        list_slots(ids_ref, pos, meta, slots, cols_n, base, excess_max)
        moves = []
        for n in range(count):
            at = n if n < LINES * base else first
            moves.append((meta[at] >= 0, pos[at], stream_ref.at[n]))
        for k in range(1, cols_n):
            owner = me_ref[0] ^ k
            for r in range(base):
                at = owner * base + r
                moves.append(((meta[at] >= 0) & (owner >= LINES), pos[at], outs[k - 1].at[r]))
        for n, (cond, slot, _) in enumerate(moves):

            @pl.when(cond)
            def _(n=n, slot=slot):
                pltpu.make_async_copy(tiles_ref.at[slot], held.at[n], sems.at[0, n]).start()

        for n, (cond, slot, dst) in enumerate(moves):

            @pl.when(cond)
            def _(n=n, slot=slot, dst=dst):
                pltpu.make_async_copy(tiles_ref.at[slot], held.at[n], sems.at[0, n]).wait()
                pltpu.make_async_copy(held.at[n], dst, sems.at[1, n]).start()

        for n, (cond, _, dst) in enumerate(moves):

            @pl.when(cond)
            def _(n=n, dst=dst):
                pltpu.make_async_copy(held.at[n], dst, sems.at[1, n]).wait()

    one = tiles.shape[1:]
    total = count + (cols_n - 1) * base
    got = call(
        kernel,
        8,
        out_shape=(pltpu.HBM((count,) + one, F32),)
        + tuple(pltpu.HBM((base,) + one, F32) for _ in range(1, cols_n))
        + (jax.ShapeDtypeStruct((META,), jnp.int32),),
        in_specs=[SMEM, SMEM, HBM],
        out_specs=tuple(HBM for _ in range(cols_n)) + (SMEM,),
        scratch_shapes=[
            pltpu.VMEM((total,) + one, F32),
            pltpu.SMEM((first + excess_max + cols_n + 1,), jnp.int32),
            pltpu.SemaphoreType.DMA((2, total)),
        ],
        name="pack",
    )(ids, me, tiles)
    return got[0], got[1:-1], got[-1]


def unwritten(shape):
    def kernel(out_ref):
        pass

    return call(kernel, 2, out_shape=jax.ShapeDtypeStruct(shape, F32), out_specs=HBM, name="unwritten")()


def extract(
    parts, origins, rest, near, ids, source_rows, me, odd, cols_n, base, tiles=None, arrived=(), arrived_from=()
):
    block = rest.shape[-1]
    bits = block.bit_length() - 1
    width = CBLK * cols_n
    width_bits, cols_bits = width.bit_length() - 1, cols_n.bit_length() - 1
    wide = 2 * CBLK
    own = tiles is not None
    count = LINES * base + 1
    depth = cols_n // LINES
    tiles_n = ids.shape[0]
    first = cols_n * base
    per = rest.shape[0] // cols_n

    def kernel(near_ref, ids_ref, rows_ref, me_ref, odd_ref, *rest_refs):
        part_refs, rest_refs = rest_refs[: len(parts)], rest_refs[len(parts) :]
        rest_ref, rest_refs = rest_refs[0], rest_refs[1:]
        if own:
            tiles_ref, arrived_refs = rest_refs[0], rest_refs[1 : 1 + len(arrived)]
        held_out, keep, send, top, held, sem, out_sem = rest_refs[-7:]
        me = me_ref[0]
        level, line = lax.shift_right_logical(me, 1), me & 1
        gathered = me < LINES

        def fetch(src, t, wanted):
            column = t & (width - 1)
            row = lax.shift_right_logical(t, width_bits)
            if own:
                ours = (column & (cols_n - 1)) == me
                place = row * CBLK + lax.shift_right_logical(column, cols_bits)
            else:
                ours = column < LINES
                place = row * CBLK + column

            @pl.when((t >= 0) & ours & wanted)
            def _():
                pltpu.make_async_copy(src, held.at[place], sem).start()

        if own:

            @pl.when(~gathered)
            def _():
                def one(j, carry):
                    fetch(tiles_ref.at[j], ids_ref[j], True)
                    return carry

                lax.fori_loop(0, tiles_n, one, 0)
                for ref, (k, pairs) in zip(arrived_refs, arrived_from):
                    here = functools.reduce(jnp.logical_or, [me == b for _, b in pairs])
                    for r in range(base):
                        fetch(ref.at[r], near_ref[k, me * base + r], here)

        for ref, (step, cross) in zip(part_refs, origins):
            if isinstance(step, tuple):
                by_level = step[0]
                for z in range(1, depth):
                    by_level = jnp.where(level == z, step[z], by_level)
                step = by_level
            at = level + step
            valid = (at >= 0) & (at < depth)
            source = at * LINES + (1 - line if cross else line)
            if own:
                valid = valid & (gathered | (source != me))

            @pl.when(valid)
            def _(ref=ref, source=source):
                k = source ^ me

                def streams():
                    for q in range(count - 1):
                        fetch(ref.at[q], near_ref[k, q], True)

                if own:
                    pl.when(gathered)(streams)
                else:
                    streams()
                fetch(ref.at[count - 1], near_ref[k, first], True)

        most = near_ref[0, first + per + 1]
        for k in range(1, cols_n):
            most = jnp.maximum(most, near_ref[k, first + per + 1])

        @pl.when(most > 1)
        def _():
            for k in range(cols_n):

                def one(e, carry, k=k):
                    fetch(rest_ref.at[k * per + e], near_ref[k, first + 1 + e], (gathered | (k > 0)) if own else True)
                    return carry

                lax.fori_loop(0, per, one, 0)

        pltpu.make_async_copy(held, held, sem).wait()
        copy_out = pltpu.make_async_copy(held, held_out, out_sem)
        copy_out.start()
        for m in range(CBLK):
            for c in range(2):
                top[2 * m + c] = held[m, c]
        for out, half in ((keep, odd_ref[0]), (send, 1 - odd_ref[0])):

            def pick(j, carry, out=out, half=half):
                row = rows_ref[half * block + j]
                here = row >= 0
                row = jnp.maximum(row, 0)
                tile = lax.shift_right_logical(row, bits) * CBLK
                inner = row & (block - 1)
                for m in range(CBLK):
                    for c in range(2):
                        value = held[tile + m, c, pl.ds(inner, 1), :]
                        out[2 * m + c, pl.ds(j, 1), :] = jnp.where(here, value, 0.0)
                return carry

            lax.fori_loop(0, block, pick, 0, unroll=8)
        copy_out.wait()

    part_rows = jax.ShapeDtypeStruct((wide, block, block), F32)
    operands = list(parts) + [rest] + ([tiles] + list(arrived) if own else [])
    operands = [pltpu.with_memory_space_constraint(x, pltpu.HBM) for x in operands]
    return call(
        kernel,
        12,
        out_shape=(pltpu.HBM((tiles_n, 2, block, block), F32), part_rows, part_rows, part_rows),
        in_specs=[SMEM] * 5 + [HBM] * len(operands),
        out_specs=(HBM, VMEM, VMEM, VMEM),
        scratch_shapes=[
            pltpu.VMEM((tiles_n, 2, block, block), F32),
            pltpu.SemaphoreType.DMA,
            pltpu.SemaphoreType.DMA,
        ],
        name="own_rows" if own else "panel_rows",
    )(near, ids, source_rows, me, odd, *operands)


def exchange(keep, send, top, my_row, rows_n):
    def cross(x, step):
        return lax.ppermute(x, "prow", [(p, p ^ step) for p in range(rows_n)])

    held = top
    step = 2
    while step < rows_n:
        got = lax.ppermute(held, "prow", [(p, p + step) for p in range(step)])
        held = jnp.where((my_row >= step) & (my_row < 2 * step), got, held)
        step *= 2
    total = keep + cross(send, 1)
    step = 2
    while step < rows_n:
        total = total + cross(total, step)
        step *= 2
    return (total, cross(total, 1)), (held, cross(held, 1))


def replace_rows(targets_ref, odd, old_refs, held, block):
    bits = block.bit_length() - 1

    spare = held.shape[0] - CBLK
    for ref, half in ((old_refs[0], odd), (old_refs[1], 1 - odd)):

        def one(j, carry, ref=ref, half=half):
            row = targets_ref[half * block + j]
            tile = jnp.where(row >= 0, lax.shift_right_logical(row, bits) * CBLK, spare)
            inner = row & (block - 1)
            for m in range(CBLK):
                for c in range(2):
                    held[tile + m, c, pl.ds(inner, 1), :] = ref[2 * m + c, pl.ds(j, 1), :]
            return carry

        lax.fori_loop(0, block, one, 0, unroll=8)


def split(x):
    high = x.astype(BF16)
    return high, (x - high.astype(F32)).astype(BF16)


def dot3(high, low, w_high, w_low):
    return (
        jnp.dot(high, w_high, preferred_element_type=F32)
        + jnp.dot(high, w_low, preferred_element_type=F32)
        + jnp.dot(low, w_high, preferred_element_type=F32)
    )


def store_complex(high_ref, low_ref, row, col, re, im):
    k, n = re.shape
    for r, c, value in ((0, 0, re), (0, 1, im), (1, 0, -im), (1, 1, re)):
        high, low = split(value)
        rows, cols = pl.ds(row + r * k, k), pl.ds(col + c * n, n)
        high_ref[rows, cols] = high
        low_ref[rows, cols] = low


def panel_factors(held, new, old, inverses, targets, my_row, group):
    block = held.shape[-1]
    row_tiles = held.shape[0] // CBLK
    rows = row_tiles * block

    def kernel(tgt, row_ref, held_in, new_a, new_b, old_a, old_b, inv_ref, high_ref, low_ref, top_ref, *rest):
        held_ref, new_ref, i0h, i0l, i1h, i1l, uh, ul, sem = rest
        odd = lax.rem(row_ref[0], 2)
        copy = pltpu.make_async_copy(held_in, held_ref.at[: CBLK * row_tiles], sem)
        copy.start()
        new_ref[odd] = new_a[...]
        new_ref[1 - odd] = new_b[...]
        store_complex(i0h, i0l, 0, 0, inv_ref[0, 0], inv_ref[0, 1])
        store_complex(i1h, i1l, 0, 0, inv_ref[1, 0], inv_ref[1, 1])
        store_complex(uh, ul, 0, 0, new_ref[0, 2], new_ref[0, 3])
        lower = dot3(
            *split(jnp.concatenate([new_ref[1, 0], new_ref[1, 1]], axis=1)), i0h[...], i0l[...]
        )
        top_ref[...] = lower
        copy.wait()
        replace_rows(tgt, odd, (old_a, old_b), held_ref, block)

        @pl.when(row_ref[0] == 1)
        def _():
            for m in range(CBLK):
                for c in range(2):
                    held_ref[m, c] = new_ref[1, 2 * m + c]

        def one(g, carry):
            x = [
                jnp.concatenate(
                    [
                        jnp.concatenate(
                            [held_ref[(g * group + t) * CBLK + m, 0], held_ref[(g * group + t) * CBLK + m, 1]], axis=1
                        )
                        for t in range(group)
                    ],
                    axis=0,
                )
                for m in range(CBLK)
            ]
            at = pl.ds(pl.multiple_of(g * (group * block), group * block), group * block)
            l0h, l0l = split(dot3(*split(x[0]), i0h[...], i0l[...]))
            high_ref[at, : 2 * block] = l0h
            low_ref[at, : 2 * block] = l0l
            y = x[1] - dot3(l0h, l0l, uh[...], ul[...])
            l1h, l1l = split(dot3(*split(y), i1h[...], i1l[...]))
            high_ref[at, 2 * block :] = l1h
            low_ref[at, 2 * block :] = l1l
            return carry

        lax.fori_loop(0, row_tiles // group, one, 0)

    wide = pltpu.VMEM((2 * block, 2 * block), BF16)
    return call(
        kernel,
        20,
        out_shape=(
            jax.ShapeDtypeStruct((rows, 4 * block), BF16),
            jax.ShapeDtypeStruct((rows, 4 * block), BF16),
            jax.ShapeDtypeStruct((block, 2 * block), F32),
        ),
        in_specs=[SMEM, SMEM, ANY] + [VMEM] * 5,
        out_specs=(VMEM, VMEM, VMEM),
        scratch_shapes=[pltpu.VMEM((held.shape[0] + CBLK,) + held.shape[1:], F32), pltpu.VMEM((2, 2 * CBLK, block, block), F32)]
        + [wide] * 6
        + [pltpu.SemaphoreType.DMA],
        name="panel_factors",
    )(targets, my_row, held, *new, *old, inverses)


def update(held, new, old, high, low, lower_top, targets, my_row, my_col, rows_n, group):
    block = held.shape[-1]
    row_tiles = held.shape[0] // CBLK
    rows = row_tiles * block
    steps = row_tiles // group
    span = group * block

    def kernel(tgt, row_ref, col_ref, held_in, new_a, new_b, old_a, old_b, high_in, low_in, top_ref, out_ref, *rest):
        held_ref, new_ref, high_ref, low_ref, res_ref, wh, wl, sem, in_sems, out_sems = rest
        odd = lax.rem(row_ref[0], 2)
        copy = pltpu.make_async_copy(held_in, held_ref.at[: CBLK * row_tiles], sem)
        copy.start()
        for g in range(steps):
            at = pl.ds(g * span, span)
            for n, (src, dst) in enumerate(((high_in, high_ref), (low_in, low_ref))):
                pltpu.make_async_copy(src.at[at], dst.at[at], in_sems.at[2 * g + n]).start()
        new_ref[odd] = new_a[...]
        new_ref[1 - odd] = new_b[...]
        for m in range(CBLK):
            store_complex(wh, wl, 0, 2 * m * block, new_ref[0, 2 * m], new_ref[0, 2 * m + 1])
        first = dot3(*split(top_ref[...]), wh[: 2 * block, :], wl[: 2 * block, :])
        second = []
        for n in range(2 * CBLK):
            second.append(new_ref[1, n] - first[:, n * block : (n + 1) * block])
            new_ref[1, n] = second[n]
        for m in range(CBLK):
            store_complex(wh, wl, 2 * block, 2 * m * block, second[2 * m], second[2 * m + 1])
        copy.wait()
        replace_rows(tgt, odd, (old_a, old_b), held_ref, block)
        for g in range(steps):
            at = pl.ds(g * span, span)
            for n, (src, dst) in enumerate(((high_in, high_ref), (low_in, low_ref))):
                pltpu.make_async_copy(src.at[at], dst.at[at], in_sems.at[2 * g + n]).wait()
            y = dot3(high_ref[at, :], low_ref[at, :], wh[...], wl[...])
            for t in range(group):
                tile = g * group + t
                for m in range(CBLK):
                    for c in range(2):
                        n = 2 * m + c
                        res_ref[c, tile * block : (tile + 1) * block, m * block : (m + 1) * block] = (
                            held_ref[tile * CBLK + m, c]
                            - y[t * block : (t + 1) * block, n * block : (n + 1) * block]
                        )
            for panel in range(2):

                @pl.when(col_ref[0] == panel)
                def _(panel=panel, at=at):
                    for c in range(2):
                        cols = slice((2 * panel + c) * block, (2 * panel + c + 1) * block)
                        res_ref[c, at, :block] = high_ref[at, cols].astype(F32) + low_ref[at, cols].astype(F32)

            if g == 0:
                for p in range(2):

                    @pl.when(row_ref[0] == p)
                    def _(p=p):
                        for c in range(2):
                            for m in range(CBLK):
                                res_ref[c, :block, m * block : (m + 1) * block] = new_ref[p, 2 * m + c]

                @pl.when((row_ref[0] == 1) & (col_ref[0] == 0))
                def _():
                    for c in range(2):
                        res_ref[c, :block, :block] = top_ref[:, c * block : (c + 1) * block]

            for c in range(2):
                pltpu.make_async_copy(res_ref.at[c, at], out_ref.at[c, at], out_sems.at[2 * g + c]).start()
        for g in range(steps):
            at = pl.ds(g * span, span)
            for c in range(2):
                pltpu.make_async_copy(res_ref.at[c, at], out_ref.at[c, at], out_sems.at[2 * g + c]).wait()

    return call(
        kernel,
        24,
        out_shape=jax.ShapeDtypeStruct((2, rows, CBLK * block), F32),
        in_specs=[SMEM] * 3 + [ANY] + [VMEM] * 4 + [ANY] * 2 + [VMEM],
        out_specs=ANY,
        scratch_shapes=[
            pltpu.VMEM((held.shape[0] + CBLK,) + held.shape[1:], F32),
            pltpu.VMEM((2, 2 * CBLK, block, block), F32),
            pltpu.VMEM((rows, 4 * block), BF16),
            pltpu.VMEM((rows, 4 * block), BF16),
            pltpu.VMEM((2, rows, CBLK * block), F32),
            pltpu.VMEM((4 * block, 4 * block), BF16),
            pltpu.VMEM((4 * block, 4 * block), BF16),
            pltpu.SemaphoreType.DMA,
            pltpu.SemaphoreType.DMA((2 * steps,)),
            pltpu.SemaphoreType.DMA((2 * steps,)),
        ],
        name="update",
    )(targets, my_row, my_col, held, *new, *old, high, low, lower_top)


def per_device(assembly, slot_tile, pivots, inverses):
    cols_n = lax.axis_size("pcol")
    rows_n = lax.axis_size("prow")
    my_col = lax.axis_index("pcol")
    my_row = lax.axis_index("prow")
    tiles = assembly[0]
    slots = tiles.shape[0]
    block = tiles.shape[-1]
    row_tiles = slots // CBLK
    base = (slots + cols_n - 1) // cols_n
    excess_max = slots // (base + 1)
    depth = cols_n // LINES
    group = 4 if row_tiles % 4 == 0 else 1
    level = my_col // LINES
    me = my_col.astype(jnp.int32).reshape(1)
    me_row = my_row.astype(jnp.int32).reshape(1)
    odd = me_row % 2
    ids = slot_tile[0]

    picks = jnp.arange(2 * block, dtype=jnp.int32)
    first, second = pivots[0], pivots[1]
    same = (second[:, None] == first[None, :]) & (first[None, :] >= 2 * block)
    chained = jnp.sum(jnp.where(same, picks[None, :block], 0), axis=1)
    second_source = jnp.where(jnp.any(same, axis=1), chained, second)
    replaced = jnp.any(same, axis=0)
    wanted = jnp.concatenate([first, second_source])
    named = jnp.concatenate([first, second])
    moved = (named != picks) & ~jnp.concatenate([replaced, jnp.zeros_like(replaced)])

    def local_row(row, keep):
        ours = (row // block % rows_n == my_row) & keep
        return jnp.where(ours, row // block // rows_n * block + row % block, -1)

    source_rows = local_row(wanted, True)
    targets = local_row(named, moved)

    def after(values, earlier):
        return lax.optimization_barrier((tuple(values), tuple(earlier)))[0]

    def swapped(phase):
        due = []
        for z in range(depth):
            chunks = []
            for t in range(1, depth):
                chunks += [("up", t)] * (z - t >= 0) + [("down", t)] * (z + t < depth)
            due.append(chunks[phase - 2])
        return due

    def shift_pairs(k, phase):
        zm, dx = k // LINES, k % LINES
        pairs = []
        for i in range(cols_n):
            due = depth + 1
            if dx == 0 and zm >= 2:
                due = depth if (i ^ k) // LINES == depth - 1 else depth - 1
            elif (dx == 1 and zm == depth // 2) or (dx == 0 and zm == 1):
                due = depth
            if (i ^ k) >= LINES and due == phase:
                pairs.append((i, i ^ k))
        return pairs

    packed, shifted, meta = pack(tiles, ids, me, cols_n, base, excess_max)
    parts, origins = [packed], [(0, False)]
    chunk = {("up", 0): packed, ("down", 0): packed}
    arrived, arrived_from = [], []
    done = []
    near = meta[None]
    for phase in range(1, depth + 2):
        work = []
        if phase < depth:
            t = phase
            up = [(i, i + LINES) for i in range((t - 1) * LINES, cols_n - LINES)]
            down = [(i, i - LINES) for i in range(LINES, cols_n - (t - 1) * LINES)]
            work.append((chunk["up", t - 1], up, ("up", t), (-t, False)))
            work.append((chunk["down", t - 1], down, ("down", t), (t, False)))
        if phase == 1:
            work.append((packed, [(i, i ^ 1) for i in range(cols_n)], None, (0, True)))
        elif phase <= depth:
            due = swapped(phase)
            x = chunk[due[0]]
            for key in sorted(set(due[1:]) - {due[0]}):
                here = functools.reduce(jnp.logical_or, [level == z for z in range(depth) if due[z] == key])
                x = jnp.where(here, chunk[key], x)
            steps = tuple(-t if d == "up" else t for d, t in due)
            work.append((x, [(i, i ^ 1) for i in range(cols_n)], None, (steps, True)))
        else:
            gathered_all = done
        for k in range(1, cols_n):
            pairs = shift_pairs(k, phase)
            if pairs:
                work.append((shifted[k - 1], pairs, k, pairs))
        before = done
        values = after([w[0] for w in work], done) if done else [w[0] for w in work]
        done = [lax.ppermute(x, "pcol", w[1]) for x, w in zip(values, work)]
        for got, (_, _, key, origin) in zip(done, work):
            if isinstance(key, int):
                arrived.append(got)
                arrived_from.append((key, origin))
            else:
                parts.append(got)
                origins.append(origin)
                if key is not None:
                    chunk[key] = got
        step = 1 << (phase - 1)
        if step < cols_n:
            if phase > 1:
                near = after([near], before)[0]
            got = lax.ppermute(near, "pcol", [(i, i ^ step) for i in range(cols_n)])
            near = jnp.concatenate([near, got])
            done = done + [near]
        if phase == 1:
            done = done + [source_rows, targets]
    shifted_all = done
    most = jnp.max(near[:, cols_n * base + excess_max])

    def gather_rest():
        mine = meta[cols_n * base + 1 : cols_n * base + excess_max]
        slot = jnp.sum(
            jnp.where(mine[:, None] == ids[None, :], jnp.arange(slots, dtype=jnp.int32)[None, :], 0), axis=1
        )
        rest = jnp.stack(
            [lax.dynamic_index_in_dim(tiles, slot[e], 0, False) for e in range(excess_max - 1)]
        )
        others = [
            lax.ppermute(rest, "pcol", [(i, i ^ k) for i in range(cols_n)]) for k in range(1, cols_n)
        ]
        return jnp.concatenate([rest] + others)

    def no_rest():
        return unwritten((cols_n * (excess_max - 1),) + tiles.shape[1:])

    rest = lax.cond(most > 1, gather_rest, no_rest)

    late_rows = after([source_rows], gathered_all)[0]
    held_p, keep_p, send_p, top_p = extract(
        parts, origins, rest, near, ids, late_rows, me, odd, cols_n, base
    )
    keep_p, send_p, top_p = after((keep_p, send_p, top_p), shifted_all)
    new_p, old_p = exchange(keep_p, send_p, top_p, my_row, rows_n)
    high, low, lower_top = panel_factors(held_p, new_p, old_p, inverses, targets, me_row, group)

    held, keep, send, top = extract(
        parts, origins, rest, near, ids, source_rows, me, odd, cols_n, base, tiles, arrived, arrived_from
    )
    new, old = exchange(keep, send, top, my_row, rows_n)
    return update(held, new, old, high, low, lower_top, targets, me_row, me, rows_n, group)


def solution(mesh):
    in_specs = (P("prow", "pcol", None, None, None), P("prow", "pcol"), P(), P())
    out_specs = P(None, "prow", "pcol")
    return jax.shard_map(
        per_device, mesh=mesh, in_specs=in_specs, out_specs=out_specs, check_vma=False
    )
```

time: 322 us -> 250 us (0.78)
  waiting for transfers between devices: 98.2 us -> 143 us
  other arithmetic: 36.2 us -> 4.74 us
  Pallas kernels: 54.3 us -> 30.5 us
  starting transfers between devices: 88.7 us -> 65.6 us
  local copies, waits for them, and re-layouts: 25.9 us -> 3.33 us
  between operations: 14.7 us -> 1.29 us
    ppermute x25 -> x22, waiting for transfers between devices: 85.6 us -> 128 us  [the longest x19 82.7 us: per_device(): done = [lax.ppermute(x, 'pcol', w[1]) for x, w in zip(values, work)]]
    pallas_call x5 -> x4, Pallas kernels: 36.1 us -> 16.1 us  [the longest x2 10.1 us: extract(): call(kernel, 12, out_shape=(pltpu.HBM((tiles_n, 2, block, block), F32), p...]
    ppermute x25 -> x22, starting transfers between devices: 63.7 us -> 50 us  [the longest x19 43.4 us: per_device(): done = [lax.ppermute(x, 'pcol', w[1]) for x, w in zip(values, work)]]
    unnamed x44 -> x60, local copies, waits for them, and re-layouts: 14.3 us -> 3.32 us
    ppermute x8, starting transfers between devices: 22.4 us -> 13.1 us  [cross(): return lax.ppermute(x, 'prow', [(p, p ^ step) for p in range(rows_n)])]
    reduce_sum x8 -> x0, other arithmetic: 8.47 us -> none  [the longest x2 1.75 us: ids_where(): return jnp.sum(jnp.where(hit, all_ids[:, None, :] + 1, 0), axis=2) - 1]
    eq x10 -> x0, other arithmetic: 6.33 us -> none  [the longest x7 4.03 us: per_device(): order[:, None] == (my_col - k) % cols_n]
    select_n x8 -> x3, other arithmetic: 8.69 us -> 3.43 us  [per_device(): x = jnp.where(here, chunk[key], x)]
  transfers between devices with their start and end apart: 35 -> 32, of which waited for: 10 -> 12; matrix products, arithmetic and copies ran while one was open for 15% -> 2% of each run, Pallas kernels for 13% -> 7%
where the time goes in v3:
time: 250 us; the launch traced here: 249 us
  waiting for transfers between devices  143 us (57%)
  starting transfers between devices  65.6 us (26%)
  Pallas kernels  30.5 us (12%)
  other arithmetic  4.74 us (2%)
  local copies, waits for them, and re-layouts  3.33 us (1%)
    ppermute x19, waiting for transfers between devices, per_device(): done = [lax.ppermute(x, 'pcol', w[1]) for x, w in zip(values, work)]  82.7 us
    ppermute x3, waiting for transfers between devices, per_device(): got = lax.ppermute(near, 'pcol', [(i, i ^ step) for i in range(cols_n)])  44.8 us
    ppermute x19, starting transfers between devices, per_device(): done = [lax.ppermute(x, 'pcol', w[1]) for x, w in zip(values, work)]  43.4 us
    ppermute x8, starting transfers between devices, cross(): return lax.ppermute(x, 'prow', [(p, p ^ step) for p in range(rows_n)])  13.1 us
    pallas_call x2, Pallas kernels, extract(): call(kernel, 12, out_shape=(pltpu.HBM((tiles_n, 2, block, block), F32), p...  10.1 us
    ppermute x8, waiting for transfers between devices, cross(): return lax.ppermute(x, 'prow', [(p, p ^ step) for p in range(rows_n)])  8.63 us
    pallas_call x1, Pallas kernels, update(): call(kernel, 24, out_shape=jax.ShapeDtypeStruct((2, rows, CBLK * block),...  7.62 us
    ppermute x2, waiting for transfers between devices, exchange(): got = lax.ppermute(held, 'prow', [(p, p + step) for p in range(step)])  7.1 us
  transfers between devices with their start and end apart: 32, of which 12 were waited for; matrix products, arithmetic and copies ran while one was open for 2% of the time, Pallas kernels for 7%

profile of v3, /device:TPU:29, one launch (start us, length us, event | category | flops | bytes accessed | tf_op | source)
XLA Modules:
  0.0 248.8 jit_solution(1795845277260928389)
XLA Ops:
  0.0 6.0 %pack.1 = (f32[9,2,128,128]{3,2,1,0:T(8,128)}, f32[4,2,128,128]{3,2,1,0:T(8,128)}, f32[4,2,128,128]{3,2,1,0:T(8,128)}, f32[4,2,128,128]{3,2,1,0:T(8,128)}, f32[4...) custom-call(s32[32]{0:T(128)} %bitcast.22, ...), custom_call_target="tpu_custom_call" | custom-call | tf_op jit(solution)/shard_map/pack/pallas_call | solution.py:95
  7.3 4.1 %collective-permute-start.9 = (f32[9,2,128,128]{3,2,1,0:T(8,128)}, f32[9,2,128,128]{3,2,1,0:T(8,128)S(1)}, u32[]{:S(2)}, u32[]{:S(2)}) collective-permute-start(f32[9,2,128,128]{3,2,1,0:T(8,128)} %get-tuple-element.60.rest_refs_0_), channel_id=1, source_target_pairs={{2,0},{3,1},{4,2},{5,3},{6,4},{7,5},{10,8},{11,9},{12,10},{13,11},... | collective-permute-start | bytes 3538952 | tf_op jit(solution)/shard_map/ppermute | solution.py:570
  11.4 1.3 collective-permute-start.10
  13.4 24.3 %collective-permute-done.7 = s32[1,128]{1,0:T(1,128)S(1)} collective-permute-done((s32[1,128]{1,0:T(1,128)S(1)}, s32[1,128]{1,0:T(1,128)S(1)}, u32[]{:S(2)}, u32[]{:S(2)}) %collective-permute-start.7) | collective-permute-done | bytes 544 | tf_op jit(solution)/shard_map/ppermute | solution.py:584
  37.8 1.8 broadcast_select_fusion
  42.7 1.3 collective-permute-start.14
  44.0 3.5 %collective-permute-start.11 = (s32[2,128]{1,0:T(2,128)S(1)}, s32[2,128]{1,0:T(2,128)S(1)}, u32[]{:S(2)}, u32[]{:S(2)}) collective-permute-start(s32[2,128]{1,0:T(2,128)S(1)} %pad_add_fusion.4), channel_id=1, source_target_pairs={{0,2},{1,3},{2,0},{3,1},{4,6},{5,7},{6,4},{7,5},{8,10},{9,11},{10,... | collective-permute-start | bytes 3080 | tf_op jit(solution)/shard_map/ppermute | solution.py:584
  47.5 20.4 %collective-permute-done.11 = s32[2,128]{1,0:T(2,128)S(1)} collective-permute-done((s32[2,128]{1,0:T(2,128)S(1)}, s32[2,128]{1,0:T(2,128)S(1)}, u32[]{:S(2)}, u32[]{:S(2)}) %collective-permute-start.11) | collective-permute-done | bytes 1056 | tf_op jit(solution)/shard_map/ppermute | solution.py:584
  68.0 2.9 %collective-permute-start.15 = (s32[4,128]{1,0:T(4,128)S(1)}, s32[4,128]{1,0:T(4,128)S(1)}, u32[]{:S(2)}, u32[]{:S(2)}) collective-permute-start(s32[4,128]{1,0:T(4,128)S(1)} %pad_add_fusion.1), channel_id=1, source_target_pairs={{0,4},{1,5},{2,6},{3,7},{4,0},{5,1},{6,2},{7,3},{8,12},{9,13},{10,... | collective-permute-start | bytes 6152 | tf_op jit(solution)/shard_map/ppermute | solution.py:584
  73.5 1.6 collective-permute-start.16
  77.1 5.1 %collective-permute-start.19 = (f32[4,2,128,128]{3,2,1,0:T(8,128)}, f32[4,2,128,128]{3,2,1,0:T(8,128)S(1)}, u32[]{:S(2)}, u32[]{:S(2)}) collective-permute-start(f32[4,2,128,128]{3,2,1,0:T(8,128)} %get-tuple-element.77), channel_id=1, source_target_pairs={{0,4},{1,5},{6,2},{7,3},{8,12},{9,13},{14,10},{15,11},{16,20},{17,... | collective-permute-start | bytes 1572872 | tf_op jit(solution)/shard_map/ppermute | solution.py:570
  82.8 15.7 %collective-permute-done.16.rest_refs_7_ = f32[9,2,128,128]{3,2,1,0:T(8,128)S(1)} collective-permute-done((f32[9,2,128,128]{3,2,1,0:T(8,128)S(1)}, f32[9,2,128,128]{3,2,1,0:T(8,128)S(1)}, u32[]{:S(2)}, u32[]{:S(2)}) %collective-permute-start.16) | collective-permute-done | bytes 1179680 | tf_op jit(solution)/shard_map/ppermute | solution.py:570
  100.5 9.1 %collective-permute-start.22 = (f32[4,2,128,128]{3,2,1,0:T(8,128)S(1)}, f32[4,2,128,128]{3,2,1,0:T(8,128)S(1)}, u32[]{:S(2)}, u32[]{:S(2)}) collective-permute-start(f32[4,2,128,128]{3,2,1,0:T(8,128)S(1)} %copy-done.29), channel_id=1, source_target_pairs={{0,2},{1,3},{4,6},{5,7},{6,4},{7,5},{8,10},{9,11},{12,14},{13,15},... | collective-permute-start | bytes 1572872 | tf_op jit(solution)/shard_map/ppermute | solution.py:570
  110.9 5.8 %collective-permute-start.24 = (f32[4,2,128,128]{3,2,1,0:T(8,128)S(1)}, f32[4,2,128,128]{3,2,1,0:T(8,128)S(1)}, u32[]{:S(2)}, u32[]{:S(2)}) collective-permute-start(f32[4,2,128,128]{3,2,1,0:T(8,128)S(1)} %copy-done.27), channel_id=1, source_target_pairs={{0,5},{1,4},{2,7},{3,6},{6,3},{7,2},{8,13},{9,12},{10,15},{11,14},... | collective-permute-start | bytes 1572872 | tf_op jit(solution)/shard_map/ppermute | solution.py:570
  118.1 10.9 %collective-permute-done.22.rest_refs_15_ = f32[4,2,128,128]{3,2,1,0:T(8,128)S(1)} collective-permute-done((f32[4,2,128,128]{3,2,1,0:T(8,128)S(1)}, f32[4,2,128,128]{3,2,1,0:T(8,128)S(1)}, u32[]{:S(2)}, u32[]{:S(2)}) %collective-permute-start.22) | collective-permute-done | bytes 524320 | tf_op jit(solution)/shard_map/ppermute | solution.py:570
  129.0 18.3 %collective-permute-done.23.rest_refs_16_ = f32[4,2,128,128]{3,2,1,0:T(8,128)S(1)} collective-permute-done((f32[4,2,128,128]{3,2,1,0:T(8,128)S(1)}, f32[4,2,128,128]{3,2,1,0:T(8,128)S(1)}, u32[]{:S(2)}, u32[]{:S(2)}) %collective-permute-start.23) | collective-permute-done | bytes 524320 | tf_op jit(solution)/shard_map/ppermute | solution.py:570
  147.3 12.2 %collective-permute-done.24.rest_refs_17_ = f32[4,2,128,128]{3,2,1,0:T(8,128)S(1)} collective-permute-done((f32[4,2,128,128]{3,2,1,0:T(8,128)S(1)}, f32[4,2,128,128]{3,2,1,0:T(8,128)S(1)}, u32[]{:S(2)}, u32[]{:S(2)}) %collective-permute-start.24) | collective-permute-done | bytes 524320 | tf_op jit(solution)/shard_map/ppermute | solution.py:570
  159.5 2.2 collective-permute-start.26
  161.7 1.9 collective-permute-start.27
  165.0 5.0 %panel_rows.1 = (f32[32,2,128,128]{3,2,1,0:T(8,128)}, f32[4,128,128]{2,1,0:T(8,128)S(1)}, f32[4,128,128]{2,1,0:T(8,128)S(1)}, f32[4,128,128]{2,1,0:T(8,128)S(1)}) custom-call(s32[8,128]{1,0:T(8,128)S(1)} %pad_add_fusion.near_ref, s32[32]{0:T(128)S(1)} %bitcast.23, s32[256]{0:T(256)S(1)} %get-tuple-element.90.rows_ref, s32[1]{0:T(128)} %bitcast.10.me_ref.col_ref, ...), custom_call_target="tpu_custom_call" | custom-call | tf_op jit(solution)/shard_map/panel_rows/pallas_call | solution.py:239
  170.0 25.3 %collective-permute-done.26.rest_refs_19_ = f32[4,2,128,128]{3,2,1,0:T(8,128)S(1)} collective-permute-done((f32[4,2,128,128]{3,2,1,0:T(8,128)S(1)}, f32[4,2,128,128]{3,2,1,0:T(8,128)S(1)}, u32[]{:S(2)}, u32[]{:S(2)}) %collective-permute-start.26) | collective-permute-done | bytes 524320 | tf_op jit(solution)/shard_map/ppermute | solution.py:570
  195.3 3.0 %collective-permute-start.34 = (f32[4,128,128]{2,1,0:T(8,128)S(1)}, f32[4,128,128]{2,1,0:T(8,128)S(1)}, u32[]{:S(2)}, u32[]{:S(2)}) collective-permute-start(f32[4,128,128]{2,1,0:T(8,128)S(1)} %get-tuple-element.96), channel_id=1, source_target_pairs={{0,8},{8,0},{16,24},{24,16},{1,9},{9,1},{17,25},{25,17},{2,10},{10... | collective-permute-start | bytes 786440 | tf_op jit(solution)/shard_map/ppermute | solution.py:256
  198.3 5.1 %own_rows.1 = (f32[32,2,128,128]{3,2,1,0:T(8,128)}, f32[4,128,128]{2,1,0:T(8,128)S(1)}, f32[4,128,128]{2,1,0:T(8,128)S(1)}, f32[4,128,128]{2,1,0:T(8,128)S(1)}) custom-call(s32[8,128]{1,0:T(8,128)S(1)} %pad_add_fusion.near_ref, s32[32]{0:T(128)S(1)} %bitcast.24, s32[256]{0:T(256)S(1)} %get-tuple-element.90.rows_ref, s32[1]{0:T(128)} %bitcast.10.me_ref.col_ref, ...), custom_call_target="tpu_custom_call" | custom-call | tf_op jit(solution)/shard_map/own_rows/pallas_call | solution.py:239
  205.9 2.2 collective-permute-start.35
  209.4 2.2 collective-permute-start.30
  211.6 2.8 %collective-permute-done.37 = f32[4,128,128]{2,1,0:T(8,128)S(1)} collective-permute-done((f32[4,128,128]{2,1,0:T(8,128)S(1)}, f32[4,128,128]{2,1,0:T(8,128)S(1)}, u32[]{:S(2)}, u32[]{:S(2)}) %collective-permute-start.37) | collective-permute-done | bytes 262176 | tf_op jit(solution)/shard_map/ppermute | solution.py:261
  215.7 4.3 %collective-permute-done.35 = f32[4,128,128]{2,1,0:T(8,128)S(1)} collective-permute-done((f32[4,128,128]{2,1,0:T(8,128)S(1)}, f32[4,128,128]{2,1,0:T(8,128)S(1)}, u32[]{:S(2)}, u32[]{:S(2)}) %collective-permute-start.35) | collective-permute-done | bytes 262176 | tf_op jit(solution)/shard_map/ppermute | solution.py:256
  221.3 4.3 %collective-permute-done.32 = f32[4,128,128]{2,1,0:T(8,128)S(1)} collective-permute-done((f32[4,128,128]{2,1,0:T(8,128)S(1)}, f32[4,128,128]{2,1,0:T(8,128)S(1)}, u32[]{:S(2)}, u32[]{:S(2)}) %collective-permute-start.32) | collective-permute-done | bytes 262176 | tf_op jit(solution)/shard_map/ppermute | solution.py:261
  226.9 4.3 %collective-permute-done.30 = f32[4,128,128]{2,1,0:T(8,128)S(1)} collective-permute-done((f32[4,128,128]{2,1,0:T(8,128)S(1)}, f32[4,128,128]{2,1,0:T(8,128)S(1)}, u32[]{:S(2)}, u32[]{:S(2)}) %collective-permute-start.30) | collective-permute-done | bytes 262176 | tf_op jit(solution)/shard_map/ppermute | solution.py:256
  232.1 2.2 copy-done
  234.3 6.8 %panel_factors.1 = (bf16[2048,512]{1,0:T(8,128)(2,1)S(1)}, bf16[2048,512]{1,0:T(8,128)(2,1)S(1)}, f32[128,256]{1,0:T(8,128)S(1)}) custom-call(s32[256]{0:T(256)S(1)} %get-tuple-element.113.tgt, s32[1]{0:T(128)} %bitcast.9.row_ref, f32[32,2,128,128]{3,2,1,0:T(8,128)S(1)} %copy-done, f32[4,128,128]{2,1,0:T(8,128)S(1)} %add.73.new_a, ...), custom_call_target="tpu_custom_call" | custom-call | tf_op jit(solution)/shard_map/panel_factors/pallas_call | solution.py:366
  241.2 7.6 %update.1 = f32[2,2048,256]{2,1,0:T(8,128)} custom-call(s32[256]{0:T(256)S(1)} %get-tuple-element.113.tgt, s32[1]{0:T(128)} %bitcast.9.row_ref, s32[1]{0:T(128)} %bitcast.10.me_ref.col_ref, f32[32,2,128,128]{3,2,1,0:T(8,128)S(1)} %copy-done.1, f32[4,128,128]{2,1,0:T(8,128)S(1)} %add.71.new_a, f32[4,128,128]{2,1,0:T(8,128)S(1)} %collective-permute-done.31.new_b, ...), custom_call_target="tpu_custom_call" | custom-call | tf_op jit(solution)/shard_map/update/pallas_call | solution.py:455
  (120 shorter events, 24.1 us)
Async XLA Ops:
  6.0 31.7 %collective-permute-start.8 = (f32[9,2,128,128]{3,2,1,0:T(8,128)}, f32[9,2,128,128]{3,2,1,0:T(8,128)}, u32[]{:S(2)}, u32[]{:S(2)}) collective-permute-start(f32[9,2,128,128]{3,2,1,0:T(8,128)} %get-tuple-element.60.rest_refs_0_), channel_id=1, source_target_pairs={{0,2},{1,3},{2,4},{3,5},{4,6},{5,7},{8,10},{9,11},{10,12},{11,13},... | collective-permute-start | bytes 3538952 | tf_op jit(solution)/shard_map/ppermute | solution.py:570
  7.3 30.4 %collective-permute-start.9 = (f32[9,2,128,128]{3,2,1,0:T(8,128)}, f32[9,2,128,128]{3,2,1,0:T(8,128)S(1)}, u32[]{:S(2)}, u32[]{:S(2)}) collective-permute-start(f32[9,2,128,128]{3,2,1,0:T(8,128)} %get-tuple-element.60.rest_refs_0_), channel_id=1, source_target_pairs={{2,0},{3,1},{4,2},{5,3},{6,4},{7,5},{10,8},{11,9},{12,10},{13,11},... | collective-permute-start | bytes 3538952 | tf_op jit(solution)/shard_map/ppermute | solution.py:570
  11.4 28.2 %collective-permute-start.10 = (f32[9,2,128,128]{3,2,1,0:T(8,128)}, f32[9,2,128,128]{3,2,1,0:T(8,128)S(1)}, u32[]{:S(2)}, u32[]{:S(2)}) collective-permute-start(f32[9,2,128,128]{3,2,1,0:T(8,128)} %get-tuple-element.60.rest_refs_0_), channel_id=1, source_target_pairs={{0,1},{1,0},{2,3},{3,2},{4,5},{5,4},{6,7},{7,6},{8,9},{9,8},{10,11... | collective-permute-start | bytes 3538952 | tf_op jit(solution)/shard_map/ppermute | solution.py:570
  12.7 25.0 %collective-permute-start.7 = (s32[1,128]{1,0:T(1,128)S(1)}, s32[1,128]{1,0:T(1,128)S(1)}, u32[]{:S(2)}, u32[]{:S(2)}) collective-permute-start(s32[1,128]{1,0:T(1,128)S(1)} %bitcast.26), channel_id=1, source_target_pairs={{0,1},{1,0},{2,3},{3,2},{4,5},{5,4},{6,7},{7,6},{8,9},{9,8},{10,11... | collective-permute-start | bytes 1544 | tf_op jit(solution)/shard_map/ppermute | solution.py:584
  40.7 27.3 %collective-permute-start.12 = (f32[9,2,128,128]{3,2,1,0:T(8,128)}, f32[9,2,128,128]{3,2,1,0:T(8,128)S(1)}, u32[]{:S(2)}, u32[]{:S(2)}) collective-permute-start(f32[9,2,128,128]{3,2,1,0:T(8,128)} %collective-permute-done.8.rest_refs_1_), channel_id=1, source_target_pairs={{2,4},{3,5},{4,6},{5,7},{10,12},{11,13},{12,14},{13,15},{18,20},{1... | collective-permute-start | bytes 3538952 | tf_op jit(solution)/shard_map/ppermute | solution.py:570
  41.9 26.0 %collective-permute-start.13 = (f32[9,2,128,128]{3,2,1,0:T(8,128)S(1)}, f32[9,2,128,128]{3,2,1,0:T(8,128)S(1)}, u32[]{:S(2)}, u32[]{:S(2)}) collective-permute-start(f32[9,2,128,128]{3,2,1,0:T(8,128)S(1)} %collective-permute-done.9.rest_refs_2_), channel_id=1, source_target_pairs={{2,0},{3,1},{4,2},{5,3},{10,8},{11,9},{12,10},{13,11},{18,16},{19,... | collective-permute-start | bytes 3538952 | tf_op jit(solution)/shard_map/ppermute | solution.py:570
  42.7 25.3 %collective-permute-start.14 = (f32[9,2,128,128]{3,2,1,0:T(8,128)S(1)}, f32[9,2,128,128]{3,2,1,0:T(8,128)}, u32[]{:S(2)}, u32[]{:S(2)}) collective-permute-start(f32[9,2,128,128]{3,2,1,0:T(8,128)S(1)} %broadcast_select_fusion), channel_id=1, source_target_pairs={{0,1},{1,0},{2,3},{3,2},{4,5},{5,4},{6,7},{7,6},{8,9},{9,8},{10,11... | collective-permute-start | bytes 3538952 | tf_op jit(solution)/shard_map/ppermute | solution.py:570
  44.0 23.9 %collective-permute-start.11 = (s32[2,128]{1,0:T(2,128)S(1)}, s32[2,128]{1,0:T(2,128)S(1)}, u32[]{:S(2)}, u32[]{:S(2)}) collective-permute-start(s32[2,128]{1,0:T(2,128)S(1)} %pad_add_fusion.4), channel_id=1, source_target_pairs={{0,2},{1,3},{2,0},{3,1},{4,6},{5,7},{6,4},{7,5},{8,10},{9,11},{10,... | collective-permute-start | bytes 3080 | tf_op jit(solution)/shard_map/ppermute | solution.py:584
  68.0 4.1 %collective-permute-start.15 = (s32[4,128]{1,0:T(4,128)S(1)}, s32[4,128]{1,0:T(4,128)S(1)}, u32[]{:S(2)}, u32[]{:S(2)}) collective-permute-start(s32[4,128]{1,0:T(4,128)S(1)} %pad_add_fusion.1), channel_id=1, source_target_pairs={{0,4},{1,5},{2,6},{3,7},{4,0},{5,1},{6,2},{7,3},{8,12},{9,13},{10,... | collective-permute-start | bytes 6152 | tf_op jit(solution)/shard_map/ppermute | solution.py:584
  73.5 25.0 %collective-permute-start.16 = (f32[9,2,128,128]{3,2,1,0:T(8,128)S(1)}, f32[9,2,128,128]{3,2,1,0:T(8,128)S(1)}, u32[]{:S(2)}, u32[]{:S(2)}) collective-permute-start(f32[9,2,128,128]{3,2,1,0:T(8,128)S(1)} %collective-permute-done.12.rest_refs_4_), channel_id=1, source_target_pairs={{4,6},{5,7},{12,14},{13,15},{20,22},{21,23},{28,30},{29,31}} | collective-permute-start | bytes 3538952 | tf_op jit(solution)/shard_map/ppermute | solution.py:570
  75.1 23.5 %collective-permute-start.17 = (f32[9,2,128,128]{3,2,1,0:T(8,128)S(1)}, f32[9,2,128,128]{3,2,1,0:T(8,128)S(1)}, u32[]{:S(2)}, u32[]{:S(2)}) collective-permute-start(f32[9,2,128,128]{3,2,1,0:T(8,128)S(1)} %collective-permute-done.13.rest_refs_5_), channel_id=1, source_target_pairs={{2,0},{3,1},{10,8},{11,9},{18,16},{19,17},{26,24},{27,25}} | collective-permute-start | bytes 3538952 | tf_op jit(solution)/shard_map/ppermute | solution.py:570
  75.8 23.5 %collective-permute-start.18 = (f32[9,2,128,128]{3,2,1,0:T(8,128)}, f32[9,2,128,128]{3,2,1,0:T(8,128)S(1)}, u32[]{:S(2)}, u32[]{:S(2)}) collective-permute-start(f32[9,2,128,128]{3,2,1,0:T(8,128)} %select_select_fusion.1), channel_id=1, source_target_pairs={{0,1},{1,0},{2,3},{3,2},{4,5},{5,4},{6,7},{7,6},{8,9},{9,8},{10,11... | collective-permute-start | bytes 3538952 | tf_op jit(solution)/shard_map/ppermute | solution.py:570
  77.1 21.9 %collective-permute-start.19 = (f32[4,2,128,128]{3,2,1,0:T(8,128)}, f32[4,2,128,128]{3,2,1,0:T(8,128)S(1)}, u32[]{:S(2)}, u32[]{:S(2)}) collective-permute-start(f32[4,2,128,128]{3,2,1,0:T(8,128)} %get-tuple-element.77), channel_id=1, source_target_pairs={{0,4},{1,5},{6,2},{7,3},{8,12},{9,13},{14,10},{15,11},{16,20},{17,... | collective-permute-start | bytes 1572872 | tf_op jit(solution)/shard_map/ppermute | solution.py:570
  82.1 16.9 %collective-permute-start.20 = (f32[4,2,128,128]{3,2,1,0:T(8,128)}, f32[4,2,128,128]{3,2,1,0:T(8,128)S(1)}, u32[]{:S(2)}, u32[]{:S(2)}) collective-permute-start(f32[4,2,128,128]{3,2,1,0:T(8,128)} %get-tuple-element.79), channel_id=1, source_target_pairs={{2,4},{3,5},{4,2},{5,3},{10,12},{11,13},{12,10},{13,11},{18,20},{1... | collective-permute-start | bytes 1572872 | tf_op jit(solution)/shard_map/ppermute | solution.py:570
  99.3 60.1 %collective-permute-start.21 = (f32[9,2,128,128]{3,2,1,0:T(8,128)S(1)}, f32[9,2,128,128]{3,2,1,0:T(8,128)S(1)}, u32[]{:S(2)}, u32[]{:S(2)}) collective-permute-start(f32[9,2,128,128]{3,2,1,0:T(8,128)S(1)} %select_select_fusion), channel_id=1, source_target_pairs={{0,1},{1,0},{2,3},{3,2},{4,5},{5,4},{6,7},{7,6},{8,9},{9,8},{10,11... | collective-permute-start | bytes 3538952 | tf_op jit(solution)/shard_map/ppermute | solution.py:570
  100.5 28.4 %collective-permute-start.22 = (f32[4,2,128,128]{3,2,1,0:T(8,128)S(1)}, f32[4,2,128,128]{3,2,1,0:T(8,128)S(1)}, u32[]{:S(2)}, u32[]{:S(2)}) collective-permute-start(f32[4,2,128,128]{3,2,1,0:T(8,128)S(1)} %copy-done.29), channel_id=1, source_target_pairs={{0,2},{1,3},{4,6},{5,7},{6,4},{7,5},{8,10},{9,11},{12,14},{13,15},... | collective-permute-start | bytes 1572872 | tf_op jit(solution)/shard_map/ppermute | solution.py:570
  109.6 37.7 %collective-permute-start.23 = (f32[4,2,128,128]{3,2,1,0:T(8,128)S(1)}, f32[4,2,128,128]{3,2,1,0:T(8,128)S(1)}, u32[]{:S(2)}, u32[]{:S(2)}) collective-permute-start(f32[4,2,128,128]{3,2,1,0:T(8,128)S(1)} %copy-done.28), channel_id=1, source_target_pairs={{2,6},{3,7},{10,14},{11,15},{18,22},{19,23},{26,30},{27,31}} | collective-permute-start | bytes 1572872 | tf_op jit(solution)/shard_map/ppermute | solution.py:570
  110.9 48.5 %collective-permute-start.24 = (f32[4,2,128,128]{3,2,1,0:T(8,128)S(1)}, f32[4,2,128,128]{3,2,1,0:T(8,128)S(1)}, u32[]{:S(2)}, u32[]{:S(2)}) collective-permute-start(f32[4,2,128,128]{3,2,1,0:T(8,128)S(1)} %copy-done.27), channel_id=1, source_target_pairs={{0,5},{1,4},{2,7},{3,6},{6,3},{7,2},{8,13},{9,12},{10,15},{11,14},... | collective-permute-start | bytes 1572872 | tf_op jit(solution)/shard_map/ppermute | solution.py:570
  116.8 42.7 %collective-permute-start.25 = (f32[4,2,128,128]{3,2,1,0:T(8,128)S(1)}, f32[4,2,128,128]{3,2,1,0:T(8,128)S(1)}, u32[]{:S(2)}, u32[]{:S(2)}) collective-permute-start(f32[4,2,128,128]{3,2,1,0:T(8,128)S(1)} %copy-done.26), channel_id=1, source_target_pairs={{0,6},{1,7},{8,14},{9,15},{16,22},{17,23},{24,30},{25,31}} | collective-permute-start | bytes 1572872 | tf_op jit(solution)/shard_map/ppermute | solution.py:570
  159.5 35.8 %collective-permute-start.26 = (f32[4,2,128,128]{3,2,1,0:T(8,128)S(1)}, f32[4,2,128,128]{3,2,1,0:T(8,128)S(1)}, u32[]{:S(2)}, u32[]{:S(2)}) collective-permute-start(f32[4,2,128,128]{3,2,1,0:T(8,128)S(1)} %copy-done.25), channel_id=1, source_target_pairs={{2,3},{3,2},{4,5},{5,4},{6,7},{7,6},{10,11},{11,10},{12,13},{13,12... | collective-permute-start | bytes 1572872 | tf_op jit(solution)/shard_map/ppermute | solution.py:570
  161.7 33.6 %collective-permute-start.27 = (f32[4,2,128,128]{3,2,1,0:T(8,128)S(1)}, f32[4,2,128,128]{3,2,1,0:T(8,128)S(1)}, u32[]{:S(2)}, u32[]{:S(2)}) collective-permute-start(f32[4,2,128,128]{3,2,1,0:T(8,128)S(1)} %copy-done.24), channel_id=1, source_target_pairs={{0,3},{1,2},{4,7},{5,6},{6,5},{7,4},{8,11},{9,10},{12,15},{13,14},... | collective-permute-start | bytes 1572872 | tf_op jit(solution)/shard_map/ppermute | solution.py:570
  163.6 31.7 %collective-permute-start.28 = (f32[4,2,128,128]{3,2,1,0:T(8,128)S(1)}, f32[4,2,128,128]{3,2,1,0:T(8,128)S(1)}, u32[]{:S(2)}, u32[]{:S(2)}) collective-permute-start(f32[4,2,128,128]{3,2,1,0:T(8,128)S(1)} %copy-done.23), channel_id=1, source_target_pairs={{0,7},{1,6},{2,5},{3,4},{4,3},{5,2},{8,15},{9,14},{10,13},{11,12},... | collective-permute-start | bytes 1572872 | tf_op jit(solution)/shard_map/ppermute | solution.py:570
  195.3 10.5 %collective-permute-start.34 = (f32[4,128,128]{2,1,0:T(8,128)S(1)}, f32[4,128,128]{2,1,0:T(8,128)S(1)}, u32[]{:S(2)}, u32[]{:S(2)}) collective-permute-start(f32[4,128,128]{2,1,0:T(8,128)S(1)} %get-tuple-element.96), channel_id=1, source_target_pairs={{0,8},{8,0},{16,24},{24,16},{1,9},{9,1},{17,25},{25,17},{2,10},{10... | collective-permute-start | bytes 786440 | tf_op jit(solution)/shard_map/ppermute | solution.py:256
  203.5 5.9 %collective-permute-start.29 = (f32[4,128,128]{2,1,0:T(8,128)S(1)}, f32[4,128,128]{2,1,0:T(8,128)S(1)}, u32[]{:S(2)}, u32[]{:S(2)}) collective-permute-start(f32[4,128,128]{2,1,0:T(8,128)S(1)} %get-tuple-element.88), channel_id=1, source_target_pairs={{0,8},{8,0},{16,24},{24,16},{1,9},{9,1},{17,25},{25,17},{2,10},{10... | collective-permute-start | bytes 786440 | tf_op jit(solution)/shard_map/ppermute | solution.py:256
  204.6 9.8 %collective-permute-start.37 = (f32[4,128,128]{2,1,0:T(8,128)S(1)}, f32[4,128,128]{2,1,0:T(8,128)S(1)}, u32[]{:S(2)}, u32[]{:S(2)}) collective-permute-start(f32[4,128,128]{2,1,0:T(8,128)S(1)} %get-tuple-element.97), channel_id=1, source_target_pairs={{0,16},{8,24},{1,17},{9,25},{2,18},{10,26},{3,19},{11,27},{4,20},{... | collective-permute-start | bytes 786440 | tf_op jit(solution)/shard_map/ppermute | solution.py:261
  205.9 14.1 %collective-permute-start.35 = (f32[4,128,128]{2,1,0:T(8,128)S(1)}, f32[4,128,128]{2,1,0:T(8,128)S(1)}, u32[]{:S(2)}, u32[]{:S(2)}) collective-permute-start(f32[4,128,128]{2,1,0:T(8,128)S(1)} %add.72), channel_id=1, source_target_pairs={{0,16},{8,24},{16,0},{24,8},{1,17},{9,25},{17,1},{25,9},{2,18},{10... | collective-permute-start | bytes 786440 | tf_op jit(solution)/shard_map/ppermute | solution.py:256
  208.1 17.5 %collective-permute-start.32 = (f32[4,128,128]{2,1,0:T(8,128)S(1)}, f32[4,128,128]{2,1,0:T(8,128)S(1)}, u32[]{:S(2)}, u32[]{:S(2)}) collective-permute-start(f32[4,128,128]{2,1,0:T(8,128)S(1)} %get-tuple-element.89), channel_id=1, source_target_pairs={{0,16},{8,24},{1,17},{9,25},{2,18},{10,26},{3,19},{11,27},{4,20},{... | collective-permute-start | bytes 786440 | tf_op jit(solution)/shard_map/ppermute | solution.py:261
  209.4 21.8 %collective-permute-start.30 = (f32[4,128,128]{2,1,0:T(8,128)S(1)}, f32[4,128,128]{2,1,0:T(8,128)S(1)}, u32[]{:S(2)}, u32[]{:S(2)}) collective-permute-start(f32[4,128,128]{2,1,0:T(8,128)S(1)} %add.70), channel_id=1, source_target_pairs={{0,16},{8,24},{16,0},{24,8},{1,17},{9,25},{17,1},{25,9},{2,18},{10... | collective-permute-start | bytes 786440 | tf_op jit(solution)/shard_map/ppermute | solution.py:256
  214.4 17.7 %collective-permute-start.38 = (f32[4,128,128]{2,1,0:T(8,128)S(1)}, f32[4,128,128]{2,1,0:T(8,128)S(1)}, u32[]{:S(2)}, u32[]{:S(2)}) collective-permute-start(f32[4,128,128]{2,1,0:T(8,128)S(1)} %broadcast_select_fusion.1.old_a), channel_id=1, source_target_pairs={{0,8},{8,0},{16,24},{24,16},{1,9},{9,1},{17,25},{25,17},{2,10},{10... | collective-permute-start | bytes 786440 | tf_op jit(solution)/shard_map/ppermute | solution.py:256
  220.0 12.1 %collective-permute-start.36 = (f32[4,128,128]{2,1,0:T(8,128)S(1)}, f32[4,128,128]{2,1,0:T(8,128)S(1)}, u32[]{:S(2)}, u32[]{:S(2)}) collective-permute-start(f32[4,128,128]{2,1,0:T(8,128)S(1)} %add.73.new_a), channel_id=1, source_target_pairs={{0,8},{8,0},{16,24},{24,16},{1,9},{9,1},{17,25},{25,17},{2,10},{10... | collective-permute-start | bytes 786440 | tf_op jit(solution)/shard_map/ppermute | solution.py:256
  225.6 15.5 %collective-permute-start.33 = (f32[4,128,128]{2,1,0:T(8,128)S(1)}, f32[4,128,128]{2,1,0:T(8,128)S(1)}, u32[]{:S(2)}, u32[]{:S(2)}) collective-permute-start(f32[4,128,128]{2,1,0:T(8,128)S(1)} %broadcast_select_fusion.2.old_a), channel_id=1, source_target_pairs={{0,8},{8,0},{16,24},{24,16},{1,9},{9,1},{17,25},{25,17},{2,10},{10... | collective-permute-start | bytes 786440 | tf_op jit(solution)/shard_map/ppermute | solution.py:256
  231.3 9.9 %collective-permute-start.31 = (f32[4,128,128]{2,1,0:T(8,128)S(1)}, f32[4,128,128]{2,1,0:T(8,128)S(1)}, u32[]{:S(2)}, u32[]{:S(2)}) collective-permute-start(f32[4,128,128]{2,1,0:T(8,128)S(1)} %add.71.new_a), channel_id=1, source_target_pairs={{0,8},{8,0},{16,24},{24,16},{1,9},{9,1},{17,25},{25,17},{2,10},{10... | collective-permute-start | bytes 786440 | tf_op jit(solution)/shard_map/ppermute | solution.py:256
  (30 other events, 1268.5 us)

commit v4 on v3

--- a/solution.py
+++ b/solution.py
@@ -251,22 +251,49 @@
     )(near, ids, source_rows, me, odd, *operands)
 
 
-def exchange(keep, send, top, my_row, rows_n):
+def exchange(keep, send, top, far, my_row, rows_n, earlier=(), meanwhile=None):
     def cross(x, step):
         return lax.ppermute(x, "prow", [(p, p ^ step) for p in range(rows_n)])
 
+    total = keep + cross(send, 1)
+    if rows_n == 4:
+        there = far[None, :, None]
+        second = my_row >= 2
+        message = jnp.where(there & ~second, top, total)
+        message = lax.optimization_barrier((message, tuple(earlier)))[0]
+        got = cross(message, 2)
+        if meanwhile is not None:
+            got = lax.optimization_barrier((got, meanwhile))[0]
+        total = total + jnp.where(there & second, 0.0, got)
+        held = jnp.where(second, got, top)
+        return (total, cross(total, 1)), (held, cross(held, 1)), got
     held = top
     step = 2
     while step < rows_n:
         got = lax.ppermute(held, "prow", [(p, p + step) for p in range(step)])
         held = jnp.where((my_row >= step) & (my_row < 2 * step), got, held)
-        step *= 2
-    total = keep + cross(send, 1)
-    step = 2
-    while step < rows_n:
         total = total + cross(total, step)
         step *= 2
-    return (total, cross(total, 1)), (held, cross(held, 1))
+    return (total, cross(total, 1)), (held, cross(held, 1)), total
+
+
+def fix_chained(chain_ref, new_ref, odd, old_refs, block):
+    @pl.when(chain_ref[block] > 0)
+    def _():
+        def one(i, carry):
+            j = chain_ref[i]
+
+            @pl.when((j >= 0) & (odd == 0))
+            def _():
+                new_ref[1, :, pl.ds(i, 1), :] = old_refs[0][:, pl.ds(j, 1), :]
+
+            @pl.when((j >= 0) & (odd == 1))
+            def _():
+                new_ref[1, :, pl.ds(i, 1), :] = old_refs[1][:, pl.ds(j, 1), :]
+
+            return carry
+
+        lax.fori_loop(0, block, one, 0)
 
 
 def replace_rows(targets_ref, odd, old_refs, held, block):
@@ -309,18 +336,19 @@
         low_ref[rows, cols] = low
 
 
-def panel_factors(held, new, old, inverses, targets, my_row, group):
+def panel_factors(held, new, old, inverses, targets, chain, my_row, group):
     block = held.shape[-1]
     row_tiles = held.shape[0] // CBLK
     rows = row_tiles * block
 
-    def kernel(tgt, row_ref, held_in, new_a, new_b, old_a, old_b, inv_ref, high_ref, low_ref, top_ref, *rest):
+    def kernel(tgt, chain_ref, row_ref, held_in, new_a, new_b, old_a, old_b, inv_ref, high_ref, low_ref, top_ref, *rest):
         held_ref, new_ref, i0h, i0l, i1h, i1l, uh, ul, sem = rest
         odd = lax.rem(row_ref[0], 2)
         copy = pltpu.make_async_copy(held_in, held_ref.at[: CBLK * row_tiles], sem)
         copy.start()
         new_ref[odd] = new_a[...]
         new_ref[1 - odd] = new_b[...]
+        fix_chained(chain_ref, new_ref, odd, (old_a, old_b), block)
         store_complex(i0h, i0l, 0, 0, inv_ref[0, 0], inv_ref[0, 1])
         store_complex(i1h, i1l, 0, 0, inv_ref[1, 0], inv_ref[1, 1])
         store_complex(uh, ul, 0, 0, new_ref[0, 2], new_ref[0, 3])
@@ -371,23 +399,23 @@
             jax.ShapeDtypeStruct((rows, 4 * block), BF16),
             jax.ShapeDtypeStruct((block, 2 * block), F32),
         ),
-        in_specs=[SMEM, SMEM, ANY] + [VMEM] * 5,
+        in_specs=[SMEM, SMEM, SMEM, HBM] + [VMEM] * 5,
         out_specs=(VMEM, VMEM, VMEM),
         scratch_shapes=[pltpu.VMEM((held.shape[0] + CBLK,) + held.shape[1:], F32), pltpu.VMEM((2, 2 * CBLK, block, block), F32)]
         + [wide] * 6
         + [pltpu.SemaphoreType.DMA],
         name="panel_factors",
-    )(targets, my_row, held, *new, *old, inverses)
-
-
-def update(held, new, old, high, low, lower_top, targets, my_row, my_col, rows_n, group):
+    )(targets, chain, my_row, pltpu.with_memory_space_constraint(held, pltpu.HBM), *new, *old, inverses)
+
+
+def update(held, new, old, high, low, lower_top, targets, chain, my_row, my_col, rows_n, group):
     block = held.shape[-1]
     row_tiles = held.shape[0] // CBLK
     rows = row_tiles * block
     steps = row_tiles // group
     span = group * block
 
-    def kernel(tgt, row_ref, col_ref, held_in, new_a, new_b, old_a, old_b, high_in, low_in, top_ref, out_ref, *rest):
+    def kernel(tgt, chain_ref, row_ref, col_ref, held_in, new_a, new_b, old_a, old_b, high_in, low_in, top_ref, out_ref, *rest):
         held_ref, new_ref, high_ref, low_ref, res_ref, wh, wl, sem, in_sems, out_sems = rest
         odd = lax.rem(row_ref[0], 2)
         copy = pltpu.make_async_copy(held_in, held_ref.at[: CBLK * row_tiles], sem)
@@ -398,6 +426,7 @@
                 pltpu.make_async_copy(src.at[at], dst.at[at], in_sems.at[2 * g + n]).start()
         new_ref[odd] = new_a[...]
         new_ref[1 - odd] = new_b[...]
+        fix_chained(chain_ref, new_ref, odd, (old_a, old_b), block)
         for m in range(CBLK):
             store_complex(wh, wl, 0, 2 * m * block, new_ref[0, 2 * m], new_ref[0, 2 * m + 1])
         first = dot3(*split(top_ref[...]), wh[: 2 * block, :], wl[: 2 * block, :])
@@ -456,7 +485,7 @@
         kernel,
         24,
         out_shape=jax.ShapeDtypeStruct((2, rows, CBLK * block), F32),
-        in_specs=[SMEM] * 3 + [ANY] + [VMEM] * 4 + [ANY] * 2 + [VMEM],
+        in_specs=[SMEM] * 4 + [HBM] + [VMEM] * 4 + [ANY] * 2 + [VMEM],
         out_specs=ANY,
         scratch_shapes=[
             pltpu.VMEM((held.shape[0] + CBLK,) + held.shape[1:], F32),
@@ -471,7 +500,9 @@
             pltpu.SemaphoreType.DMA((2 * steps,)),
         ],
         name="update",
-    )(targets, my_row, my_col, held, *new, *old, high, low, lower_top)
+    )(
+        targets, chain, my_row, my_col, pltpu.with_memory_space_constraint(held, pltpu.HBM), *new, *old, high, low, lower_top
+    )
 
 
 def per_device(assembly, slot_tile, pivots, inverses):
@@ -509,6 +540,10 @@
 
     source_rows = local_row(wanted, True)
     targets = local_row(named, moved)
+    away = named // block % rows_n >= 2
+    far = jnp.where(my_row % 2 == 0, away[:block], away[block:])
+    fix = jnp.any(same, axis=1) & away[block:] & (my_row >= 2) & (rows_n == 4)
+    chain = jnp.concatenate([jnp.where(fix, chained, -1), jnp.sum(fix.astype(jnp.int32))[None]])
 
     def after(values, earlier):
         return lax.optimization_barrier((tuple(values), tuple(earlier)))[0]
@@ -526,11 +561,12 @@
         zm, dx = k // LINES, k % LINES
         pairs = []
         for i in range(cols_n):
-            due = depth + 1
-            if dx == 0 and zm >= 2:
-                due = depth if (i ^ k) // LINES == depth - 1 else depth - 1
-            elif (dx == 1 and zm == depth // 2) or (dx == 0 and zm == 1):
+            if dx == 0 and zm >= 2 and (i ^ k) // LINES < depth - 1:
+                due = depth - 1
+            elif zm == depth - 1 or (dx == 0 and zm == 1):
                 due = depth
+            else:
+                due = depth + 1
             if (i ^ k) >= LINES and due == phase:
                 pairs.append((i, i ^ k))
         return pairs
@@ -539,10 +575,10 @@
     parts, origins = [packed], [(0, False)]
     chunk = {("up", 0): packed, ("down", 0): packed}
     arrived, arrived_from = [], []
-    done = []
+    done, work = [], []
     near = meta[None]
     for phase in range(1, depth + 2):
-        work = []
+        last, work = work, []
         if phase < depth:
             t = phase
             up = [(i, i + LINES) for i in range((t - 1) * LINES, cols_n - LINES)]
@@ -553,14 +589,26 @@
             work.append((packed, [(i, i ^ 1) for i in range(cols_n)], None, (0, True)))
         elif phase <= depth:
             due = swapped(phase)
-            x = chunk[due[0]]
-            for key in sorted(set(due[1:]) - {due[0]}):
-                here = functools.reduce(jnp.logical_or, [level == z for z in range(depth) if due[z] == key])
-                x = jnp.where(here, chunk[key], x)
-            steps = tuple(-t if d == "up" else t for d, t in due)
-            work.append((x, [(i, i ^ 1) for i in range(cols_n)], None, (steps, True)))
+            keys = sorted(set(due))
+            if len(keys) <= 2:
+                for key in keys:
+                    levels = [z for z in range(depth) if due[z] == key]
+                    pairs = [(i, i ^ 1) for z in levels for i in range(z * LINES, (z + 1) * LINES)]
+                    steps = tuple(
+                        (-key[1] if key[0] == "up" else key[1]) if z in levels else depth for z in range(depth)
+                    )
+                    work.append((chunk[key], pairs, None, (steps, True)))
+            else:
+                x = chunk[due[0]]
+                for key in keys:
+                    if key != due[0]:
+                        levels = [level == z for z in range(depth) if due[z] == key]
+                        x = jnp.where(functools.reduce(jnp.logical_or, levels), chunk[key], x)
+                steps = tuple(-t if d == "up" else t for d, t in due)
+                work.append((x, [(i, i ^ 1) for i in range(cols_n)], None, (steps, True)))
         else:
-            gathered_all = done
+            gathered_all = [got for got, w in zip(done, last) if not isinstance(w[2], int)]
+            shifted_first = [got for got, w in zip(done, last) if isinstance(w[2], int)]
         for k in range(1, cols_n):
             pairs = shift_pairs(k, phase)
             if pairs:
@@ -583,10 +631,9 @@
                 near = after([near], before)[0]
             got = lax.ppermute(near, "pcol", [(i, i ^ step) for i in range(cols_n)])
             near = jnp.concatenate([near, got])
-            done = done + [near]
+            done = done + [got]
         if phase == 1:
-            done = done + [source_rows, targets]
-    shifted_all = done
+            done = done + [source_rows, targets, far, chain]
     most = jnp.max(near[:, cols_n * base + excess_max])
 
     def gather_rest():
@@ -611,15 +658,15 @@
     held_p, keep_p, send_p, top_p = extract(
         parts, origins, rest, near, ids, late_rows, me, odd, cols_n, base
     )
-    keep_p, send_p, top_p = after((keep_p, send_p, top_p), shifted_all)
-    new_p, old_p = exchange(keep_p, send_p, top_p, my_row, rows_n)
-    high, low, lower_top = panel_factors(held_p, new_p, old_p, inverses, targets, me_row, group)
-
+    new_p, old_p, crossed = exchange(keep_p, send_p, top_p, far, my_row, rows_n, shifted_first)
+    high, low, lower_top = panel_factors(held_p, new_p, old_p, inverses, targets, chain, me_row, group)
+
+    late_rows = after([source_rows], [crossed])[0]
     held, keep, send, top = extract(
-        parts, origins, rest, near, ids, source_rows, me, odd, cols_n, base, tiles, arrived, arrived_from
+        parts, origins, rest, near, ids, late_rows, me, odd, cols_n, base, tiles, arrived, arrived_from
     )
-    new, old = exchange(keep, send, top, my_row, rows_n)
-    return update(held, new, old, high, low, lower_top, targets, me_row, me, rows_n, group)
+    new, old, _ = exchange(keep, send, top, far, my_row, rows_n, meanwhile=high)
+    return update(held, new, old, high, low, lower_top, targets, chain, me_row, me, rows_n, group)
 
 
 def solution(mesh):

time: 250 us -> 227 us (0.908)
  waiting for transfers between devices: 143 us -> 118 us
  Pallas kernels: 30.5 us -> 35.1 us
    ppermute x19 -> x20, waiting for transfers between devices: 82.7 us -> 70.1 us  [per_device(): done = [lax.ppermute(x, 'pcol', w[1]) for x, w in zip(values, work)]]
    ppermute x2 -> x0, waiting for transfers between devices: 7.1 us -> none  [exchange(): got = lax.ppermute(held, 'prow', [(p, p + step) for p in range(step)])]
    ppermute x3, waiting for transfers between devices: 44.8 us -> 39.1 us  [per_device(): got = lax.ppermute(near, 'pcol', [(i, i ^ step) for i in range(cols_n)])]
    ppermute x19 -> x20, starting transfers between devices: 43.4 us -> 48.3 us  [per_device(): done = [lax.ppermute(x, 'pcol', w[1]) for x, w in zip(values, work)]]
    ppermute x8, starting transfers between devices: 13.1 us -> 8.98 us  [cross(): return lax.ppermute(x, 'prow', [(p, p ^ step) for p in range(rows_n)])]
    ppermute x2 -> x0, starting transfers between devices: 2.56 us -> none  [exchange(): got = lax.ppermute(held, 'prow', [(p, p + step) for p in range(step)])]
  transfers between devices with their start and end apart: 32 -> 31, of which waited for: 12 -> 16; matrix products, arithmetic and copies ran while one was open for 2% -> 2% of each run, Pallas kernels for 7% -> 6%
where the time goes in v4:
time: 227 us; the launch traced here: 226 us
  waiting for transfers between devices  118 us (52%)
  starting transfers between devices  64 us (28%)
  Pallas kernels  35.1 us (15%)
  other arithmetic  6.26 us (3%)
    ppermute x20, waiting for transfers between devices, per_device(): done = [lax.ppermute(x, 'pcol', w[1]) for x, w in zip(values, work)]  70.1 us
    ppermute x20, starting transfers between devices, per_device(): done = [lax.ppermute(x, 'pcol', w[1]) for x, w in zip(values, work)]  48.3 us
    ppermute x3, waiting for transfers between devices, per_device(): got = lax.ppermute(near, 'pcol', [(i, i ^ step) for i in range(cols_n)])  39.1 us
    pallas_call x2, Pallas kernels, extract(): call(kernel, 12, out_shape=(pltpu.HBM((tiles_n, 2, block, block), F32), p...  10.1 us
    pallas_call x1, Pallas kernels, update(): call(kernel, 24, out_shape=jax.ShapeDtypeStruct((2, rows, CBLK * block),...  9.85 us
    pallas_call x1, Pallas kernels, panel_factors(): call(kernel, 20, out_shape=(jax.ShapeDtypeStruct((rows, 4 * block), BF16)...  9.12 us
    ppermute x8, starting transfers between devices, cross(): return lax.ppermute(x, 'prow', [(p, p ^ step) for p in range(rows_n)])  8.98 us
    ppermute x8, waiting for transfers between devices, cross(): return lax.ppermute(x, 'prow', [(p, p ^ step) for p in range(rows_n)])  8.84 us
  transfers between devices with their start and end apart: 31, of which 16 were waited for; matrix products, arithmetic and copies ran while one was open for 2% of the time, Pallas kernels for 6%

profile of v4, /device:TPU:29, one launch (start us, length us, event | category | flops | bytes accessed | tf_op | source)
XLA Modules:
  0.0 226.5 jit_solution(18314611343956517081)
XLA Ops:
  0.0 6.0 %pack.1 = (f32[9,2,128,128]{3,2,1,0:T(8,128)}, f32[4,2,128,128]{3,2,1,0:T(8,128)}, f32[4,2,128,128]{3,2,1,0:T(8,128)}, f32[4,2,128,128]{3,2,1,0:T(8,128)}, f32[4...) custom-call(s32[32]{0:T(128)} %bitcast.23, ...), custom_call_target="tpu_custom_call" | custom-call | tf_op jit(solution)/shard_map/pack/pallas_call | solution.py:95
  6.1 2.2 collective-permute-start.9
  13.4 21.7 %collective-permute-done.7 = s32[1,128]{1,0:T(1,128)S(1)} collective-permute-done((s32[1,128]{1,0:T(1,128)S(1)}, s32[1,128]{1,0:T(1,128)S(1)}, u32[]{:S(2)}, u32[]{:S(2)}) %collective-permute-start.7) | collective-permute-done | bytes 544 | tf_op jit(solution)/shard_map/ppermute | solution.py:632
  35.1 2.8 %collective-permute-done.8.rest_refs_1_ = f32[9,2,128,128]{3,2,1,0:T(8,128)} collective-permute-done((f32[9,2,128,128]{3,2,1,0:T(8,128)}, f32[9,2,128,128]{3,2,1,0:T(8,128)}, u32[]{:S(2)}, u32[]{:S(2)}) %collective-permute-start.8) | collective-permute-done | bytes 1179680 | tf_op jit(solution)/shard_map/ppermute | solution.py:618
  37.9 1.3 collective-permute-start.12
  40.0 1.7 collective-permute-start.14
  41.7 2.2 collective-permute-start.15
  44.5 3.5 %collective-permute-start.11 = (s32[2,128]{1,0:T(2,128)S(1)}, s32[2,128]{1,0:T(2,128)}, u32[]{:S(2)}, u32[]{:S(2)}) collective-permute-start(s32[2,128]{1,0:T(2,128)S(1)} %pad_add_fusion.5), channel_id=1, source_target_pairs={{0,2},{1,3},{2,0},{3,1},{4,6},{5,7},{6,4},{7,5},{8,10},{9,11},{10,... | collective-permute-start | bytes 3080 | tf_op jit(solution)/shard_map/ppermute | solution.py:632
  48.0 17.5 %collective-permute-done.11 = s32[2,128]{1,0:T(2,128)} collective-permute-done((s32[2,128]{1,0:T(2,128)S(1)}, s32[2,128]{1,0:T(2,128)}, u32[]{:S(2)}, u32[]{:S(2)}) %collective-permute-start.11) | collective-permute-done | bytes 1056 | tf_op jit(solution)/shard_map/ppermute | solution.py:632
  66.1 3.0 %collective-permute-done.15.rest_refs_7_ = f32[9,2,128,128]{3,2,1,0:T(8,128)} collective-permute-done((f32[9,2,128,128]{3,2,1,0:T(8,128)}, f32[9,2,128,128]{3,2,1,0:T(8,128)}, u32[]{:S(2)}, u32[]{:S(2)}) %collective-permute-start.15) | collective-permute-done | bytes 1179680 | tf_op jit(solution)/shard_map/ppermute | solution.py:618
  69.2 2.9 %collective-permute-start.16 = (s32[4,128]{1,0:T(4,128)S(1)}, s32[4,128]{1,0:T(4,128)S(1)}, u32[]{:S(2)}, u32[]{:S(2)}) collective-permute-start(s32[4,128]{1,0:T(4,128)S(1)} %pad_add_fusion.1), channel_id=1, source_target_pairs={{0,4},{1,5},{2,6},{3,7},{4,0},{5,1},{6,2},{7,3},{8,12},{9,13},{10,... | collective-permute-start | bytes 6152 | tf_op jit(solution)/shard_map/ppermute | solution.py:632
  74.7 1.3 collective-permute-start.17
  77.1 5.0 %collective-permute-start.20 = (f32[4,2,128,128]{3,2,1,0:T(8,128)}, f32[4,2,128,128]{3,2,1,0:T(8,128)S(1)}, u32[]{:S(2)}, u32[]{:S(2)}) collective-permute-start(f32[4,2,128,128]{3,2,1,0:T(8,128)} %get-tuple-element.92), channel_id=1, source_target_pairs={{0,4},{1,5},{6,2},{7,3},{8,12},{9,13},{14,10},{15,11},{16,20},{17,... | collective-permute-start | bytes 1572872 | tf_op jit(solution)/shard_map/ppermute | solution.py:618
  82.8 16.8 %collective-permute-done.17.rest_refs_8_ = f32[9,2,128,128]{3,2,1,0:T(8,128)S(1)} collective-permute-done((f32[9,2,128,128]{3,2,1,0:T(8,128)S(1)}, f32[9,2,128,128]{3,2,1,0:T(8,128)S(1)}, u32[]{:S(2)}, u32[]{:S(2)}) %collective-permute-start.17) | collective-permute-done | bytes 1179680 | tf_op jit(solution)/shard_map/ppermute | solution.py:618
  100.8 9.8 %collective-permute-start.24 = (f32[4,2,128,128]{3,2,1,0:T(8,128)}, f32[4,2,128,128]{3,2,1,0:T(8,128)S(1)}, u32[]{:S(2)}, u32[]{:S(2)}) collective-permute-start(f32[4,2,128,128]{3,2,1,0:T(8,128)} %get-tuple-element.82), channel_id=1, source_target_pairs={{0,2},{1,3},{4,6},{5,7},{6,4},{7,5},{8,10},{9,11},{12,14},{13,15},... | collective-permute-start | bytes 1572872 | tf_op jit(solution)/shard_map/ppermute | solution.py:618
  110.6 1.3 collective-permute-start.25
  111.9 1.3 collective-permute-start.26
  113.2 11.8 %collective-permute-done.22.rest_refs_11_ = f32[9,2,128,128]{3,2,1,0:T(8,128)S(1)} collective-permute-done((f32[9,2,128,128]{3,2,1,0:T(8,128)S(1)}, f32[9,2,128,128]{3,2,1,0:T(8,128)S(1)}, u32[]{:S(2)}, u32[]{:S(2)}) %collective-permute-start.22) | collective-permute-done | bytes 1179680 | tf_op jit(solution)/shard_map/ppermute | solution.py:618
  126.0 5.0 %panel_rows.1 = (f32[32,2,128,128]{3,2,1,0:T(8,128)}, f32[4,128,128]{2,1,0:T(8,128)S(1)}, f32[4,128,128]{2,1,0:T(8,128)S(1)}, f32[4,128,128]{2,1,0:T(8,128)S(1)}) custom-call(s32[8,128]{1,0:T(8,128)S(1)} %pad_add_fusion.near_ref, s32[32]{0:T(128)S(1)} %bitcast.24, s32[256]{0:T(256)S(1)} %get-tuple-element.86.rows_ref, s32[1]{0:T(128)} %bitcast.11.me_ref.col_ref, ...), custom_call_target="tpu_custom_call" | custom-call | tf_op jit(solution)/shard_map/panel_rows/pallas_call | solution.py:239
  131.0 5.8 %collective-permute-start.23 = (f32[4,128,128]{2,1,0:T(8,128)S(1)}, f32[4,128,128]{2,1,0:T(8,128)S(1)}, u32[]{:S(2)}, u32[]{:S(2)}) collective-permute-start(f32[4,128,128]{2,1,0:T(8,128)S(1)} %get-tuple-element.81), channel_id=1, source_target_pairs={{0,8},{8,0},{16,24},{24,16},{1,9},{9,1},{17,25},{25,17},{2,10},{10... | collective-permute-start | bytes 786440 | tf_op jit(solution)/shard_map/ppermute | solution.py:256
  136.8 9.8 %collective-permute-done.26.rest_refs_18_ = f32[4,2,128,128]{3,2,1,0:T(8,128)} collective-permute-done((f32[4,2,128,128]{3,2,1,0:T(8,128)}, f32[4,2,128,128]{3,2,1,0:T(8,128)}, u32[]{:S(2)}, u32[]{:S(2)}) %collective-permute-start.26) | collective-permute-done | bytes 524320 | tf_op jit(solution)/shard_map/ppermute | solution.py:618
  146.6 3.1 %collective-permute-start.28 = (f32[4,2,128,128]{3,2,1,0:T(8,128)}, f32[4,2,128,128]{3,2,1,0:T(8,128)S(1)}, u32[]{:S(2)}, u32[]{:S(2)}) collective-permute-start(f32[4,2,128,128]{3,2,1,0:T(8,128)} %get-tuple-element.90), channel_id=1, source_target_pairs={{2,3},{3,2},{4,5},{5,4},{6,7},{7,6},{10,11},{11,10},{12,13},{13,12... | collective-permute-start | bytes 1572872 | tf_op jit(solution)/shard_map/ppermute | solution.py:618
  149.7 6.5 %collective-permute-start.29 = (f32[4,2,128,128]{3,2,1,0:T(8,128)}, f32[4,2,128,128]{3,2,1,0:T(8,128)S(1)}, u32[]{:S(2)}, u32[]{:S(2)}) collective-permute-start(f32[4,2,128,128]{3,2,1,0:T(8,128)} %get-tuple-element.91), channel_id=1, source_target_pairs={{0,3},{1,2},{4,7},{5,6},{6,5},{7,4},{8,11},{9,10},{12,15},{13,14},... | collective-permute-start | bytes 1572872 | tf_op jit(solution)/shard_map/ppermute | solution.py:618
  156.3 1.3 collective-permute-start.30
  157.6 6.1 %collective-permute-start.31 = (f32[4,2,128,128]{3,2,1,0:T(8,128)}, f32[4,2,128,128]{3,2,1,0:T(8,128)S(1)}, u32[]{:S(2)}, u32[]{:S(2)}) collective-permute-start(f32[4,2,128,128]{3,2,1,0:T(8,128)} %get-tuple-element.93), channel_id=1, source_target_pairs={{0,5},{1,4},{2,7},{3,6},{6,3},{7,2},{8,13},{9,12},{10,15},{11,14},... | collective-permute-start | bytes 1572872 | tf_op jit(solution)/shard_map/ppermute | solution.py:618
  164.1 6.4 %collective-permute-done.27 = f32[4,128,128]{2,1,0:T(8,128)S(1)} collective-permute-done((f32[4,128,128]{2,1,0:T(8,128)S(1)}, f32[4,128,128]{2,1,0:T(8,128)S(1)}, u32[]{:S(2)}, u32[]{:S(2)}) %collective-permute-start.27) | collective-permute-done | bytes 262176 | tf_op jit(solution)/shard_map/ppermute | solution.py:256
  170.5 9.2 %collective-permute-done.29.rest_refs_20_ = f32[4,2,128,128]{3,2,1,0:T(8,128)S(1)} collective-permute-done((f32[4,2,128,128]{3,2,1,0:T(8,128)}, f32[4,2,128,128]{3,2,1,0:T(8,128)S(1)}, u32[]{:S(2)}, u32[]{:S(2)}) %collective-permute-start.29) | collective-permute-done | bytes 524320 | tf_op jit(solution)/shard_map/ppermute | solution.py:618
  179.8 16.1 %collective-permute-done.31.rest_refs_22_ = f32[4,2,128,128]{3,2,1,0:T(8,128)S(1)} collective-permute-done((f32[4,2,128,128]{3,2,1,0:T(8,128)}, f32[4,2,128,128]{3,2,1,0:T(8,128)S(1)}, u32[]{:S(2)}, u32[]{:S(2)}) %collective-permute-start.31) | collective-permute-done | bytes 524320 | tf_op jit(solution)/shard_map/ppermute | solution.py:618
  196.7 5.1 %own_rows.1 = (f32[32,2,128,128]{3,2,1,0:T(8,128)}, f32[4,128,128]{2,1,0:T(8,128)S(1)}, f32[4,128,128]{2,1,0:T(8,128)S(1)}, f32[4,128,128]{2,1,0:T(8,128)S(1)}) custom-call(s32[8,128]{1,0:T(8,128)S(1)} %pad_add_fusion.near_ref, s32[32]{0:T(128)S(1)} %bitcast.25, s32[256]{0:T(256)S(1)} %get-tuple-element.86.rows_ref, s32[1]{0:T(128)} %bitcast.11.me_ref.col_ref, ...), custom_call_target="tpu_custom_call" | custom-call | tf_op jit(solution)/shard_map/own_rows/pallas_call | solution.py:239
  201.9 1.4 collective-permute-start.32
  205.4 9.1 %panel_factors.1 = (bf16[2048,512]{1,0:T(8,128)(2,1)S(1)}, bf16[2048,512]{1,0:T(8,128)(2,1)S(1)}, f32[128,256]{1,0:T(8,128)S(1)}) custom-call(s32[256]{0:T(256)S(1)} %get-tuple-element.130.tgt, s32[129]{0:T(256)S(1)} %pad_add_fusion.4.chain_ref, s32[1]{0:T(128)} %bitcast.10.row_ref, f32[32,2,128,128]{3,2,1,0:T(8,128)} %get-tuple-element.98.held_in, ...), custom_call_target="tpu_custom_call" | custom-call | tf_op jit(solution)/shard_map/panel_factors/pallas_call | solution.py:394
  216.6 9.8 %update.1 = f32[2,2048,256]{2,1,0:T(8,128)} custom-call(s32[256]{0:T(256)S(1)} %get-tuple-element.130.tgt, s32[129]{0:T(256)S(1)} %pad_add_fusion.4.chain_ref, s32[1]{0:T(128)} %bitcast.10.row_ref, s32[1]{0:T(128)} %bitcast.11.me_ref.col_ref, f32[32,2,128,128]{3,2,1,0:T(8,128)} %get-tuple-element.94.held_in, f32[4,128,128]{2,1,0:T(8,128)S(1)} %get-tuple-element.121.new_a, ...), custom_call_target="tpu_custom_call" | custom-call | tf_op jit(solution)/shard_map/update/pallas_call | solution.py:484
  (107 shorter events, 18.5 us)
Async XLA Ops:
  6.1 29.1 %collective-permute-start.9 = (f32[9,2,128,128]{3,2,1,0:T(8,128)}, f32[9,2,128,128]{3,2,1,0:T(8,128)S(1)}, u32[]{:S(2)}, u32[]{:S(2)}) collective-permute-start(f32[9,2,128,128]{3,2,1,0:T(8,128)} %get-tuple-element.61.rest_refs_0_), channel_id=1, source_target_pairs={{2,0},{3,1},{4,2},{5,3},{6,4},{7,5},{10,8},{11,9},{12,10},{13,11},... | collective-permute-start | bytes 3538952 | tf_op jit(solution)/shard_map/ppermute | solution.py:618
  8.2 26.9 %collective-permute-start.10 = (f32[9,2,128,128]{3,2,1,0:T(8,128)}, f32[9,2,128,128]{3,2,1,0:T(8,128)S(1)}, u32[]{:S(2)}, u32[]{:S(2)}) collective-permute-start(f32[9,2,128,128]{3,2,1,0:T(8,128)} %get-tuple-element.61.rest_refs_0_), channel_id=1, source_target_pairs={{0,1},{1,0},{2,3},{3,2},{4,5},{5,4},{6,7},{7,6},{8,9},{9,8},{10,11... | collective-permute-start | bytes 3538952 | tf_op jit(solution)/shard_map/ppermute | solution.py:618
  9.5 28.4 %collective-permute-start.8 = (f32[9,2,128,128]{3,2,1,0:T(8,128)}, f32[9,2,128,128]{3,2,1,0:T(8,128)}, u32[]{:S(2)}, u32[]{:S(2)}) collective-permute-start(f32[9,2,128,128]{3,2,1,0:T(8,128)} %get-tuple-element.61.rest_refs_0_), channel_id=1, source_target_pairs={{0,2},{1,3},{2,4},{3,5},{4,6},{5,7},{8,10},{9,11},{10,12},{11,13},... | collective-permute-start | bytes 3538952 | tf_op jit(solution)/shard_map/ppermute | solution.py:618
  10.8 24.3 %collective-permute-start.7 = (s32[1,128]{1,0:T(1,128)S(1)}, s32[1,128]{1,0:T(1,128)S(1)}, u32[]{:S(2)}, u32[]{:S(2)}) collective-permute-start(s32[1,128]{1,0:T(1,128)S(1)} %bitcast.27), channel_id=1, source_target_pairs={{0,1},{1,0},{2,3},{3,2},{4,5},{5,4},{6,7},{7,6},{8,9},{9,8},{10,11... | collective-permute-start | bytes 1544 | tf_op jit(solution)/shard_map/ppermute | solution.py:632
  37.9 28.2 %collective-permute-start.12 = (f32[9,2,128,128]{3,2,1,0:T(8,128)}, f32[9,2,128,128]{3,2,1,0:T(8,128)S(1)}, u32[]{:S(2)}, u32[]{:S(2)}) collective-permute-start(f32[9,2,128,128]{3,2,1,0:T(8,128)} %collective-permute-done.8.rest_refs_1_), channel_id=1, source_target_pairs={{2,4},{3,5},{4,6},{5,7},{10,12},{11,13},{12,14},{13,15},{18,20},{1... | collective-permute-start | bytes 3538952 | tf_op jit(solution)/shard_map/ppermute | solution.py:618
  39.2 26.9 %collective-permute-start.13 = (f32[9,2,128,128]{3,2,1,0:T(8,128)S(1)}, f32[9,2,128,128]{3,2,1,0:T(8,128)S(1)}, u32[]{:S(2)}, u32[]{:S(2)}) collective-permute-start(f32[9,2,128,128]{3,2,1,0:T(8,128)S(1)} %collective-permute-done.9.rest_refs_2_), channel_id=1, source_target_pairs={{2,0},{3,1},{4,2},{5,3},{10,8},{11,9},{12,10},{13,11},{18,16},{19,... | collective-permute-start | bytes 3538952 | tf_op jit(solution)/shard_map/ppermute | solution.py:618
  40.0 26.1 %collective-permute-start.14 = (f32[9,2,128,128]{3,2,1,0:T(8,128)S(1)}, f32[9,2,128,128]{3,2,1,0:T(8,128)}, u32[]{:S(2)}, u32[]{:S(2)}) collective-permute-start(f32[9,2,128,128]{3,2,1,0:T(8,128)S(1)} %collective-permute-done.9.rest_refs_2_), channel_id=1, source_target_pairs={{0,1},{1,0},{8,9},{9,8},{16,17},{17,16},{24,25},{25,24}} | collective-permute-start | bytes 3538952 | tf_op jit(solution)/shard_map/ppermute | solution.py:618
  41.7 27.5 %collective-permute-start.15 = (f32[9,2,128,128]{3,2,1,0:T(8,128)}, f32[9,2,128,128]{3,2,1,0:T(8,128)}, u32[]{:S(2)}, u32[]{:S(2)}) collective-permute-start(f32[9,2,128,128]{3,2,1,0:T(8,128)} %collective-permute-done.8.rest_refs_1_), channel_id=1, source_target_pairs={{2,3},{3,2},{4,5},{5,4},{6,7},{7,6},{10,11},{11,10},{12,13},{13,12... | collective-permute-start | bytes 3538952 | tf_op jit(solution)/shard_map/ppermute | solution.py:618
  44.5 20.9 %collective-permute-start.11 = (s32[2,128]{1,0:T(2,128)S(1)}, s32[2,128]{1,0:T(2,128)}, u32[]{:S(2)}, u32[]{:S(2)}) collective-permute-start(s32[2,128]{1,0:T(2,128)S(1)} %pad_add_fusion.5), channel_id=1, source_target_pairs={{0,2},{1,3},{2,0},{3,1},{4,6},{5,7},{6,4},{7,5},{8,10},{9,11},{10,... | collective-permute-start | bytes 3080 | tf_op jit(solution)/shard_map/ppermute | solution.py:632
  69.2 4.1 %collective-permute-start.16 = (s32[4,128]{1,0:T(4,128)S(1)}, s32[4,128]{1,0:T(4,128)S(1)}, u32[]{:S(2)}, u32[]{:S(2)}) collective-permute-start(s32[4,128]{1,0:T(4,128)S(1)} %pad_add_fusion.1), channel_id=1, source_target_pairs={{0,4},{1,5},{2,6},{3,7},{4,0},{5,1},{6,2},{7,3},{8,12},{9,13},{10,... | collective-permute-start | bytes 6152 | tf_op jit(solution)/shard_map/ppermute | solution.py:632
  74.7 24.9 %collective-permute-start.17 = (f32[9,2,128,128]{3,2,1,0:T(8,128)S(1)}, f32[9,2,128,128]{3,2,1,0:T(8,128)S(1)}, u32[]{:S(2)}, u32[]{:S(2)}) collective-permute-start(f32[9,2,128,128]{3,2,1,0:T(8,128)S(1)} %collective-permute-done.12.rest_refs_4_), channel_id=1, source_target_pairs={{4,6},{5,7},{12,14},{13,15},{20,22},{21,23},{28,30},{29,31}} | collective-permute-start | bytes 3538952 | tf_op jit(solution)/shard_map/ppermute | solution.py:618
  76.0 23.6 %collective-permute-start.18 = (f32[9,2,128,128]{3,2,1,0:T(8,128)S(1)}, f32[9,2,128,128]{3,2,1,0:T(8,128)S(1)}, u32[]{:S(2)}, u32[]{:S(2)}) collective-permute-start(f32[9,2,128,128]{3,2,1,0:T(8,128)S(1)} %collective-permute-done.13.rest_refs_5_), channel_id=1, source_target_pairs={{2,0},{3,1},{10,8},{11,9},{18,16},{19,17},{26,24},{27,25}} | collective-permute-start | bytes 3538952 | tf_op jit(solution)/shard_map/ppermute | solution.py:618
  76.8 23.8 %collective-permute-start.19 = (f32[9,2,128,128]{3,2,1,0:T(8,128)}, f32[9,2,128,128]{3,2,1,0:T(8,128)S(1)}, u32[]{:S(2)}, u32[]{:S(2)}) collective-permute-start(f32[9,2,128,128]{3,2,1,0:T(8,128)} %select_select_fusion.1), channel_id=1, source_target_pairs={{0,1},{1,0},{2,3},{3,2},{4,5},{5,4},{6,7},{7,6},{8,9},{9,8},{10,11... | collective-permute-start | bytes 3538952 | tf_op jit(solution)/shard_map/ppermute | solution.py:618
  77.1 22.9 %collective-permute-start.20 = (f32[4,2,128,128]{3,2,1,0:T(8,128)}, f32[4,2,128,128]{3,2,1,0:T(8,128)S(1)}, u32[]{:S(2)}, u32[]{:S(2)}) collective-permute-start(f32[4,2,128,128]{3,2,1,0:T(8,128)} %get-tuple-element.92), channel_id=1, source_target_pairs={{0,4},{1,5},{6,2},{7,3},{8,12},{9,13},{14,10},{15,11},{16,20},{17,... | collective-permute-start | bytes 1572872 | tf_op jit(solution)/shard_map/ppermute | solution.py:618
  82.1 17.9 %collective-permute-start.21 = (f32[4,2,128,128]{3,2,1,0:T(8,128)}, f32[4,2,128,128]{3,2,1,0:T(8,128)S(1)}, u32[]{:S(2)}, u32[]{:S(2)}) collective-permute-start(f32[4,2,128,128]{3,2,1,0:T(8,128)} %get-tuple-element.83), channel_id=1, source_target_pairs={{2,4},{3,5},{4,2},{5,3},{10,12},{11,13},{12,10},{13,11},{18,20},{1... | collective-permute-start | bytes 1572872 | tf_op jit(solution)/shard_map/ppermute | solution.py:618
  100.5 24.4 %collective-permute-start.22 = (f32[9,2,128,128]{3,2,1,0:T(8,128)S(1)}, f32[9,2,128,128]{3,2,1,0:T(8,128)S(1)}, u32[]{:S(2)}, u32[]{:S(2)}) collective-permute-start(f32[9,2,128,128]{3,2,1,0:T(8,128)S(1)} %select_select_fusion), channel_id=1, source_target_pairs={{0,1},{1,0},{2,3},{3,2},{4,5},{5,4},{6,7},{7,6},{8,9},{9,8},{10,11... | collective-permute-start | bytes 3538952 | tf_op jit(solution)/shard_map/ppermute | solution.py:618
  100.8 36.0 %collective-permute-start.24 = (f32[4,2,128,128]{3,2,1,0:T(8,128)}, f32[4,2,128,128]{3,2,1,0:T(8,128)S(1)}, u32[]{:S(2)}, u32[]{:S(2)}) collective-permute-start(f32[4,2,128,128]{3,2,1,0:T(8,128)} %get-tuple-element.82), channel_id=1, source_target_pairs={{0,2},{1,3},{4,6},{5,7},{6,4},{7,5},{8,10},{9,11},{12,14},{13,15},... | collective-permute-start | bytes 1572872 | tf_op jit(solution)/shard_map/ppermute | solution.py:618
  110.6 26.2 %collective-permute-start.25 = (f32[4,2,128,128]{3,2,1,0:T(8,128)}, f32[4,2,128,128]{3,2,1,0:T(8,128)S(1)}, u32[]{:S(2)}, u32[]{:S(2)}) collective-permute-start(f32[4,2,128,128]{3,2,1,0:T(8,128)} %get-tuple-element.83), channel_id=1, source_target_pairs={{0,6},{1,7},{8,14},{9,15},{16,22},{17,23},{24,30},{25,31}} | collective-permute-start | bytes 1572872 | tf_op jit(solution)/shard_map/ppermute | solution.py:618
  111.9 34.8 %collective-permute-start.26 = (f32[4,2,128,128]{3,2,1,0:T(8,128)}, f32[4,2,128,128]{3,2,1,0:T(8,128)}, u32[]{:S(2)}, u32[]{:S(2)}) collective-permute-start(f32[4,2,128,128]{3,2,1,0:T(8,128)} %get-tuple-element.84), channel_id=1, source_target_pairs={{0,7},{1,6},{2,5},{3,4},{4,3},{5,2},{8,15},{9,14},{10,13},{11,12},... | collective-permute-start | bytes 1572872 | tf_op jit(solution)/shard_map/ppermute | solution.py:618
  113.2 83.6 %copy-start.18 = (s32[1,32]{1,0:T(1,128)S(1)}, s32[1,32]{1,0:T(1,128)}, u32[]{:S(2)}) copy-start(s32[1,32]{1,0:T(1,128)} %param.7) | copy-start | bytes 388
  131.0 32.7 %collective-permute-start.23 = (f32[4,128,128]{2,1,0:T(8,128)S(1)}, f32[4,128,128]{2,1,0:T(8,128)S(1)}, u32[]{:S(2)}, u32[]{:S(2)}) collective-permute-start(f32[4,128,128]{2,1,0:T(8,128)S(1)} %get-tuple-element.81), channel_id=1, source_target_pairs={{0,8},{8,0},{16,24},{24,16},{1,9},{9,1},{17,25},{25,17},{2,10},{10... | collective-permute-start | bytes 786440 | tf_op jit(solution)/shard_map/ppermute | solution.py:256
  146.6 23.9 %collective-permute-start.28 = (f32[4,2,128,128]{3,2,1,0:T(8,128)}, f32[4,2,128,128]{3,2,1,0:T(8,128)S(1)}, u32[]{:S(2)}, u32[]{:S(2)}) collective-permute-start(f32[4,2,128,128]{3,2,1,0:T(8,128)} %get-tuple-element.90), channel_id=1, source_target_pairs={{2,3},{3,2},{4,5},{5,4},{6,7},{7,6},{10,11},{11,10},{12,13},{13,12... | collective-permute-start | bytes 1572872 | tf_op jit(solution)/shard_map/ppermute | solution.py:618
  149.7 30.1 %collective-permute-start.29 = (f32[4,2,128,128]{3,2,1,0:T(8,128)}, f32[4,2,128,128]{3,2,1,0:T(8,128)S(1)}, u32[]{:S(2)}, u32[]{:S(2)}) collective-permute-start(f32[4,2,128,128]{3,2,1,0:T(8,128)} %get-tuple-element.91), channel_id=1, source_target_pairs={{0,3},{1,2},{4,7},{5,6},{6,5},{7,4},{8,11},{9,10},{12,15},{13,14},... | collective-permute-start | bytes 1572872 | tf_op jit(solution)/shard_map/ppermute | solution.py:618
  156.3 23.5 %collective-permute-start.30 = (f32[4,2,128,128]{3,2,1,0:T(8,128)}, f32[4,2,128,128]{3,2,1,0:T(8,128)S(1)}, u32[]{:S(2)}, u32[]{:S(2)}) collective-permute-start(f32[4,2,128,128]{3,2,1,0:T(8,128)} %get-tuple-element.92), channel_id=1, source_target_pairs={{2,6},{3,7},{10,14},{11,15},{18,22},{19,23},{26,30},{27,31}} | collective-permute-start | bytes 1572872 | tf_op jit(solution)/shard_map/ppermute | solution.py:618
  157.6 38.3 %collective-permute-start.31 = (f32[4,2,128,128]{3,2,1,0:T(8,128)}, f32[4,2,128,128]{3,2,1,0:T(8,128)S(1)}, u32[]{:S(2)}, u32[]{:S(2)}) collective-permute-start(f32[4,2,128,128]{3,2,1,0:T(8,128)} %get-tuple-element.93), channel_id=1, source_target_pairs={{0,5},{1,4},{2,7},{3,6},{6,3},{7,2},{8,13},{9,12},{10,15},{11,14},... | collective-permute-start | bytes 1572872 | tf_op jit(solution)/shard_map/ppermute | solution.py:618
  163.8 6.7 %collective-permute-start.27 = (f32[4,128,128]{2,1,0:T(8,128)S(1)}, f32[4,128,128]{2,1,0:T(8,128)S(1)}, u32[]{:S(2)}, u32[]{:S(2)}) collective-permute-start(f32[4,128,128]{2,1,0:T(8,128)S(1)} %get-tuple-element.85), channel_id=1, source_target_pairs={{0,16},{8,24},{16,0},{24,8},{1,17},{9,25},{17,1},{25,9},{2,18},{10... | collective-permute-start | bytes 786440 | tf_op jit(solution)/shard_map/ppermute | solution.py:256
  201.9 2.6 %collective-permute-start.32 = (f32[4,128,128]{2,1,0:T(8,128)S(1)}, f32[4,128,128]{2,1,0:T(8,128)S(1)}, u32[]{:S(2)}, u32[]{:S(2)}) collective-permute-start(f32[4,128,128]{2,1,0:T(8,128)S(1)} %get-tuple-element.96), channel_id=1, source_target_pairs={{0,8},{8,0},{16,24},{24,16},{1,9},{9,1},{17,25},{25,17},{2,10},{10... | collective-permute-start | bytes 786440 | tf_op jit(solution)/shard_map/ppermute | solution.py:256
  203.4 1.6 collective-permute-start.34
  203.5 1.9 collective-permute-start.35
  204.6 10.0 %collective-permute-start.33 = (f32[4,128,128]{2,1,0:T(8,128)S(1)}, f32[4,128,128]{2,1,0:T(8,128)S(1)}, u32[]{:S(2)}, u32[]{:S(2)}) collective-permute-start(f32[4,128,128]{2,1,0:T(8,128)S(1)} %get-tuple-element.107), channel_id=1, source_target_pairs={{0,16},{8,24},{16,0},{24,8},{1,17},{9,25},{17,1},{25,9},{2,18},{10... | collective-permute-start | bytes 786440 | tf_op jit(solution)/shard_map/ppermute | solution.py:256
  214.7 1.6 collective-permute-start.36
  214.9 1.7 collective-permute-start.37
  (23 other events, 678.1 us)

commit v5 on v4

--- a/solution.py
+++ b/solution.py
@@ -609,7 +609,7 @@
         else:
             gathered_all = [got for got, w in zip(done, last) if not isinstance(w[2], int)]
             shifted_first = [got for got, w in zip(done, last) if isinstance(w[2], int)]
-        for k in range(1, cols_n):
+        for k in reversed(range(1, cols_n)):
             pairs = shift_pairs(k, phase)
             if pairs:
                 work.append((shifted[k - 1], pairs, k, pairs))

time: 227 us -> 224 us (0.987)
  starting transfers between devices: 64 us -> 54 us
  waiting for transfers between devices: 118 us -> 123 us
    ppermute x20, starting transfers between devices: 48.3 us -> 41 us  [per_device(): done = [lax.ppermute(x, 'pcol', w[1]) for x, w in zip(values, work)]]
    ppermute x20, waiting for transfers between devices: 70.1 us -> 73.7 us  [per_device(): done = [lax.ppermute(x, 'pcol', w[1]) for x, w in zip(values, work)]]
    ppermute x8, starting transfers between devices: 8.98 us -> 6.34 us  [cross(): return lax.ppermute(x, 'prow', [(p, p ^ step) for p in range(rows_n)])]
where the time goes in v5:
time: 224 us; the launch traced here: 222 us
  waiting for transfers between devices  123 us (55%)
  starting transfers between devices  54 us (24%)
  Pallas kernels  35.3 us (16%)
  other arithmetic  6.26 us (3%)
  local copies, waits for them, and re-layouts  2.67 us (1%)
    ppermute x20, waiting for transfers between devices, per_device(): done = [lax.ppermute(x, 'pcol', w[1]) for x, w in zip(values, work)]  73.7 us
    ppermute x20, starting transfers between devices, per_device(): done = [lax.ppermute(x, 'pcol', w[1]) for x, w in zip(values, work)]  41 us
    ppermute x3, waiting for transfers between devices, per_device(): got = lax.ppermute(near, 'pcol', [(i, i ^ step) for i in range(cols_n)])  39.4 us
    pallas_call x2, Pallas kernels, extract(): call(kernel, 12, out_shape=(pltpu.HBM((tiles_n, 2, block, block), F32), p...  10.1 us
    ppermute x8, waiting for transfers between devices, cross(): return lax.ppermute(x, 'prow', [(p, p ^ step) for p in range(rows_n)])  9.88 us
    pallas_call x1, Pallas kernels, update(): call(kernel, 24, out_shape=jax.ShapeDtypeStruct((2, rows, CBLK * block),...  9.85 us
    pallas_call x1, Pallas kernels, panel_factors(): call(kernel, 20, out_shape=(jax.ShapeDtypeStruct((rows, 4 * block), BF16)...  9.12 us
    ppermute x3, starting transfers between devices, per_device(): got = lax.ppermute(near, 'pcol', [(i, i ^ step) for i in range(cols_n)])  6.73 us
  transfers between devices with their start and end apart: 31, of which 16 were waited for; matrix products, arithmetic and copies ran while one was open for 2% of the time, Pallas kernels for 6%

profile of v5, /device:TPU:29, one launch (start us, length us, event | category | flops | bytes accessed | tf_op | source)
XLA Modules:
  0.0 222.5 jit_solution(6312683907837648622)
XLA Ops:
  0.0 6.2 %pack.1 = (f32[9,2,128,128]{3,2,1,0:T(8,128)}, f32[4,2,128,128]{3,2,1,0:T(8,128)}, f32[4,2,128,128]{3,2,1,0:T(8,128)}, f32[4,2,128,128]{3,2,1,0:T(8,128)}, f32[4...) custom-call(s32[32]{0:T(128)} %bitcast.23, ...), custom_call_target="tpu_custom_call" | custom-call | tf_op jit(solution)/shard_map/pack/pallas_call | solution.py:95
  6.2 2.2 collective-permute-start.9
  9.6 1.3 collective-permute-start.8
  13.6 21.8 %collective-permute-done.7 = s32[1,128]{1,0:T(1,128)S(1)} collective-permute-done((s32[1,128]{1,0:T(1,128)S(1)}, s32[1,128]{1,0:T(1,128)S(1)}, u32[]{:S(2)}, u32[]{:S(2)}) %collective-permute-start.7) | collective-permute-done | bytes 544 | tf_op jit(solution)/shard_map/ppermute | solution.py:632
  35.4 2.8 %collective-permute-done.8.rest_refs_1_ = f32[9,2,128,128]{3,2,1,0:T(8,128)} collective-permute-done((f32[9,2,128,128]{3,2,1,0:T(8,128)}, f32[9,2,128,128]{3,2,1,0:T(8,128)}, u32[]{:S(2)}, u32[]{:S(2)}) %collective-permute-start.8) | collective-permute-done | bytes 1179680 | tf_op jit(solution)/shard_map/ppermute | solution.py:618
  38.2 1.3 collective-permute-start.12
  40.3 1.7 collective-permute-start.14
  42.0 2.2 collective-permute-start.15
  44.8 3.5 %collective-permute-start.11 = (s32[2,128]{1,0:T(2,128)S(1)}, s32[2,128]{1,0:T(2,128)}, u32[]{:S(2)}, u32[]{:S(2)}) collective-permute-start(s32[2,128]{1,0:T(2,128)S(1)} %pad_add_fusion.5), channel_id=1, source_target_pairs={{0,2},{1,3},{2,0},{3,1},{4,6},{5,7},{6,4},{7,5},{8,10},{9,11},{10,... | collective-permute-start | bytes 3080 | tf_op jit(solution)/shard_map/ppermute | solution.py:632
  48.3 17.6 %collective-permute-done.11 = s32[2,128]{1,0:T(2,128)} collective-permute-done((s32[2,128]{1,0:T(2,128)S(1)}, s32[2,128]{1,0:T(2,128)}, u32[]{:S(2)}, u32[]{:S(2)}) %collective-permute-start.11) | collective-permute-done | bytes 1056 | tf_op jit(solution)/shard_map/ppermute | solution.py:632
  66.5 3.0 %collective-permute-done.15.rest_refs_7_ = f32[9,2,128,128]{3,2,1,0:T(8,128)} collective-permute-done((f32[9,2,128,128]{3,2,1,0:T(8,128)}, f32[9,2,128,128]{3,2,1,0:T(8,128)}, u32[]{:S(2)}, u32[]{:S(2)}) %collective-permute-start.15) | collective-permute-done | bytes 1179680 | tf_op jit(solution)/shard_map/ppermute | solution.py:618
  69.6 2.9 %collective-permute-start.16 = (s32[4,128]{1,0:T(4,128)S(1)}, s32[4,128]{1,0:T(4,128)S(1)}, u32[]{:S(2)}, u32[]{:S(2)}) collective-permute-start(s32[4,128]{1,0:T(4,128)S(1)} %pad_add_fusion.1), channel_id=1, source_target_pairs={{0,4},{1,5},{2,6},{3,7},{4,0},{5,1},{6,2},{7,3},{8,12},{9,13},{10,... | collective-permute-start | bytes 6152 | tf_op jit(solution)/shard_map/ppermute | solution.py:632
  75.2 1.3 collective-permute-start.17
  78.2 6.6 %collective-permute-start.21 = (f32[4,2,128,128]{3,2,1,0:T(8,128)}, f32[4,2,128,128]{3,2,1,0:T(8,128)S(1)}, u32[]{:S(2)}, u32[]{:S(2)}) collective-permute-start(f32[4,2,128,128]{3,2,1,0:T(8,128)} %get-tuple-element.91), channel_id=1, source_target_pairs={{0,4},{1,5},{6,2},{7,3},{8,12},{9,13},{14,10},{15,11},{16,20},{17,... | collective-permute-start | bytes 1572872 | tf_op jit(solution)/shard_map/ppermute | solution.py:618
  84.8 15.5 %collective-permute-done.17.rest_refs_8_ = f32[9,2,128,128]{3,2,1,0:T(8,128)S(1)} collective-permute-done((f32[9,2,128,128]{3,2,1,0:T(8,128)S(1)}, f32[9,2,128,128]{3,2,1,0:T(8,128)S(1)}, u32[]{:S(2)}, u32[]{:S(2)}) %collective-permute-start.17) | collective-permute-done | bytes 1179680 | tf_op jit(solution)/shard_map/ppermute | solution.py:618
  101.3 1.3 collective-permute-start.24
  102.6 1.3 collective-permute-start.25
  103.9 6.7 %collective-permute-start.26 = (f32[4,2,128,128]{3,2,1,0:T(8,128)}, f32[4,2,128,128]{3,2,1,0:T(8,128)}, u32[]{:S(2)}, u32[]{:S(2)}) collective-permute-start(f32[4,2,128,128]{3,2,1,0:T(8,128)} %get-tuple-element.84), channel_id=1, source_target_pairs={{0,2},{1,3},{4,6},{5,7},{6,4},{7,5},{8,10},{9,11},{12,14},{13,15},... | collective-permute-start | bytes 1572872 | tf_op jit(solution)/shard_map/ppermute | solution.py:618
  110.7 27.8 %collective-permute-done.22.rest_refs_11_ = f32[9,2,128,128]{3,2,1,0:T(8,128)S(1)} collective-permute-done((f32[9,2,128,128]{3,2,1,0:T(8,128)S(1)}, f32[9,2,128,128]{3,2,1,0:T(8,128)S(1)}, u32[]{:S(2)}, u32[]{:S(2)}) %collective-permute-start.22) | collective-permute-done | bytes 1179680 | tf_op jit(solution)/shard_map/ppermute | solution.py:618
  139.6 5.0 %panel_rows.1 = (f32[32,2,128,128]{3,2,1,0:T(8,128)}, f32[4,128,128]{2,1,0:T(8,128)S(1)}, f32[4,128,128]{2,1,0:T(8,128)S(1)}, f32[4,128,128]{2,1,0:T(8,128)S(1)}) custom-call(s32[8,128]{1,0:T(8,128)S(1)} %pad_add_fusion.near_ref, s32[32]{0:T(128)S(1)} %bitcast.24, s32[256]{0:T(256)S(1)} %get-tuple-element.86.rows_ref, s32[1]{0:T(128)} %bitcast.11.me_ref.col_ref, ...), custom_call_target="tpu_custom_call" | custom-call | tf_op jit(solution)/shard_map/panel_rows/pallas_call | solution.py:239
  144.5 3.9 %collective-permute-start.23 = (f32[4,128,128]{2,1,0:T(8,128)S(1)}, f32[4,128,128]{2,1,0:T(8,128)S(1)}, u32[]{:S(2)}, u32[]{:S(2)}) collective-permute-start(f32[4,128,128]{2,1,0:T(8,128)S(1)} %get-tuple-element.81), channel_id=1, source_target_pairs={{0,8},{8,0},{16,24},{24,16},{1,9},{9,1},{17,25},{25,17},{2,10},{10... | collective-permute-start | bytes 786440 | tf_op jit(solution)/shard_map/ppermute | solution.py:256
  148.5 5.0 %collective-permute-start.28 = (f32[4,2,128,128]{3,2,1,0:T(8,128)}, f32[4,2,128,128]{3,2,1,0:T(8,128)S(1)}, u32[]{:S(2)}, u32[]{:S(2)}) collective-permute-start(f32[4,2,128,128]{3,2,1,0:T(8,128)} %get-tuple-element.90), channel_id=1, source_target_pairs={{0,5},{1,4},{2,7},{3,6},{6,3},{7,2},{8,13},{9,12},{10,15},{11,14},... | collective-permute-start | bytes 1572872 | tf_op jit(solution)/shard_map/ppermute | solution.py:618
  153.5 1.3 collective-permute-start.29
  154.8 1.9 collective-permute-start.30
  156.7 3.2 %collective-permute-start.31 = (f32[4,2,128,128]{3,2,1,0:T(8,128)}, f32[4,2,128,128]{3,2,1,0:T(8,128)S(1)}, u32[]{:S(2)}, u32[]{:S(2)}) collective-permute-start(f32[4,2,128,128]{3,2,1,0:T(8,128)} %get-tuple-element.93), channel_id=1, source_target_pairs={{2,3},{3,2},{4,5},{5,4},{6,7},{7,6},{10,11},{11,10},{12,13},{13,12... | collective-permute-start | bytes 1572872 | tf_op jit(solution)/shard_map/ppermute | solution.py:618
  160.1 7.2 %collective-permute-done.27 = f32[4,128,128]{2,1,0:T(8,128)S(1)} collective-permute-done((f32[4,128,128]{2,1,0:T(8,128)S(1)}, f32[4,128,128]{2,1,0:T(8,128)S(1)}, u32[]{:S(2)}, u32[]{:S(2)}) %collective-permute-start.27) | collective-permute-done | bytes 262176 | tf_op jit(solution)/shard_map/ppermute | solution.py:256
  167.3 9.9 %collective-permute-done.28.rest_refs_19_ = f32[4,2,128,128]{3,2,1,0:T(8,128)S(1)} collective-permute-done((f32[4,2,128,128]{3,2,1,0:T(8,128)}, f32[4,2,128,128]{3,2,1,0:T(8,128)S(1)}, u32[]{:S(2)}, u32[]{:S(2)}) %collective-permute-start.28) | collective-permute-done | bytes 524320 | tf_op jit(solution)/shard_map/ppermute | solution.py:618
  177.2 11.3 %collective-permute-done.29.rest_refs_20_ = f32[4,2,128,128]{3,2,1,0:T(8,128)S(1)} collective-permute-done((f32[4,2,128,128]{3,2,1,0:T(8,128)}, f32[4,2,128,128]{3,2,1,0:T(8,128)S(1)}, u32[]{:S(2)}, u32[]{:S(2)}) %collective-permute-start.29) | collective-permute-done | bytes 524320 | tf_op jit(solution)/shard_map/ppermute | solution.py:618
  188.5 2.9 %collective-permute-done.30.rest_refs_21_ = f32[4,2,128,128]{3,2,1,0:T(8,128)S(1)} collective-permute-done((f32[4,2,128,128]{3,2,1,0:T(8,128)}, f32[4,2,128,128]{3,2,1,0:T(8,128)S(1)}, u32[]{:S(2)}, u32[]{:S(2)}) %collective-permute-start.30) | collective-permute-done | bytes 524320 | tf_op jit(solution)/shard_map/ppermute | solution.py:618
  193.0 5.2 %own_rows.1 = (f32[32,2,128,128]{3,2,1,0:T(8,128)}, f32[4,128,128]{2,1,0:T(8,128)S(1)}, f32[4,128,128]{2,1,0:T(8,128)S(1)}, f32[4,128,128]{2,1,0:T(8,128)S(1)}) custom-call(s32[8,128]{1,0:T(8,128)S(1)} %pad_add_fusion.near_ref, s32[32]{0:T(128)S(1)} %bitcast.25, s32[256]{0:T(256)S(1)} %get-tuple-element.86.rows_ref, s32[1]{0:T(128)} %bitcast.11.me_ref.col_ref, ...), custom_call_target="tpu_custom_call" | custom-call | tf_op jit(solution)/shard_map/own_rows/pallas_call | solution.py:239
  201.4 9.1 %panel_factors.1 = (bf16[2048,512]{1,0:T(8,128)(2,1)S(1)}, bf16[2048,512]{1,0:T(8,128)(2,1)S(1)}, f32[128,256]{1,0:T(8,128)S(1)}) custom-call(s32[256]{0:T(256)S(1)} %get-tuple-element.130.tgt, s32[129]{0:T(256)S(1)} %pad_add_fusion.4.chain_ref, s32[1]{0:T(128)} %bitcast.10.row_ref, f32[32,2,128,128]{3,2,1,0:T(8,128)} %get-tuple-element.98.held_in, ...), custom_call_target="tpu_custom_call" | custom-call | tf_op jit(solution)/shard_map/panel_factors/pallas_call | solution.py:394
  212.6 9.8 %update.1 = f32[2,2048,256]{2,1,0:T(8,128)} custom-call(s32[256]{0:T(256)S(1)} %get-tuple-element.130.tgt, s32[129]{0:T(256)S(1)} %pad_add_fusion.4.chain_ref, s32[1]{0:T(128)} %bitcast.10.row_ref, s32[1]{0:T(128)} %bitcast.11.me_ref.col_ref, f32[32,2,128,128]{3,2,1,0:T(8,128)} %get-tuple-element.94.held_in, f32[4,128,128]{2,1,0:T(8,128)S(1)} %get-tuple-element.121.new_a, ...), custom_call_target="tpu_custom_call" | custom-call | tf_op jit(solution)/shard_map/update/pallas_call | solution.py:484
  (107 shorter events, 18.7 us)
Async XLA Ops:
  6.2 29.2 %collective-permute-start.9 = (f32[9,2,128,128]{3,2,1,0:T(8,128)}, f32[9,2,128,128]{3,2,1,0:T(8,128)S(1)}, u32[]{:S(2)}, u32[]{:S(2)}) collective-permute-start(f32[9,2,128,128]{3,2,1,0:T(8,128)} %get-tuple-element.61.rest_refs_0_), channel_id=1, source_target_pairs={{2,0},{3,1},{4,2},{5,3},{6,4},{7,5},{10,8},{11,9},{12,10},{13,11},... | collective-permute-start | bytes 3538952 | tf_op jit(solution)/shard_map/ppermute | solution.py:618
  8.4 27.1 %collective-permute-start.10 = (f32[9,2,128,128]{3,2,1,0:T(8,128)}, f32[9,2,128,128]{3,2,1,0:T(8,128)S(1)}, u32[]{:S(2)}, u32[]{:S(2)}) collective-permute-start(f32[9,2,128,128]{3,2,1,0:T(8,128)} %get-tuple-element.61.rest_refs_0_), channel_id=1, source_target_pairs={{0,1},{1,0},{2,3},{3,2},{4,5},{5,4},{6,7},{7,6},{8,9},{9,8},{10,11... | collective-permute-start | bytes 3538952 | tf_op jit(solution)/shard_map/ppermute | solution.py:618
  9.6 28.6 %collective-permute-start.8 = (f32[9,2,128,128]{3,2,1,0:T(8,128)}, f32[9,2,128,128]{3,2,1,0:T(8,128)}, u32[]{:S(2)}, u32[]{:S(2)}) collective-permute-start(f32[9,2,128,128]{3,2,1,0:T(8,128)} %get-tuple-element.61.rest_refs_0_), channel_id=1, source_target_pairs={{0,2},{1,3},{2,4},{3,5},{4,6},{5,7},{8,10},{9,11},{10,12},{11,13},... | collective-permute-start | bytes 3538952 | tf_op jit(solution)/shard_map/ppermute | solution.py:618
  10.9 24.5 %collective-permute-start.7 = (s32[1,128]{1,0:T(1,128)S(1)}, s32[1,128]{1,0:T(1,128)S(1)}, u32[]{:S(2)}, u32[]{:S(2)}) collective-permute-start(s32[1,128]{1,0:T(1,128)S(1)} %bitcast.27), channel_id=1, source_target_pairs={{0,1},{1,0},{2,3},{3,2},{4,5},{5,4},{6,7},{7,6},{8,9},{9,8},{10,11... | collective-permute-start | bytes 1544 | tf_op jit(solution)/shard_map/ppermute | solution.py:632
  38.2 28.3 %collective-permute-start.12 = (f32[9,2,128,128]{3,2,1,0:T(8,128)}, f32[9,2,128,128]{3,2,1,0:T(8,128)S(1)}, u32[]{:S(2)}, u32[]{:S(2)}) collective-permute-start(f32[9,2,128,128]{3,2,1,0:T(8,128)} %collective-permute-done.8.rest_refs_1_), channel_id=1, source_target_pairs={{2,4},{3,5},{4,6},{5,7},{10,12},{11,13},{12,14},{13,15},{18,20},{1... | collective-permute-start | bytes 3538952 | tf_op jit(solution)/shard_map/ppermute | solution.py:618
  39.5 27.0 %collective-permute-start.13 = (f32[9,2,128,128]{3,2,1,0:T(8,128)S(1)}, f32[9,2,128,128]{3,2,1,0:T(8,128)S(1)}, u32[]{:S(2)}, u32[]{:S(2)}) collective-permute-start(f32[9,2,128,128]{3,2,1,0:T(8,128)S(1)} %collective-permute-done.9.rest_refs_2_), channel_id=1, source_target_pairs={{2,0},{3,1},{4,2},{5,3},{10,8},{11,9},{12,10},{13,11},{18,16},{19,... | collective-permute-start | bytes 3538952 | tf_op jit(solution)/shard_map/ppermute | solution.py:618
  40.3 26.3 %collective-permute-start.14 = (f32[9,2,128,128]{3,2,1,0:T(8,128)S(1)}, f32[9,2,128,128]{3,2,1,0:T(8,128)}, u32[]{:S(2)}, u32[]{:S(2)}) collective-permute-start(f32[9,2,128,128]{3,2,1,0:T(8,128)S(1)} %collective-permute-done.9.rest_refs_2_), channel_id=1, source_target_pairs={{0,1},{1,0},{8,9},{9,8},{16,17},{17,16},{24,25},{25,24}} | collective-permute-start | bytes 3538952 | tf_op jit(solution)/shard_map/ppermute | solution.py:618
  42.0 27.6 %collective-permute-start.15 = (f32[9,2,128,128]{3,2,1,0:T(8,128)}, f32[9,2,128,128]{3,2,1,0:T(8,128)}, u32[]{:S(2)}, u32[]{:S(2)}) collective-permute-start(f32[9,2,128,128]{3,2,1,0:T(8,128)} %collective-permute-done.8.rest_refs_1_), channel_id=1, source_target_pairs={{2,3},{3,2},{4,5},{5,4},{6,7},{7,6},{10,11},{11,10},{12,13},{13,12... | collective-permute-start | bytes 3538952 | tf_op jit(solution)/shard_map/ppermute | solution.py:618
  44.8 21.1 %collective-permute-start.11 = (s32[2,128]{1,0:T(2,128)S(1)}, s32[2,128]{1,0:T(2,128)}, u32[]{:S(2)}, u32[]{:S(2)}) collective-permute-start(s32[2,128]{1,0:T(2,128)S(1)} %pad_add_fusion.5), channel_id=1, source_target_pairs={{0,2},{1,3},{2,0},{3,1},{4,6},{5,7},{6,4},{7,5},{8,10},{9,11},{10,... | collective-permute-start | bytes 3080 | tf_op jit(solution)/shard_map/ppermute | solution.py:632
  69.6 4.2 %collective-permute-start.16 = (s32[4,128]{1,0:T(4,128)S(1)}, s32[4,128]{1,0:T(4,128)S(1)}, u32[]{:S(2)}, u32[]{:S(2)}) collective-permute-start(s32[4,128]{1,0:T(4,128)S(1)} %pad_add_fusion.1), channel_id=1, source_target_pairs={{0,4},{1,5},{2,6},{3,7},{4,0},{5,1},{6,2},{7,3},{8,12},{9,13},{10,... | collective-permute-start | bytes 6152 | tf_op jit(solution)/shard_map/ppermute | solution.py:632
  75.2 25.1 %collective-permute-start.17 = (f32[9,2,128,128]{3,2,1,0:T(8,128)S(1)}, f32[9,2,128,128]{3,2,1,0:T(8,128)S(1)}, u32[]{:S(2)}, u32[]{:S(2)}) collective-permute-start(f32[9,2,128,128]{3,2,1,0:T(8,128)S(1)} %collective-permute-done.12.rest_refs_4_), channel_id=1, source_target_pairs={{4,6},{5,7},{12,14},{13,15},{20,22},{21,23},{28,30},{29,31}} | collective-permute-start | bytes 3538952 | tf_op jit(solution)/shard_map/ppermute | solution.py:618
  76.5 23.8 %collective-permute-start.18 = (f32[9,2,128,128]{3,2,1,0:T(8,128)S(1)}, f32[9,2,128,128]{3,2,1,0:T(8,128)S(1)}, u32[]{:S(2)}, u32[]{:S(2)}) collective-permute-start(f32[9,2,128,128]{3,2,1,0:T(8,128)S(1)} %collective-permute-done.13.rest_refs_5_), channel_id=1, source_target_pairs={{2,0},{3,1},{10,8},{11,9},{18,16},{19,17},{26,24},{27,25}} | collective-permute-start | bytes 3538952 | tf_op jit(solution)/shard_map/ppermute | solution.py:618
  77.2 23.9 %collective-permute-start.19 = (f32[9,2,128,128]{3,2,1,0:T(8,128)}, f32[9,2,128,128]{3,2,1,0:T(8,128)S(1)}, u32[]{:S(2)}, u32[]{:S(2)}) collective-permute-start(f32[9,2,128,128]{3,2,1,0:T(8,128)} %select_select_fusion.1), channel_id=1, source_target_pairs={{0,1},{1,0},{2,3},{3,2},{4,5},{5,4},{6,7},{7,6},{8,9},{9,8},{10,11... | collective-permute-start | bytes 3538952 | tf_op jit(solution)/shard_map/ppermute | solution.py:618
  77.5 23.1 %collective-permute-start.20 = (f32[4,2,128,128]{3,2,1,0:T(8,128)}, f32[4,2,128,128]{3,2,1,0:T(8,128)S(1)}, u32[]{:S(2)}, u32[]{:S(2)}) collective-permute-start(f32[4,2,128,128]{3,2,1,0:T(8,128)} %get-tuple-element.83), channel_id=1, source_target_pairs={{2,4},{3,5},{4,2},{5,3},{10,12},{11,13},{12,10},{13,11},{18,20},{1... | collective-permute-start | bytes 1572872 | tf_op jit(solution)/shard_map/ppermute | solution.py:618
  78.2 22.5 %collective-permute-start.21 = (f32[4,2,128,128]{3,2,1,0:T(8,128)}, f32[4,2,128,128]{3,2,1,0:T(8,128)S(1)}, u32[]{:S(2)}, u32[]{:S(2)}) collective-permute-start(f32[4,2,128,128]{3,2,1,0:T(8,128)} %get-tuple-element.91), channel_id=1, source_target_pairs={{0,4},{1,5},{6,2},{7,3},{8,12},{9,13},{14,10},{15,11},{16,20},{17,... | collective-permute-start | bytes 1572872 | tf_op jit(solution)/shard_map/ppermute | solution.py:618
  101.1 37.4 %collective-permute-start.22 = (f32[9,2,128,128]{3,2,1,0:T(8,128)S(1)}, f32[9,2,128,128]{3,2,1,0:T(8,128)S(1)}, u32[]{:S(2)}, u32[]{:S(2)}) collective-permute-start(f32[9,2,128,128]{3,2,1,0:T(8,128)S(1)} %select_select_fusion), channel_id=1, source_target_pairs={{0,1},{1,0},{2,3},{3,2},{4,5},{5,4},{6,7},{7,6},{8,9},{9,8},{10,11... | collective-permute-start | bytes 3538952 | tf_op jit(solution)/shard_map/ppermute | solution.py:618
  101.3 47.1 %collective-permute-start.24 = (f32[4,2,128,128]{3,2,1,0:T(8,128)}, f32[4,2,128,128]{3,2,1,0:T(8,128)S(1)}, u32[]{:S(2)}, u32[]{:S(2)}) collective-permute-start(f32[4,2,128,128]{3,2,1,0:T(8,128)} %get-tuple-element.82), channel_id=1, source_target_pairs={{0,7},{1,6},{2,5},{3,4},{4,3},{5,2},{8,15},{9,14},{10,13},{11,12},... | collective-permute-start | bytes 1572872 | tf_op jit(solution)/shard_map/ppermute | solution.py:618
  102.6 45.8 %collective-permute-start.25 = (f32[4,2,128,128]{3,2,1,0:T(8,128)}, f32[4,2,128,128]{3,2,1,0:T(8,128)S(1)}, u32[]{:S(2)}, u32[]{:S(2)}) collective-permute-start(f32[4,2,128,128]{3,2,1,0:T(8,128)} %get-tuple-element.83), channel_id=1, source_target_pairs={{0,6},{1,7},{8,14},{9,15},{16,22},{17,23},{24,30},{25,31}} | collective-permute-start | bytes 1572872 | tf_op jit(solution)/shard_map/ppermute | solution.py:618
  103.9 44.6 %collective-permute-start.26 = (f32[4,2,128,128]{3,2,1,0:T(8,128)}, f32[4,2,128,128]{3,2,1,0:T(8,128)}, u32[]{:S(2)}, u32[]{:S(2)}) collective-permute-start(f32[4,2,128,128]{3,2,1,0:T(8,128)} %get-tuple-element.84), channel_id=1, source_target_pairs={{0,2},{1,3},{4,6},{5,7},{6,4},{7,5},{8,10},{9,11},{12,14},{13,15},... | collective-permute-start | bytes 1572872 | tf_op jit(solution)/shard_map/ppermute | solution.py:618
  110.7 82.3 %copy-start.18 = (s32[1,32]{1,0:T(1,128)S(1)}, s32[1,32]{1,0:T(1,128)}, u32[]{:S(2)}) copy-start(s32[1,32]{1,0:T(1,128)} %param.7) | copy-start | bytes 388
  144.5 15.3 %collective-permute-start.23 = (f32[4,128,128]{2,1,0:T(8,128)S(1)}, f32[4,128,128]{2,1,0:T(8,128)S(1)}, u32[]{:S(2)}, u32[]{:S(2)}) collective-permute-start(f32[4,128,128]{2,1,0:T(8,128)S(1)} %get-tuple-element.81), channel_id=1, source_target_pairs={{0,8},{8,0},{16,24},{24,16},{1,9},{9,1},{17,25},{25,17},{2,10},{10... | collective-permute-start | bytes 786440 | tf_op jit(solution)/shard_map/ppermute | solution.py:256
  148.5 28.7 %collective-permute-start.28 = (f32[4,2,128,128]{3,2,1,0:T(8,128)}, f32[4,2,128,128]{3,2,1,0:T(8,128)S(1)}, u32[]{:S(2)}, u32[]{:S(2)}) collective-permute-start(f32[4,2,128,128]{3,2,1,0:T(8,128)} %get-tuple-element.90), channel_id=1, source_target_pairs={{0,5},{1,4},{2,7},{3,6},{6,3},{7,2},{8,13},{9,12},{10,15},{11,14},... | collective-permute-start | bytes 1572872 | tf_op jit(solution)/shard_map/ppermute | solution.py:618
  153.5 35.0 %collective-permute-start.29 = (f32[4,2,128,128]{3,2,1,0:T(8,128)}, f32[4,2,128,128]{3,2,1,0:T(8,128)S(1)}, u32[]{:S(2)}, u32[]{:S(2)}) collective-permute-start(f32[4,2,128,128]{3,2,1,0:T(8,128)} %get-tuple-element.91), channel_id=1, source_target_pairs={{2,6},{3,7},{10,14},{11,15},{18,22},{19,23},{26,30},{27,31}} | collective-permute-start | bytes 1572872 | tf_op jit(solution)/shard_map/ppermute | solution.py:618
  154.8 36.7 %collective-permute-start.30 = (f32[4,2,128,128]{3,2,1,0:T(8,128)}, f32[4,2,128,128]{3,2,1,0:T(8,128)S(1)}, u32[]{:S(2)}, u32[]{:S(2)}) collective-permute-start(f32[4,2,128,128]{3,2,1,0:T(8,128)} %get-tuple-element.92), channel_id=1, source_target_pairs={{0,3},{1,2},{4,7},{5,6},{6,5},{7,4},{8,11},{9,10},{12,15},{13,14},... | collective-permute-start | bytes 1572872 | tf_op jit(solution)/shard_map/ppermute | solution.py:618
  156.7 34.7 %collective-permute-start.31 = (f32[4,2,128,128]{3,2,1,0:T(8,128)}, f32[4,2,128,128]{3,2,1,0:T(8,128)S(1)}, u32[]{:S(2)}, u32[]{:S(2)}) collective-permute-start(f32[4,2,128,128]{3,2,1,0:T(8,128)} %get-tuple-element.93), channel_id=1, source_target_pairs={{2,3},{3,2},{4,5},{5,4},{6,7},{7,6},{10,11},{11,10},{12,13},{13,12... | collective-permute-start | bytes 1572872 | tf_op jit(solution)/shard_map/ppermute | solution.py:618
  160.0 7.3 %collective-permute-start.27 = (f32[4,128,128]{2,1,0:T(8,128)S(1)}, f32[4,128,128]{2,1,0:T(8,128)S(1)}, u32[]{:S(2)}, u32[]{:S(2)}) collective-permute-start(f32[4,128,128]{2,1,0:T(8,128)S(1)} %get-tuple-element.85), channel_id=1, source_target_pairs={{0,16},{8,24},{16,0},{24,8},{1,17},{9,25},{17,1},{25,9},{2,18},{10... | collective-permute-start | bytes 786440 | tf_op jit(solution)/shard_map/ppermute | solution.py:256
  198.2 2.3 %collective-permute-start.32 = (f32[4,128,128]{2,1,0:T(8,128)S(1)}, f32[4,128,128]{2,1,0:T(8,128)S(1)}, u32[]{:S(2)}, u32[]{:S(2)}) collective-permute-start(f32[4,128,128]{2,1,0:T(8,128)S(1)} %get-tuple-element.96), channel_id=1, source_target_pairs={{0,8},{8,0},{16,24},{24,16},{1,9},{9,1},{17,25},{25,17},{2,10},{10... | collective-permute-start | bytes 786440 | tf_op jit(solution)/shard_map/ppermute | solution.py:256
  199.4 1.6 collective-permute-start.34
  199.5 1.9 collective-permute-start.35
  200.6 10.0 %collective-permute-start.33 = (f32[4,128,128]{2,1,0:T(8,128)S(1)}, f32[4,128,128]{2,1,0:T(8,128)S(1)}, u32[]{:S(2)}, u32[]{:S(2)}) collective-permute-start(f32[4,128,128]{2,1,0:T(8,128)S(1)} %get-tuple-element.107), channel_id=1, source_target_pairs={{0,16},{8,24},{16,0},{24,8},{1,17},{9,25},{17,1},{25,9},{2,18},{10... | collective-permute-start | bytes 786440 | tf_op jit(solution)/shard_map/ppermute | solution.py:256
  210.7 1.6 collective-permute-start.36
  210.9 1.7 collective-permute-start.37
  (23 other events, 683.3 us)

commit v6 on v5

--- a/solution.py
+++ b/solution.py
@@ -54,23 +54,27 @@
     meta[first + excess_max] = pos[first + excess_max + cols_n]
 
 
-def pack(tiles, ids, me, cols_n, base, excess_max):
+def pack(tiles, ids, me, cols_n, base, excess_max, streams):
     slots = tiles.shape[0]
     count = LINES * base + 1
     first = cols_n * base
 
-    def kernel(ids_ref, me_ref, tiles_ref, stream_ref, *rest):
-        outs, (meta, held, pos, sems) = rest[: cols_n - 1], rest[cols_n - 1 :]
+    n_out = 1 if streams else cols_n - 1
+
+    def kernel(ids_ref, me_ref, tiles_ref, *rest):
+        outs, (meta, held, pos, sems) = rest[:n_out], rest[n_out:]
         list_slots(ids_ref, pos, meta, slots, cols_n, base, excess_max)
         moves = []
-        for n in range(count):
+        for n in range(count if streams else 0):
             at = n if n < LINES * base else first
-            moves.append((meta[at] >= 0, pos[at], stream_ref.at[n]))
-        for k in range(1, cols_n):
+            moves.append((meta[at] >= 0, pos[at], outs[0].at[n]))
+        for k in range(1, 1 if streams else cols_n):
             owner = me_ref[0] ^ k
             for r in range(base):
                 at = owner * base + r
                 moves.append(((meta[at] >= 0) & (owner >= LINES), pos[at], outs[k - 1].at[r]))
+        if streams:
+            held = outs[0]
         for n, (cond, slot, _) in enumerate(moves):
 
             @pl.when(cond)
@@ -82,32 +86,34 @@
             @pl.when(cond)
             def _(n=n, slot=slot, dst=dst):
                 pltpu.make_async_copy(tiles_ref.at[slot], held.at[n], sems.at[0, n]).wait()
-                pltpu.make_async_copy(held.at[n], dst, sems.at[1, n]).start()
-
-        for n, (cond, _, dst) in enumerate(moves):
+                if not streams:
+                    pltpu.make_async_copy(held.at[n], dst, sems.at[1, n]).start()
+
+        for n, (cond, _, dst) in enumerate([] if streams else moves):
 
             @pl.when(cond)
             def _(n=n, dst=dst):
                 pltpu.make_async_copy(held.at[n], dst, sems.at[1, n]).wait()
 
     one = tiles.shape[1:]
-    total = count + (cols_n - 1) * base
+    total = count if streams else (cols_n - 1) * base
     got = call(
         kernel,
         8,
-        out_shape=(pltpu.HBM((count,) + one, F32),)
-        + tuple(pltpu.HBM((base,) + one, F32) for _ in range(1, cols_n))
+        out_shape=tuple(
+            pltpu.VMEM((count,) + one, F32) if streams else pltpu.HBM((base,) + one, F32) for _ in range(n_out)
+        )
         + (jax.ShapeDtypeStruct((META,), jnp.int32),),
         in_specs=[SMEM, SMEM, HBM],
-        out_specs=tuple(HBM for _ in range(cols_n)) + (SMEM,),
+        out_specs=tuple(VMEM if streams else HBM for _ in range(n_out)) + (SMEM,),
         scratch_shapes=[
             pltpu.VMEM((total,) + one, F32),
             pltpu.SMEM((first + excess_max + cols_n + 1,), jnp.int32),
             pltpu.SemaphoreType.DMA((2, total)),
         ],
-        name="pack",
+        name="pack_streams" if streams else "pack_shifts",
     )(ids, me, tiles)
-    return got[0], got[1:-1], got[-1]
+    return got[:-1], got[-1]
 
 
 def unwritten(shape):
@@ -378,7 +384,7 @@
                 )
                 for m in range(CBLK)
             ]
-            at = pl.ds(pl.multiple_of(g * (group * block), group * block), group * block)
+            at = pl.ds(g * (group * block), group * block)
             l0h, l0l = split(dot3(*split(x[0]), i0h[...], i0l[...]))
             high_ref[at, : 2 * block] = l0h
             low_ref[at, : 2 * block] = l0l
@@ -388,7 +394,8 @@
             low_ref[at, 2 * block :] = l1l
             return carry
 
-        lax.fori_loop(0, row_tiles // group, one, 0)
+        for g in range(row_tiles // group):
+            one(g, 0)
 
     wide = pltpu.VMEM((2 * block, 2 * block), BF16)
     return call(
@@ -571,7 +578,11 @@
                 pairs.append((i, i ^ k))
         return pairs
 
-    packed, shifted, meta = pack(tiles, ids, me, cols_n, base, excess_max)
+    def after(values, earlier):
+        return lax.optimization_barrier((tuple(values), tuple(earlier)))[0]
+
+    (packed,), meta = pack(tiles, ids, me, cols_n, base, excess_max, True)
+    shifted, _ = pack(tiles, after([ids], [packed])[0], me, cols_n, base, excess_max, False)
     parts, origins = [packed], [(0, False)]
     chunk = {("up", 0): packed, ("down", 0): packed}
     arrived, arrived_from = [], []

time: 224 us -> 220 us (0.982)
  waiting for transfers between devices: 123 us -> 113 us
  other arithmetic: 6.26 us -> 9.36 us
    ppermute x3, waiting for transfers between devices: 39.4 us -> 31.7 us  [per_device(): got = lax.ppermute(near, 'pcol', [(i, i ^ step) for i in range(cols_n)])]
    pallas_call x1 -> x2, Pallas kernels: 6.18 us -> 8.13 us  [pack(): call(kernel, 8, out_shape=tuple((pltpu.VMEM((count,) + one, F32) if strea...]
  transfers between devices with their start and end apart: 31 -> 31, of which waited for: 16 -> 16; matrix products, arithmetic and copies ran while one was open for 2% -> 4% of each run, Pallas kernels for 6% -> 8%
where the time goes in v6:
time: 220 us; the launch traced here: 219 us
  waiting for transfers between devices  113 us (51%)
  starting transfers between devices  55.7 us (25%)
  Pallas kernels  36.5 us (17%)
  other arithmetic  9.36 us (4%)
  local copies, waits for them, and re-layouts  2.65 us (1%)
    ppermute x20, waiting for transfers between devices, per_device(): done = [lax.ppermute(x, 'pcol', w[1]) for x, w in zip(values, work)]  72 us
    ppermute x20, starting transfers between devices, per_device(): done = [lax.ppermute(x, 'pcol', w[1]) for x, w in zip(values, work)]  42.2 us
    ppermute x3, waiting for transfers between devices, per_device(): got = lax.ppermute(near, 'pcol', [(i, i ^ step) for i in range(cols_n)])  31.7 us
    pallas_call x2, Pallas kernels, extract(): call(kernel, 12, out_shape=(pltpu.HBM((tiles_n, 2, block, block), F32), p...  10.2 us
    pallas_call x1, Pallas kernels, update(): call(kernel, 24, out_shape=jax.ShapeDtypeStruct((2, rows, CBLK * block),...  10 us
    ppermute x8, waiting for transfers between devices, cross(): return lax.ppermute(x, 'prow', [(p, p ^ step) for p in range(rows_n)])  9.57 us
    pallas_call x1, Pallas kernels, panel_factors(): call(kernel, 20, out_shape=(jax.ShapeDtypeStruct((rows, 4 * block), BF16)...  8.14 us
    pallas_call x2, Pallas kernels, pack(): call(kernel, 8, out_shape=tuple((pltpu.VMEM((count,) + one, F32) if strea...  8.13 us
  transfers between devices with their start and end apart: 31, of which 16 were waited for; matrix products, arithmetic and copies ran while one was open for 4% of the time, Pallas kernels for 8%

profile of v6, /device:TPU:29, one launch (start us, length us, event | category | flops | bytes accessed | tf_op | source)
XLA Modules:
  0.0 218.6 jit_solution(12353039934050469106)
XLA Ops:
  0.0 3.3 %pack_streams.1 = (f32[9,2,128,128]{3,2,1,0:T(8,128)S(1)}, s32[128]{0:T(128)}) custom-call(s32[32]{0:T(128)} %bitcast.24, s32[1]{0:T(128)} %bitcast.11.me_ref.col_ref, f32[32,2,128,128]{3,2,1,0:T(8,128)} %bitcast.20), custom_call_target="tpu_custom_call" | custom-call | tf_op jit(solution)/shard_map/pack_streams/pallas_call | solution.py:100
  3.3 2.2 %collective-permute-start.9 = (f32[9,2,128,128]{3,2,1,0:T(8,128)S(1)}, f32[9,2,128,128]{3,2,1,0:T(8,128)S(1)}, u32[]{:S(2)}, u32[]{:S(2)}) collective-permute-start(f32[9,2,128,128]{3,2,1,0:T(8,128)S(1)} %get-tuple-element.62.rest_refs_0_), channel_id=1, source_target_pairs={{2,0},{3,1},{4,2},{5,3},{6,4},{7,5},{10,8},{11,9},{12,10},{13,11},... | collective-permute-start | bytes 3538952 | tf_op jit(solution)/shard_map/ppermute | solution.py:629
  6.8 1.3 collective-permute-start.8
  12.6 19.7 %collective-permute-done.7 = s32[1,128]{1,0:T(1,128)} collective-permute-done((s32[1,128]{1,0:T(1,128)}, s32[1,128]{1,0:T(1,128)}, u32[]{:S(2)}, u32[]{:S(2)}) %collective-permute-start.7) | collective-permute-done | bytes 544 | tf_op jit(solution)/shard_map/ppermute | solution.py:643
  32.2 2.8 %collective-permute-done.8.rest_refs_1_ = f32[9,2,128,128]{3,2,1,0:T(8,128)} collective-permute-done((f32[9,2,128,128]{3,2,1,0:T(8,128)S(1)}, f32[9,2,128,128]{3,2,1,0:T(8,128)}, u32[]{:S(2)}, u32[]{:S(2)}) %collective-permute-start.8) | collective-permute-done | bytes 1179680 | tf_op jit(solution)/shard_map/ppermute | solution.py:629
  35.0 1.3 collective-permute-start.12
  37.1 1.7 collective-permute-start.14
  38.8 2.2 collective-permute-start.15
  42.2 3.5 %collective-permute-start.11 = (s32[2,128]{1,0:T(2,128)}, s32[2,128]{1,0:T(2,128)}, u32[]{:S(2)}, u32[]{:S(2)}) collective-permute-start(s32[2,128]{1,0:T(2,128)} %pad_add_fusion.5), channel_id=1, source_target_pairs={{0,2},{1,3},{2,0},{3,1},{4,6},{5,7},{6,4},{7,5},{8,10},{9,11},{10,... | collective-permute-start | bytes 3080 | tf_op jit(solution)/shard_map/ppermute | solution.py:643
  45.7 4.8 %pack_shifts.1 = (f32[4,2,128,128]{3,2,1,0:T(8,128)}, f32[4,2,128,128]{3,2,1,0:T(8,128)}, f32[4,2,128,128]{3,2,1,0:T(8,128)}, f32[4,2,128,128]{3,2,1,0:T(8,128)}...) custom-call(s32[32]{0:T(128)} %bitcast.25, ...), custom_call_target="tpu_custom_call" | custom-call | tf_op jit(solution)/shard_map/pack_shifts/pallas_call | solution.py:100
  50.5 12.0 %collective-permute-done.11 = s32[2,128]{1,0:T(2,128)} collective-permute-done((s32[2,128]{1,0:T(2,128)}, s32[2,128]{1,0:T(2,128)}, u32[]{:S(2)}, u32[]{:S(2)}) %collective-permute-start.11) | collective-permute-done | bytes 1056 | tf_op jit(solution)/shard_map/ppermute | solution.py:643
  63.3 3.0 %collective-permute-done.15.rest_refs_7_ = f32[9,2,128,128]{3,2,1,0:T(8,128)} collective-permute-done((f32[9,2,128,128]{3,2,1,0:T(8,128)}, f32[9,2,128,128]{3,2,1,0:T(8,128)}, u32[]{:S(2)}, u32[]{:S(2)}) %collective-permute-start.15) | collective-permute-done | bytes 1179680 | tf_op jit(solution)/shard_map/ppermute | solution.py:629
  66.3 2.9 %collective-permute-start.16 = (s32[4,128]{1,0:T(4,128)S(1)}, s32[4,128]{1,0:T(4,128)S(1)}, u32[]{:S(2)}, u32[]{:S(2)}) collective-permute-start(s32[4,128]{1,0:T(4,128)S(1)} %pad_add_fusion.1), channel_id=1, source_target_pairs={{0,4},{1,5},{2,6},{3,7},{4,0},{5,1},{6,2},{7,3},{8,12},{9,13},{10,... | collective-permute-start | bytes 6152 | tf_op jit(solution)/shard_map/ppermute | solution.py:643
  71.7 1.3 collective-permute-start.17
  74.8 6.6 %collective-permute-start.21 = (f32[4,2,128,128]{3,2,1,0:T(8,128)}, f32[4,2,128,128]{3,2,1,0:T(8,128)S(1)}, u32[]{:S(2)}, u32[]{:S(2)}) collective-permute-start(f32[4,2,128,128]{3,2,1,0:T(8,128)} %get-tuple-element.93), channel_id=1, source_target_pairs={{0,4},{1,5},{6,2},{7,3},{8,12},{9,13},{14,10},{15,11},{16,20},{17,... | collective-permute-start | bytes 1572872 | tf_op jit(solution)/shard_map/ppermute | solution.py:629
  81.4 15.2 %collective-permute-done.17.rest_refs_8_ = f32[9,2,128,128]{3,2,1,0:T(8,128)S(1)} collective-permute-done((f32[9,2,128,128]{3,2,1,0:T(8,128)S(1)}, f32[9,2,128,128]{3,2,1,0:T(8,128)S(1)}, u32[]{:S(2)}, u32[]{:S(2)}) %collective-permute-start.17) | collective-permute-done | bytes 1179680 | tf_op jit(solution)/shard_map/ppermute | solution.py:629
  99.2 1.3 collective-permute-start.25
  100.5 7.6 %collective-permute-start.26 = (f32[4,2,128,128]{3,2,1,0:T(8,128)}, f32[4,2,128,128]{3,2,1,0:T(8,128)}, u32[]{:S(2)}, u32[]{:S(2)}) collective-permute-start(f32[4,2,128,128]{3,2,1,0:T(8,128)} %get-tuple-element.86), channel_id=1, source_target_pairs={{0,2},{1,3},{4,6},{5,7},{6,4},{7,5},{8,10},{9,11},{12,14},{13,15},... | collective-permute-start | bytes 1572872 | tf_op jit(solution)/shard_map/ppermute | solution.py:629
  108.1 26.9 %collective-permute-done.22.rest_refs_11_ = f32[9,2,128,128]{3,2,1,0:T(8,128)S(1)} collective-permute-done((f32[9,2,128,128]{3,2,1,0:T(8,128)S(1)}, f32[9,2,128,128]{3,2,1,0:T(8,128)S(1)}, u32[]{:S(2)}, u32[]{:S(2)}) %collective-permute-start.22) | collective-permute-done | bytes 1179680 | tf_op jit(solution)/shard_map/ppermute | solution.py:629
  136.0 4.9 %panel_rows.1 = (f32[32,2,128,128]{3,2,1,0:T(8,128)}, f32[4,128,128]{2,1,0:T(8,128)S(1)}, f32[4,128,128]{2,1,0:T(8,128)S(1)}, f32[4,128,128]{2,1,0:T(8,128)S(1)}) custom-call(s32[8,128]{1,0:T(8,128)S(1)} %pad_add_fusion.near_ref, s32[32]{0:T(128)S(1)} %bitcast.27, s32[256]{0:T(256)S(1)} %get-tuple-element.88.rows_ref, s32[1]{0:T(128)} %bitcast.11.me_ref.col_ref, ...), custom_call_target="tpu_custom_call" | custom-call | tf_op jit(solution)/shard_map/panel_rows/pallas_call | solution.py:245
  141.0 4.0 %collective-permute-start.23 = (f32[4,128,128]{2,1,0:T(8,128)S(1)}, f32[4,128,128]{2,1,0:T(8,128)S(1)}, u32[]{:S(2)}, u32[]{:S(2)}) collective-permute-start(f32[4,128,128]{2,1,0:T(8,128)S(1)} %get-tuple-element.83), channel_id=1, source_target_pairs={{0,8},{8,0},{16,24},{24,16},{1,9},{9,1},{17,25},{25,17},{2,10},{10... | collective-permute-start | bytes 786440 | tf_op jit(solution)/shard_map/ppermute | solution.py:262
  145.0 5.1 %collective-permute-start.28 = (f32[4,2,128,128]{3,2,1,0:T(8,128)}, f32[4,2,128,128]{3,2,1,0:T(8,128)S(1)}, u32[]{:S(2)}, u32[]{:S(2)}) collective-permute-start(f32[4,2,128,128]{3,2,1,0:T(8,128)} %get-tuple-element.92), channel_id=1, source_target_pairs={{0,5},{1,4},{2,7},{3,6},{6,3},{7,2},{8,13},{9,12},{10,15},{11,14},... | collective-permute-start | bytes 1572872 | tf_op jit(solution)/shard_map/ppermute | solution.py:629
  150.1 1.3 collective-permute-start.29
  151.4 1.9 collective-permute-start.30
  153.3 3.0 %collective-permute-start.31 = (f32[4,2,128,128]{3,2,1,0:T(8,128)}, f32[4,2,128,128]{3,2,1,0:T(8,128)S(1)}, u32[]{:S(2)}, u32[]{:S(2)}) collective-permute-start(f32[4,2,128,128]{3,2,1,0:T(8,128)} %get-tuple-element.95), channel_id=1, source_target_pairs={{2,3},{3,2},{4,5},{5,4},{6,7},{7,6},{10,11},{11,10},{12,13},{13,12... | collective-permute-start | bytes 1572872 | tf_op jit(solution)/shard_map/ppermute | solution.py:629
  157.4 7.0 %collective-permute-done.27 = f32[4,128,128]{2,1,0:T(8,128)S(1)} collective-permute-done((f32[4,128,128]{2,1,0:T(8,128)S(1)}, f32[4,128,128]{2,1,0:T(8,128)S(1)}, u32[]{:S(2)}, u32[]{:S(2)}) %collective-permute-start.27) | collective-permute-done | bytes 262176 | tf_op jit(solution)/shard_map/ppermute | solution.py:262
  164.5 9.2 %collective-permute-done.28.rest_refs_19_ = f32[4,2,128,128]{3,2,1,0:T(8,128)S(1)} collective-permute-done((f32[4,2,128,128]{3,2,1,0:T(8,128)}, f32[4,2,128,128]{3,2,1,0:T(8,128)S(1)}, u32[]{:S(2)}, u32[]{:S(2)}) %collective-permute-start.28) | collective-permute-done | bytes 524320 | tf_op jit(solution)/shard_map/ppermute | solution.py:629
  173.7 11.3 %collective-permute-done.29.rest_refs_20_ = f32[4,2,128,128]{3,2,1,0:T(8,128)S(1)} collective-permute-done((f32[4,2,128,128]{3,2,1,0:T(8,128)}, f32[4,2,128,128]{3,2,1,0:T(8,128)S(1)}, u32[]{:S(2)}, u32[]{:S(2)}) %collective-permute-start.29) | collective-permute-done | bytes 524320 | tf_op jit(solution)/shard_map/ppermute | solution.py:629
  185.0 3.0 %collective-permute-done.30.rest_refs_21_ = f32[4,2,128,128]{3,2,1,0:T(8,128)S(1)} collective-permute-done((f32[4,2,128,128]{3,2,1,0:T(8,128)}, f32[4,2,128,128]{3,2,1,0:T(8,128)S(1)}, u32[]{:S(2)}, u32[]{:S(2)}) %collective-permute-start.30) | collective-permute-done | bytes 524320 | tf_op jit(solution)/shard_map/ppermute | solution.py:629
  189.6 5.2 %own_rows.1 = (f32[32,2,128,128]{3,2,1,0:T(8,128)}, f32[4,128,128]{2,1,0:T(8,128)S(1)}, f32[4,128,128]{2,1,0:T(8,128)S(1)}, f32[4,128,128]{2,1,0:T(8,128)S(1)}) custom-call(s32[8,128]{1,0:T(8,128)S(1)} %pad_add_fusion.near_ref, s32[32]{0:T(128)} %bitcast.26, s32[256]{0:T(256)S(1)} %get-tuple-element.88.rows_ref, s32[1]{0:T(128)} %bitcast.11.me_ref.col_ref, ...), custom_call_target="tpu_custom_call" | custom-call | tf_op jit(solution)/shard_map/own_rows/pallas_call | solution.py:245
  198.1 8.1 %panel_factors.1 = (bf16[2048,512]{1,0:T(8,128)(2,1)S(1)}, bf16[2048,512]{1,0:T(8,128)(2,1)S(1)}, f32[128,256]{1,0:T(8,128)S(1)}) custom-call(s32[256]{0:T(256)S(1)} %get-tuple-element.132.tgt, s32[129]{0:T(256)S(1)} %pad_add_fusion.4.chain_ref, s32[1]{0:T(128)} %bitcast.10.row_ref, f32[32,2,128,128]{3,2,1,0:T(8,128)} %get-tuple-element.100.held_in, ...), custom_call_target="tpu_custom_call" | custom-call | tf_op jit(solution)/shard_map/panel_factors/pallas_call | solution.py:401
  208.4 10.0 %update.1 = f32[2,2048,256]{2,1,0:T(8,128)} custom-call(s32[256]{0:T(256)S(1)} %get-tuple-element.132.tgt, s32[129]{0:T(256)S(1)} %pad_add_fusion.4.chain_ref, s32[1]{0:T(128)} %bitcast.10.row_ref, s32[1]{0:T(128)} %bitcast.11.me_ref.col_ref, f32[32,2,128,128]{3,2,1,0:T(8,128)} %get-tuple-element.96.held_in, f32[4,128,128]{2,1,0:T(8,128)S(1)} %get-tuple-element.123.new_a, ...), custom_call_target="tpu_custom_call" | custom-call | tf_op jit(solution)/shard_map/update/pallas_call | solution.py:491
  (98 shorter events, 23.7 us)
Async XLA Ops:
  3.3 67.0 %copy-start = (f32[9,2,128,128]{3,2,1,0:T(8,128)}, f32[9,2,128,128]{3,2,1,0:T(8,128)S(1)}, u32[]{:S(2)}) copy-start(f32[9,2,128,128]{3,2,1,0:T(8,128)S(1)} %get-tuple-element.62.rest_refs_0_) | copy-start | bytes 3538948
  3.3 28.9 %collective-permute-start.9 = (f32[9,2,128,128]{3,2,1,0:T(8,128)S(1)}, f32[9,2,128,128]{3,2,1,0:T(8,128)S(1)}, u32[]{:S(2)}, u32[]{:S(2)}) collective-permute-start(f32[9,2,128,128]{3,2,1,0:T(8,128)S(1)} %get-tuple-element.62.rest_refs_0_), channel_id=1, source_target_pairs={{2,0},{3,1},{4,2},{5,3},{6,4},{7,5},{10,8},{11,9},{12,10},{13,11},... | collective-permute-start | bytes 3538952 | tf_op jit(solution)/shard_map/ppermute | solution.py:629
  5.5 26.7 %collective-permute-start.10 = (f32[9,2,128,128]{3,2,1,0:T(8,128)S(1)}, f32[9,2,128,128]{3,2,1,0:T(8,128)S(1)}, u32[]{:S(2)}, u32[]{:S(2)}) collective-permute-start(f32[9,2,128,128]{3,2,1,0:T(8,128)S(1)} %get-tuple-element.62.rest_refs_0_), channel_id=1, source_target_pairs={{0,1},{1,0},{2,3},{3,2},{4,5},{5,4},{6,7},{7,6},{8,9},{9,8},{10,11... | collective-permute-start | bytes 3538952 | tf_op jit(solution)/shard_map/ppermute | solution.py:629
  6.8 28.2 %collective-permute-start.8 = (f32[9,2,128,128]{3,2,1,0:T(8,128)S(1)}, f32[9,2,128,128]{3,2,1,0:T(8,128)}, u32[]{:S(2)}, u32[]{:S(2)}) collective-permute-start(f32[9,2,128,128]{3,2,1,0:T(8,128)S(1)} %get-tuple-element.62.rest_refs_0_), channel_id=1, source_target_pairs={{0,2},{1,3},{2,4},{3,5},{4,6},{5,7},{8,10},{9,11},{10,12},{11,13},... | collective-permute-start | bytes 3538952 | tf_op jit(solution)/shard_map/ppermute | solution.py:629
  8.1 24.1 %collective-permute-start.7 = (s32[1,128]{1,0:T(1,128)}, s32[1,128]{1,0:T(1,128)}, u32[]{:S(2)}, u32[]{:S(2)}) collective-permute-start(s32[1,128]{1,0:T(1,128)} %bitcast.14), channel_id=1, source_target_pairs={{0,1},{1,0},{2,3},{3,2},{4,5},{5,4},{6,7},{7,6},{8,9},{9,8},{10,11... | collective-permute-start | bytes 1544 | tf_op jit(solution)/shard_map/ppermute | solution.py:643
  35.0 28.2 %collective-permute-start.12 = (f32[9,2,128,128]{3,2,1,0:T(8,128)}, f32[9,2,128,128]{3,2,1,0:T(8,128)S(1)}, u32[]{:S(2)}, u32[]{:S(2)}) collective-permute-start(f32[9,2,128,128]{3,2,1,0:T(8,128)} %collective-permute-done.8.rest_refs_1_), channel_id=1, source_target_pairs={{2,4},{3,5},{4,6},{5,7},{10,12},{11,13},{12,14},{13,15},{18,20},{1... | collective-permute-start | bytes 3538952 | tf_op jit(solution)/shard_map/ppermute | solution.py:629
  36.3 26.9 %collective-permute-start.13 = (f32[9,2,128,128]{3,2,1,0:T(8,128)}, f32[9,2,128,128]{3,2,1,0:T(8,128)S(1)}, u32[]{:S(2)}, u32[]{:S(2)}) collective-permute-start(f32[9,2,128,128]{3,2,1,0:T(8,128)} %copy-done.4), channel_id=1, source_target_pairs={{2,0},{3,1},{4,2},{5,3},{10,8},{11,9},{12,10},{13,11},{18,16},{19,... | collective-permute-start | bytes 3538952 | tf_op jit(solution)/shard_map/ppermute | solution.py:629
  37.1 26.2 %collective-permute-start.14 = (f32[9,2,128,128]{3,2,1,0:T(8,128)}, f32[9,2,128,128]{3,2,1,0:T(8,128)}, u32[]{:S(2)}, u32[]{:S(2)}) collective-permute-start(f32[9,2,128,128]{3,2,1,0:T(8,128)} %copy-done.4), channel_id=1, source_target_pairs={{0,1},{1,0},{8,9},{9,8},{16,17},{17,16},{24,25},{25,24}} | collective-permute-start | bytes 3538952 | tf_op jit(solution)/shard_map/ppermute | solution.py:629
  38.8 27.5 %collective-permute-start.15 = (f32[9,2,128,128]{3,2,1,0:T(8,128)}, f32[9,2,128,128]{3,2,1,0:T(8,128)}, u32[]{:S(2)}, u32[]{:S(2)}) collective-permute-start(f32[9,2,128,128]{3,2,1,0:T(8,128)} %collective-permute-done.8.rest_refs_1_), channel_id=1, source_target_pairs={{2,3},{3,2},{4,5},{5,4},{6,7},{7,6},{10,11},{11,10},{12,13},{13,12... | collective-permute-start | bytes 3538952 | tf_op jit(solution)/shard_map/ppermute | solution.py:629
  42.2 20.4 %collective-permute-start.11 = (s32[2,128]{1,0:T(2,128)}, s32[2,128]{1,0:T(2,128)}, u32[]{:S(2)}, u32[]{:S(2)}) collective-permute-start(s32[2,128]{1,0:T(2,128)} %pad_add_fusion.5), channel_id=1, source_target_pairs={{0,2},{1,3},{2,0},{3,1},{4,6},{5,7},{6,4},{7,5},{8,10},{9,11},{10,... | collective-permute-start | bytes 3080 | tf_op jit(solution)/shard_map/ppermute | solution.py:643
  66.3 4.1 %collective-permute-start.16 = (s32[4,128]{1,0:T(4,128)S(1)}, s32[4,128]{1,0:T(4,128)S(1)}, u32[]{:S(2)}, u32[]{:S(2)}) collective-permute-start(s32[4,128]{1,0:T(4,128)S(1)} %pad_add_fusion.1), channel_id=1, source_target_pairs={{0,4},{1,5},{2,6},{3,7},{4,0},{5,1},{6,2},{7,3},{8,12},{9,13},{10,... | collective-permute-start | bytes 6152 | tf_op jit(solution)/shard_map/ppermute | solution.py:643
  71.7 24.9 %collective-permute-start.17 = (f32[9,2,128,128]{3,2,1,0:T(8,128)S(1)}, f32[9,2,128,128]{3,2,1,0:T(8,128)S(1)}, u32[]{:S(2)}, u32[]{:S(2)}) collective-permute-start(f32[9,2,128,128]{3,2,1,0:T(8,128)S(1)} %collective-permute-done.12.rest_refs_4_), channel_id=1, source_target_pairs={{4,6},{5,7},{12,14},{13,15},{20,22},{21,23},{28,30},{29,31}} | collective-permute-start | bytes 3538952 | tf_op jit(solution)/shard_map/ppermute | solution.py:629
  73.0 23.6 %collective-permute-start.18 = (f32[9,2,128,128]{3,2,1,0:T(8,128)S(1)}, f32[9,2,128,128]{3,2,1,0:T(8,128)S(1)}, u32[]{:S(2)}, u32[]{:S(2)}) collective-permute-start(f32[9,2,128,128]{3,2,1,0:T(8,128)S(1)} %collective-permute-done.13.rest_refs_5_), channel_id=1, source_target_pairs={{2,0},{3,1},{10,8},{11,9},{18,16},{19,17},{26,24},{27,25}} | collective-permute-start | bytes 3538952 | tf_op jit(solution)/shard_map/ppermute | solution.py:629
  73.7 23.8 %collective-permute-start.19 = (f32[9,2,128,128]{3,2,1,0:T(8,128)}, f32[9,2,128,128]{3,2,1,0:T(8,128)S(1)}, u32[]{:S(2)}, u32[]{:S(2)}) collective-permute-start(f32[9,2,128,128]{3,2,1,0:T(8,128)} %select_select_fusion.1), channel_id=1, source_target_pairs={{0,1},{1,0},{2,3},{3,2},{4,5},{5,4},{6,7},{7,6},{8,9},{9,8},{10,11... | collective-permute-start | bytes 3538952 | tf_op jit(solution)/shard_map/ppermute | solution.py:629
  74.1 22.8 %collective-permute-start.20 = (f32[4,2,128,128]{3,2,1,0:T(8,128)}, f32[4,2,128,128]{3,2,1,0:T(8,128)S(1)}, u32[]{:S(2)}, u32[]{:S(2)}) collective-permute-start(f32[4,2,128,128]{3,2,1,0:T(8,128)} %get-tuple-element.85), channel_id=1, source_target_pairs={{2,4},{3,5},{4,2},{5,3},{10,12},{11,13},{12,10},{13,11},{18,20},{1... | collective-permute-start | bytes 1572872 | tf_op jit(solution)/shard_map/ppermute | solution.py:629
  74.8 22.2 %collective-permute-start.21 = (f32[4,2,128,128]{3,2,1,0:T(8,128)}, f32[4,2,128,128]{3,2,1,0:T(8,128)S(1)}, u32[]{:S(2)}, u32[]{:S(2)}) collective-permute-start(f32[4,2,128,128]{3,2,1,0:T(8,128)} %get-tuple-element.93), channel_id=1, source_target_pairs={{0,4},{1,5},{6,2},{7,3},{8,12},{9,13},{14,10},{15,11},{16,20},{17,... | collective-permute-start | bytes 1572872 | tf_op jit(solution)/shard_map/ppermute | solution.py:629
  97.5 37.5 %collective-permute-start.22 = (f32[9,2,128,128]{3,2,1,0:T(8,128)S(1)}, f32[9,2,128,128]{3,2,1,0:T(8,128)S(1)}, u32[]{:S(2)}, u32[]{:S(2)}) collective-permute-start(f32[9,2,128,128]{3,2,1,0:T(8,128)S(1)} %select_select_fusion), channel_id=1, source_target_pairs={{0,1},{1,0},{2,3},{3,2},{4,5},{5,4},{6,7},{7,6},{8,9},{9,8},{10,11... | collective-permute-start | bytes 3538952 | tf_op jit(solution)/shard_map/ppermute | solution.py:629
  97.9 47.1 %collective-permute-start.24 = (f32[4,2,128,128]{3,2,1,0:T(8,128)}, f32[4,2,128,128]{3,2,1,0:T(8,128)}, u32[]{:S(2)}, u32[]{:S(2)}) collective-permute-start(f32[4,2,128,128]{3,2,1,0:T(8,128)} %get-tuple-element.84), channel_id=1, source_target_pairs={{0,7},{1,6},{2,5},{3,4},{4,3},{5,2},{8,15},{9,14},{10,13},{11,12},... | collective-permute-start | bytes 1572872 | tf_op jit(solution)/shard_map/ppermute | solution.py:629
  99.2 45.8 %collective-permute-start.25 = (f32[4,2,128,128]{3,2,1,0:T(8,128)}, f32[4,2,128,128]{3,2,1,0:T(8,128)}, u32[]{:S(2)}, u32[]{:S(2)}) collective-permute-start(f32[4,2,128,128]{3,2,1,0:T(8,128)} %get-tuple-element.85), channel_id=1, source_target_pairs={{0,6},{1,7},{8,14},{9,15},{16,22},{17,23},{24,30},{25,31}} | collective-permute-start | bytes 1572872 | tf_op jit(solution)/shard_map/ppermute | solution.py:629
  100.5 44.5 %collective-permute-start.26 = (f32[4,2,128,128]{3,2,1,0:T(8,128)}, f32[4,2,128,128]{3,2,1,0:T(8,128)}, u32[]{:S(2)}, u32[]{:S(2)}) collective-permute-start(f32[4,2,128,128]{3,2,1,0:T(8,128)} %get-tuple-element.86), channel_id=1, source_target_pairs={{0,2},{1,3},{4,6},{5,7},{6,4},{7,5},{8,10},{9,11},{12,14},{13,15},... | collective-permute-start | bytes 1572872 | tf_op jit(solution)/shard_map/ppermute | solution.py:629
  141.0 16.0 %collective-permute-start.23 = (f32[4,128,128]{2,1,0:T(8,128)S(1)}, f32[4,128,128]{2,1,0:T(8,128)S(1)}, u32[]{:S(2)}, u32[]{:S(2)}) collective-permute-start(f32[4,128,128]{2,1,0:T(8,128)S(1)} %get-tuple-element.83), channel_id=1, source_target_pairs={{0,8},{8,0},{16,24},{24,16},{1,9},{9,1},{17,25},{25,17},{2,10},{10... | collective-permute-start | bytes 786440 | tf_op jit(solution)/shard_map/ppermute | solution.py:262
  145.0 28.7 %collective-permute-start.28 = (f32[4,2,128,128]{3,2,1,0:T(8,128)}, f32[4,2,128,128]{3,2,1,0:T(8,128)S(1)}, u32[]{:S(2)}, u32[]{:S(2)}) collective-permute-start(f32[4,2,128,128]{3,2,1,0:T(8,128)} %get-tuple-element.92), channel_id=1, source_target_pairs={{0,5},{1,4},{2,7},{3,6},{6,3},{7,2},{8,13},{9,12},{10,15},{11,14},... | collective-permute-start | bytes 1572872 | tf_op jit(solution)/shard_map/ppermute | solution.py:629
  150.1 34.9 %collective-permute-start.29 = (f32[4,2,128,128]{3,2,1,0:T(8,128)}, f32[4,2,128,128]{3,2,1,0:T(8,128)S(1)}, u32[]{:S(2)}, u32[]{:S(2)}) collective-permute-start(f32[4,2,128,128]{3,2,1,0:T(8,128)} %get-tuple-element.93), channel_id=1, source_target_pairs={{2,6},{3,7},{10,14},{11,15},{18,22},{19,23},{26,30},{27,31}} | collective-permute-start | bytes 1572872 | tf_op jit(solution)/shard_map/ppermute | solution.py:629
  151.4 36.7 %collective-permute-start.30 = (f32[4,2,128,128]{3,2,1,0:T(8,128)}, f32[4,2,128,128]{3,2,1,0:T(8,128)S(1)}, u32[]{:S(2)}, u32[]{:S(2)}) collective-permute-start(f32[4,2,128,128]{3,2,1,0:T(8,128)} %get-tuple-element.94), channel_id=1, source_target_pairs={{0,3},{1,2},{4,7},{5,6},{6,5},{7,4},{8,11},{9,10},{12,15},{13,14},... | collective-permute-start | bytes 1572872 | tf_op jit(solution)/shard_map/ppermute | solution.py:629
  153.3 34.7 %collective-permute-start.31 = (f32[4,2,128,128]{3,2,1,0:T(8,128)}, f32[4,2,128,128]{3,2,1,0:T(8,128)S(1)}, u32[]{:S(2)}, u32[]{:S(2)}) collective-permute-start(f32[4,2,128,128]{3,2,1,0:T(8,128)} %get-tuple-element.95), channel_id=1, source_target_pairs={{2,3},{3,2},{4,5},{5,4},{6,7},{7,6},{10,11},{11,10},{12,13},{13,12... | collective-permute-start | bytes 1572872 | tf_op jit(solution)/shard_map/ppermute | solution.py:629
  157.1 7.3 %collective-permute-start.27 = (f32[4,128,128]{2,1,0:T(8,128)S(1)}, f32[4,128,128]{2,1,0:T(8,128)S(1)}, u32[]{:S(2)}, u32[]{:S(2)}) collective-permute-start(f32[4,128,128]{2,1,0:T(8,128)S(1)} %get-tuple-element.87), channel_id=1, source_target_pairs={{0,16},{8,24},{16,0},{24,8},{1,17},{9,25},{17,1},{25,9},{2,18},{10... | collective-permute-start | bytes 786440 | tf_op jit(solution)/shard_map/ppermute | solution.py:262
  194.9 2.4 %collective-permute-start.32 = (f32[4,128,128]{2,1,0:T(8,128)S(1)}, f32[4,128,128]{2,1,0:T(8,128)S(1)}, u32[]{:S(2)}, u32[]{:S(2)}) collective-permute-start(f32[4,128,128]{2,1,0:T(8,128)S(1)} %get-tuple-element.98), channel_id=1, source_target_pairs={{0,8},{8,0},{16,24},{24,16},{1,9},{9,1},{17,25},{25,17},{2,10},{10... | collective-permute-start | bytes 786440 | tf_op jit(solution)/shard_map/ppermute | solution.py:262
  196.2 1.6 collective-permute-start.34
  196.3 1.9 collective-permute-start.35
  197.3 9.0 %collective-permute-start.33 = (f32[4,128,128]{2,1,0:T(8,128)S(1)}, f32[4,128,128]{2,1,0:T(8,128)S(1)}, u32[]{:S(2)}, u32[]{:S(2)}) collective-permute-start(f32[4,128,128]{2,1,0:T(8,128)S(1)} %get-tuple-element.109), channel_id=1, source_target_pairs={{0,16},{8,24},{16,0},{24,8},{1,17},{9,25},{17,1},{25,9},{2,18},{10... | collective-permute-start | bytes 786440 | tf_op jit(solution)/shard_map/ppermute | solution.py:262
  206.4 1.6 collective-permute-start.36
  206.7 1.7 collective-permute-start.37
  (18 other events, 447.4 us)

commit v7 on v6

--- a/solution.py
+++ b/solution.py
@@ -422,15 +422,11 @@
     steps = row_tiles // group
     span = group * block
 
-    def kernel(tgt, chain_ref, row_ref, col_ref, held_in, new_a, new_b, old_a, old_b, high_in, low_in, top_ref, out_ref, *rest):
-        held_ref, new_ref, high_ref, low_ref, res_ref, wh, wl, sem, in_sems, out_sems = rest
+    def kernel(tgt, chain_ref, row_ref, col_ref, held_in, new_a, new_b, old_a, old_b, high_ref, low_ref, top_ref, out_ref, *rest):
+        held_ref, new_ref, res_ref, wh, wl, sem, out_sems = rest
         odd = lax.rem(row_ref[0], 2)
         copy = pltpu.make_async_copy(held_in, held_ref.at[: CBLK * row_tiles], sem)
         copy.start()
-        for g in range(steps):
-            at = pl.ds(g * span, span)
-            for n, (src, dst) in enumerate(((high_in, high_ref), (low_in, low_ref))):
-                pltpu.make_async_copy(src.at[at], dst.at[at], in_sems.at[2 * g + n]).start()
         new_ref[odd] = new_a[...]
         new_ref[1 - odd] = new_b[...]
         fix_chained(chain_ref, new_ref, odd, (old_a, old_b), block)
@@ -447,8 +443,6 @@
         replace_rows(tgt, odd, (old_a, old_b), held_ref, block)
         for g in range(steps):
             at = pl.ds(g * span, span)
-            for n, (src, dst) in enumerate(((high_in, high_ref), (low_in, low_ref))):
-                pltpu.make_async_copy(src.at[at], dst.at[at], in_sems.at[2 * g + n]).wait()
             y = dot3(high_ref[at, :], low_ref[at, :], wh[...], wl[...])
             for t in range(group):
                 tile = g * group + t
@@ -492,18 +486,15 @@
         kernel,
         24,
         out_shape=jax.ShapeDtypeStruct((2, rows, CBLK * block), F32),
-        in_specs=[SMEM] * 4 + [HBM] + [VMEM] * 4 + [ANY] * 2 + [VMEM],
+        in_specs=[SMEM] * 4 + [HBM] + [VMEM] * 7,
         out_specs=ANY,
         scratch_shapes=[
             pltpu.VMEM((held.shape[0] + CBLK,) + held.shape[1:], F32),
             pltpu.VMEM((2, 2 * CBLK, block, block), F32),
-            pltpu.VMEM((rows, 4 * block), BF16),
-            pltpu.VMEM((rows, 4 * block), BF16),
             pltpu.VMEM((2, rows, CBLK * block), F32),
             pltpu.VMEM((4 * block, 4 * block), BF16),
             pltpu.VMEM((4 * block, 4 * block), BF16),
             pltpu.SemaphoreType.DMA,
-            pltpu.SemaphoreType.DMA((2 * steps,)),
             pltpu.SemaphoreType.DMA((2 * steps,)),
         ],
         name="update",

time: 220 us -> 220 us (level)
  no operation moved by 1% of the time
where the time goes in v7:
time: 220 us; the launch traced here: 218 us
  waiting for transfers between devices  113 us (51%)
  starting transfers between devices  55.5 us (25%)
  Pallas kernels  36.1 us (16%)
  other arithmetic  9.36 us (4%)
  local copies, waits for them, and re-layouts  2.65 us (1%)
    ppermute x20, waiting for transfers between devices, per_device(): done = [lax.ppermute(x, 'pcol', w[1]) for x, w in zip(values, work)]  72.2 us
    ppermute x20, starting transfers between devices, per_device(): done = [lax.ppermute(x, 'pcol', w[1]) for x, w in zip(values, work)]  42 us
    ppermute x3, waiting for transfers between devices, per_device(): got = lax.ppermute(near, 'pcol', [(i, i ^ step) for i in range(cols_n)])  31.7 us
    pallas_call x2, Pallas kernels, extract(): call(kernel, 12, out_shape=(pltpu.HBM((tiles_n, 2, block, block), F32), p...  10.2 us
    pallas_call x1, Pallas kernels, update(): call(kernel, 24, out_shape=jax.ShapeDtypeStruct((2, rows, CBLK * block),...  9.65 us
    ppermute x8, waiting for transfers between devices, cross(): return lax.ppermute(x, 'prow', [(p, p ^ step) for p in range(rows_n)])  9.44 us
    pallas_call x1, Pallas kernels, panel_factors(): call(kernel, 20, out_shape=(jax.ShapeDtypeStruct((rows, 4 * block), BF16)...  8.13 us
    pallas_call x2, Pallas kernels, pack(): call(kernel, 8, out_shape=tuple((pltpu.VMEM((count,) + one, F32) if strea...  8.13 us
  transfers between devices with their start and end apart: 31, of which 16 were waited for; matrix products, arithmetic and copies ran while one was open for 4% of the time, Pallas kernels for 8%

profile of v7, /device:TPU:29, one launch (start us, length us, event | category | flops | bytes accessed | tf_op | source)
XLA Modules:
  0.0 218.1 jit_solution(6308799198303312373)
XLA Ops:
  0.0 3.3 %pack_streams.1 = (f32[9,2,128,128]{3,2,1,0:T(8,128)S(1)}, s32[128]{0:T(128)}) custom-call(s32[32]{0:T(128)} %bitcast.24, s32[1]{0:T(128)} %bitcast.11.me_ref.col_ref, f32[32,2,128,128]{3,2,1,0:T(8,128)} %bitcast.20), custom_call_target="tpu_custom_call" | custom-call | tf_op jit(solution)/shard_map/pack_streams/pallas_call | solution.py:100
  3.3 2.2 %collective-permute-start.9 = (f32[9,2,128,128]{3,2,1,0:T(8,128)S(1)}, f32[9,2,128,128]{3,2,1,0:T(8,128)S(1)}, u32[]{:S(2)}, u32[]{:S(2)}) collective-permute-start(f32[9,2,128,128]{3,2,1,0:T(8,128)S(1)} %get-tuple-element.62.rest_refs_0_), channel_id=1, source_target_pairs={{2,0},{3,1},{4,2},{5,3},{6,4},{7,5},{10,8},{11,9},{12,10},{13,11},... | collective-permute-start | bytes 3538952 | tf_op jit(solution)/shard_map/ppermute | solution.py:620
  6.8 1.3 collective-permute-start.8
  12.6 19.7 %collective-permute-done.7 = s32[1,128]{1,0:T(1,128)} collective-permute-done((s32[1,128]{1,0:T(1,128)}, s32[1,128]{1,0:T(1,128)}, u32[]{:S(2)}, u32[]{:S(2)}) %collective-permute-start.7) | collective-permute-done | bytes 544 | tf_op jit(solution)/shard_map/ppermute | solution.py:634
  32.2 2.8 %collective-permute-done.8.rest_refs_1_ = f32[9,2,128,128]{3,2,1,0:T(8,128)} collective-permute-done((f32[9,2,128,128]{3,2,1,0:T(8,128)S(1)}, f32[9,2,128,128]{3,2,1,0:T(8,128)}, u32[]{:S(2)}, u32[]{:S(2)}) %collective-permute-start.8) | collective-permute-done | bytes 1179680 | tf_op jit(solution)/shard_map/ppermute | solution.py:620
  35.0 1.3 collective-permute-start.12
  37.1 1.7 collective-permute-start.14
  38.8 2.2 collective-permute-start.15
  42.2 3.5 %collective-permute-start.11 = (s32[2,128]{1,0:T(2,128)}, s32[2,128]{1,0:T(2,128)}, u32[]{:S(2)}, u32[]{:S(2)}) collective-permute-start(s32[2,128]{1,0:T(2,128)} %pad_add_fusion.5), channel_id=1, source_target_pairs={{0,2},{1,3},{2,0},{3,1},{4,6},{5,7},{6,4},{7,5},{8,10},{9,11},{10,... | collective-permute-start | bytes 3080 | tf_op jit(solution)/shard_map/ppermute | solution.py:634
  45.7 4.8 %pack_shifts.1 = (f32[4,2,128,128]{3,2,1,0:T(8,128)}, f32[4,2,128,128]{3,2,1,0:T(8,128)}, f32[4,2,128,128]{3,2,1,0:T(8,128)}, f32[4,2,128,128]{3,2,1,0:T(8,128)}...) custom-call(s32[32]{0:T(128)} %bitcast.25, ...), custom_call_target="tpu_custom_call" | custom-call | tf_op jit(solution)/shard_map/pack_shifts/pallas_call | solution.py:100
  50.5 12.0 %collective-permute-done.11 = s32[2,128]{1,0:T(2,128)} collective-permute-done((s32[2,128]{1,0:T(2,128)}, s32[2,128]{1,0:T(2,128)}, u32[]{:S(2)}, u32[]{:S(2)}) %collective-permute-start.11) | collective-permute-done | bytes 1056 | tf_op jit(solution)/shard_map/ppermute | solution.py:634
  63.3 3.0 %collective-permute-done.15.rest_refs_7_ = f32[9,2,128,128]{3,2,1,0:T(8,128)} collective-permute-done((f32[9,2,128,128]{3,2,1,0:T(8,128)}, f32[9,2,128,128]{3,2,1,0:T(8,128)}, u32[]{:S(2)}, u32[]{:S(2)}) %collective-permute-start.15) | collective-permute-done | bytes 1179680 | tf_op jit(solution)/shard_map/ppermute | solution.py:620
  66.3 2.9 %collective-permute-start.16 = (s32[4,128]{1,0:T(4,128)S(1)}, s32[4,128]{1,0:T(4,128)S(1)}, u32[]{:S(2)}, u32[]{:S(2)}) collective-permute-start(s32[4,128]{1,0:T(4,128)S(1)} %pad_add_fusion.1), channel_id=1, source_target_pairs={{0,4},{1,5},{2,6},{3,7},{4,0},{5,1},{6,2},{7,3},{8,12},{9,13},{10,... | collective-permute-start | bytes 6152 | tf_op jit(solution)/shard_map/ppermute | solution.py:634
  71.7 1.3 collective-permute-start.17
  74.8 6.6 %collective-permute-start.21 = (f32[4,2,128,128]{3,2,1,0:T(8,128)}, f32[4,2,128,128]{3,2,1,0:T(8,128)S(1)}, u32[]{:S(2)}, u32[]{:S(2)}) collective-permute-start(f32[4,2,128,128]{3,2,1,0:T(8,128)} %get-tuple-element.93), channel_id=1, source_target_pairs={{0,4},{1,5},{6,2},{7,3},{8,12},{9,13},{14,10},{15,11},{16,20},{17,... | collective-permute-start | bytes 1572872 | tf_op jit(solution)/shard_map/ppermute | solution.py:620
  81.3 15.3 %collective-permute-done.17.rest_refs_8_ = f32[9,2,128,128]{3,2,1,0:T(8,128)S(1)} collective-permute-done((f32[9,2,128,128]{3,2,1,0:T(8,128)S(1)}, f32[9,2,128,128]{3,2,1,0:T(8,128)S(1)}, u32[]{:S(2)}, u32[]{:S(2)}) %collective-permute-start.17) | collective-permute-done | bytes 1179680 | tf_op jit(solution)/shard_map/ppermute | solution.py:620
  99.1 1.3 collective-permute-start.25
  100.4 7.6 %collective-permute-start.26 = (f32[4,2,128,128]{3,2,1,0:T(8,128)}, f32[4,2,128,128]{3,2,1,0:T(8,128)}, u32[]{:S(2)}, u32[]{:S(2)}) collective-permute-start(f32[4,2,128,128]{3,2,1,0:T(8,128)} %get-tuple-element.86), channel_id=1, source_target_pairs={{0,2},{1,3},{4,6},{5,7},{6,4},{7,5},{8,10},{9,11},{12,14},{13,15},... | collective-permute-start | bytes 1572872 | tf_op jit(solution)/shard_map/ppermute | solution.py:620
  108.0 27.1 %collective-permute-done.22.rest_refs_11_ = f32[9,2,128,128]{3,2,1,0:T(8,128)S(1)} collective-permute-done((f32[9,2,128,128]{3,2,1,0:T(8,128)S(1)}, f32[9,2,128,128]{3,2,1,0:T(8,128)S(1)}, u32[]{:S(2)}, u32[]{:S(2)}) %collective-permute-start.22) | collective-permute-done | bytes 1179680 | tf_op jit(solution)/shard_map/ppermute | solution.py:620
  136.2 5.0 %panel_rows.1 = (f32[32,2,128,128]{3,2,1,0:T(8,128)}, f32[4,128,128]{2,1,0:T(8,128)S(1)}, f32[4,128,128]{2,1,0:T(8,128)S(1)}, f32[4,128,128]{2,1,0:T(8,128)S(1)}) custom-call(s32[8,128]{1,0:T(8,128)S(1)} %pad_add_fusion.near_ref, s32[32]{0:T(128)S(1)} %bitcast.27, s32[256]{0:T(256)S(1)} %get-tuple-element.88.rows_ref, s32[1]{0:T(128)} %bitcast.11.me_ref.col_ref, ...), custom_call_target="tpu_custom_call" | custom-call | tf_op jit(solution)/shard_map/panel_rows/pallas_call | solution.py:245
  141.2 3.8 %collective-permute-start.23 = (f32[4,128,128]{2,1,0:T(8,128)S(1)}, f32[4,128,128]{2,1,0:T(8,128)S(1)}, u32[]{:S(2)}, u32[]{:S(2)}) collective-permute-start(f32[4,128,128]{2,1,0:T(8,128)S(1)} %get-tuple-element.83), channel_id=1, source_target_pairs={{0,8},{8,0},{16,24},{24,16},{1,9},{9,1},{17,25},{25,17},{2,10},{10... | collective-permute-start | bytes 786440 | tf_op jit(solution)/shard_map/ppermute | solution.py:262
  145.0 5.0 %collective-permute-start.28 = (f32[4,2,128,128]{3,2,1,0:T(8,128)}, f32[4,2,128,128]{3,2,1,0:T(8,128)S(1)}, u32[]{:S(2)}, u32[]{:S(2)}) collective-permute-start(f32[4,2,128,128]{3,2,1,0:T(8,128)} %get-tuple-element.92), channel_id=1, source_target_pairs={{0,5},{1,4},{2,7},{3,6},{6,3},{7,2},{8,13},{9,12},{10,15},{11,14},... | collective-permute-start | bytes 1572872 | tf_op jit(solution)/shard_map/ppermute | solution.py:620
  150.0 1.3 collective-permute-start.29
  151.3 1.9 collective-permute-start.30
  153.2 3.1 %collective-permute-start.31 = (f32[4,2,128,128]{3,2,1,0:T(8,128)}, f32[4,2,128,128]{3,2,1,0:T(8,128)S(1)}, u32[]{:S(2)}, u32[]{:S(2)}) collective-permute-start(f32[4,2,128,128]{3,2,1,0:T(8,128)} %get-tuple-element.95), channel_id=1, source_target_pairs={{2,3},{3,2},{4,5},{5,4},{6,7},{7,6},{10,11},{11,10},{12,13},{13,12... | collective-permute-start | bytes 1572872 | tf_op jit(solution)/shard_map/ppermute | solution.py:620
  157.4 7.1 %collective-permute-done.27 = f32[4,128,128]{2,1,0:T(8,128)S(1)} collective-permute-done((f32[4,128,128]{2,1,0:T(8,128)S(1)}, f32[4,128,128]{2,1,0:T(8,128)S(1)}, u32[]{:S(2)}, u32[]{:S(2)}) %collective-permute-start.27) | collective-permute-done | bytes 262176 | tf_op jit(solution)/shard_map/ppermute | solution.py:262
  164.5 9.2 %collective-permute-done.28.rest_refs_19_ = f32[4,2,128,128]{3,2,1,0:T(8,128)S(1)} collective-permute-done((f32[4,2,128,128]{3,2,1,0:T(8,128)}, f32[4,2,128,128]{3,2,1,0:T(8,128)S(1)}, u32[]{:S(2)}, u32[]{:S(2)}) %collective-permute-start.28) | collective-permute-done | bytes 524320 | tf_op jit(solution)/shard_map/ppermute | solution.py:620
  173.7 11.3 %collective-permute-done.29.rest_refs_20_ = f32[4,2,128,128]{3,2,1,0:T(8,128)S(1)} collective-permute-done((f32[4,2,128,128]{3,2,1,0:T(8,128)}, f32[4,2,128,128]{3,2,1,0:T(8,128)S(1)}, u32[]{:S(2)}, u32[]{:S(2)}) %collective-permute-start.29) | collective-permute-done | bytes 524320 | tf_op jit(solution)/shard_map/ppermute | solution.py:620
  185.0 3.0 %collective-permute-done.30.rest_refs_21_ = f32[4,2,128,128]{3,2,1,0:T(8,128)S(1)} collective-permute-done((f32[4,2,128,128]{3,2,1,0:T(8,128)}, f32[4,2,128,128]{3,2,1,0:T(8,128)S(1)}, u32[]{:S(2)}, u32[]{:S(2)}) %collective-permute-start.30) | collective-permute-done | bytes 524320 | tf_op jit(solution)/shard_map/ppermute | solution.py:620
  189.5 5.2 %own_rows.1 = (f32[32,2,128,128]{3,2,1,0:T(8,128)}, f32[4,128,128]{2,1,0:T(8,128)S(1)}, f32[4,128,128]{2,1,0:T(8,128)S(1)}, f32[4,128,128]{2,1,0:T(8,128)S(1)}) custom-call(s32[8,128]{1,0:T(8,128)S(1)} %pad_add_fusion.near_ref, s32[32]{0:T(128)} %bitcast.26, s32[256]{0:T(256)S(1)} %get-tuple-element.88.rows_ref, s32[1]{0:T(128)} %bitcast.11.me_ref.col_ref, ...), custom_call_target="tpu_custom_call" | custom-call | tf_op jit(solution)/shard_map/own_rows/pallas_call | solution.py:245
  198.1 8.1 %panel_factors.1 = (bf16[2048,512]{1,0:T(8,128)(2,1)S(1)}, bf16[2048,512]{1,0:T(8,128)(2,1)S(1)}, f32[128,256]{1,0:T(8,128)S(1)}) custom-call(s32[256]{0:T(256)S(1)} %get-tuple-element.132.tgt, s32[129]{0:T(256)S(1)} %pad_add_fusion.4.chain_ref, s32[1]{0:T(128)} %bitcast.10.row_ref, f32[32,2,128,128]{3,2,1,0:T(8,128)} %get-tuple-element.100.held_in, ...), custom_call_target="tpu_custom_call" | custom-call | tf_op jit(solution)/shard_map/panel_factors/pallas_call | solution.py:401
  208.3 9.6 %update.1 = f32[2,2048,256]{2,1,0:T(8,128)} custom-call(s32[256]{0:T(256)S(1)} %get-tuple-element.132.tgt, s32[129]{0:T(256)S(1)} %pad_add_fusion.4.chain_ref, s32[1]{0:T(128)} %bitcast.10.row_ref, s32[1]{0:T(128)} %bitcast.11.me_ref.col_ref, f32[32,2,128,128]{3,2,1,0:T(8,128)} %get-tuple-element.96.held_in, f32[4,128,128]{2,1,0:T(8,128)S(1)} %get-tuple-element.123.new_a, ...), custom_call_target="tpu_custom_call" | custom-call | tf_op jit(solution)/shard_map/update/pallas_call | solution.py:485
  (98 shorter events, 23.5 us)
Async XLA Ops:
  3.3 67.0 %copy-start = (f32[9,2,128,128]{3,2,1,0:T(8,128)}, f32[9,2,128,128]{3,2,1,0:T(8,128)S(1)}, u32[]{:S(2)}) copy-start(f32[9,2,128,128]{3,2,1,0:T(8,128)S(1)} %get-tuple-element.62.rest_refs_0_) | copy-start | bytes 3538948
  3.3 28.9 %collective-permute-start.9 = (f32[9,2,128,128]{3,2,1,0:T(8,128)S(1)}, f32[9,2,128,128]{3,2,1,0:T(8,128)S(1)}, u32[]{:S(2)}, u32[]{:S(2)}) collective-permute-start(f32[9,2,128,128]{3,2,1,0:T(8,128)S(1)} %get-tuple-element.62.rest_refs_0_), channel_id=1, source_target_pairs={{2,0},{3,1},{4,2},{5,3},{6,4},{7,5},{10,8},{11,9},{12,10},{13,11},... | collective-permute-start | bytes 3538952 | tf_op jit(solution)/shard_map/ppermute | solution.py:620
  5.5 26.7 %collective-permute-start.10 = (f32[9,2,128,128]{3,2,1,0:T(8,128)S(1)}, f32[9,2,128,128]{3,2,1,0:T(8,128)S(1)}, u32[]{:S(2)}, u32[]{:S(2)}) collective-permute-start(f32[9,2,128,128]{3,2,1,0:T(8,128)S(1)} %get-tuple-element.62.rest_refs_0_), channel_id=1, source_target_pairs={{0,1},{1,0},{2,3},{3,2},{4,5},{5,4},{6,7},{7,6},{8,9},{9,8},{10,11... | collective-permute-start | bytes 3538952 | tf_op jit(solution)/shard_map/ppermute | solution.py:620
  6.8 28.2 %collective-permute-start.8 = (f32[9,2,128,128]{3,2,1,0:T(8,128)S(1)}, f32[9,2,128,128]{3,2,1,0:T(8,128)}, u32[]{:S(2)}, u32[]{:S(2)}) collective-permute-start(f32[9,2,128,128]{3,2,1,0:T(8,128)S(1)} %get-tuple-element.62.rest_refs_0_), channel_id=1, source_target_pairs={{0,2},{1,3},{2,4},{3,5},{4,6},{5,7},{8,10},{9,11},{10,12},{11,13},... | collective-permute-start | bytes 3538952 | tf_op jit(solution)/shard_map/ppermute | solution.py:620
  8.1 24.1 %collective-permute-start.7 = (s32[1,128]{1,0:T(1,128)}, s32[1,128]{1,0:T(1,128)}, u32[]{:S(2)}, u32[]{:S(2)}) collective-permute-start(s32[1,128]{1,0:T(1,128)} %bitcast.14), channel_id=1, source_target_pairs={{0,1},{1,0},{2,3},{3,2},{4,5},{5,4},{6,7},{7,6},{8,9},{9,8},{10,11... | collective-permute-start | bytes 1544 | tf_op jit(solution)/shard_map/ppermute | solution.py:634
  35.0 28.2 %collective-permute-start.12 = (f32[9,2,128,128]{3,2,1,0:T(8,128)}, f32[9,2,128,128]{3,2,1,0:T(8,128)S(1)}, u32[]{:S(2)}, u32[]{:S(2)}) collective-permute-start(f32[9,2,128,128]{3,2,1,0:T(8,128)} %collective-permute-done.8.rest_refs_1_), channel_id=1, source_target_pairs={{2,4},{3,5},{4,6},{5,7},{10,12},{11,13},{12,14},{13,15},{18,20},{1... | collective-permute-start | bytes 3538952 | tf_op jit(solution)/shard_map/ppermute | solution.py:620
  36.3 26.9 %collective-permute-start.13 = (f32[9,2,128,128]{3,2,1,0:T(8,128)}, f32[9,2,128,128]{3,2,1,0:T(8,128)S(1)}, u32[]{:S(2)}, u32[]{:S(2)}) collective-permute-start(f32[9,2,128,128]{3,2,1,0:T(8,128)} %copy-done.4), channel_id=1, source_target_pairs={{2,0},{3,1},{4,2},{5,3},{10,8},{11,9},{12,10},{13,11},{18,16},{19,... | collective-permute-start | bytes 3538952 | tf_op jit(solution)/shard_map/ppermute | solution.py:620
  37.1 26.2 %collective-permute-start.14 = (f32[9,2,128,128]{3,2,1,0:T(8,128)}, f32[9,2,128,128]{3,2,1,0:T(8,128)}, u32[]{:S(2)}, u32[]{:S(2)}) collective-permute-start(f32[9,2,128,128]{3,2,1,0:T(8,128)} %copy-done.4), channel_id=1, source_target_pairs={{0,1},{1,0},{8,9},{9,8},{16,17},{17,16},{24,25},{25,24}} | collective-permute-start | bytes 3538952 | tf_op jit(solution)/shard_map/ppermute | solution.py:620
  38.8 27.5 %collective-permute-start.15 = (f32[9,2,128,128]{3,2,1,0:T(8,128)}, f32[9,2,128,128]{3,2,1,0:T(8,128)}, u32[]{:S(2)}, u32[]{:S(2)}) collective-permute-start(f32[9,2,128,128]{3,2,1,0:T(8,128)} %collective-permute-done.8.rest_refs_1_), channel_id=1, source_target_pairs={{2,3},{3,2},{4,5},{5,4},{6,7},{7,6},{10,11},{11,10},{12,13},{13,12... | collective-permute-start | bytes 3538952 | tf_op jit(solution)/shard_map/ppermute | solution.py:620
  42.2 20.4 %collective-permute-start.11 = (s32[2,128]{1,0:T(2,128)}, s32[2,128]{1,0:T(2,128)}, u32[]{:S(2)}, u32[]{:S(2)}) collective-permute-start(s32[2,128]{1,0:T(2,128)} %pad_add_fusion.5), channel_id=1, source_target_pairs={{0,2},{1,3},{2,0},{3,1},{4,6},{5,7},{6,4},{7,5},{8,10},{9,11},{10,... | collective-permute-start | bytes 3080 | tf_op jit(solution)/shard_map/ppermute | solution.py:634
  66.3 4.1 %collective-permute-start.16 = (s32[4,128]{1,0:T(4,128)S(1)}, s32[4,128]{1,0:T(4,128)S(1)}, u32[]{:S(2)}, u32[]{:S(2)}) collective-permute-start(s32[4,128]{1,0:T(4,128)S(1)} %pad_add_fusion.1), channel_id=1, source_target_pairs={{0,4},{1,5},{2,6},{3,7},{4,0},{5,1},{6,2},{7,3},{8,12},{9,13},{10,... | collective-permute-start | bytes 6152 | tf_op jit(solution)/shard_map/ppermute | solution.py:634
  71.7 24.9 %collective-permute-start.17 = (f32[9,2,128,128]{3,2,1,0:T(8,128)S(1)}, f32[9,2,128,128]{3,2,1,0:T(8,128)S(1)}, u32[]{:S(2)}, u32[]{:S(2)}) collective-permute-start(f32[9,2,128,128]{3,2,1,0:T(8,128)S(1)} %collective-permute-done.12.rest_refs_4_), channel_id=1, source_target_pairs={{4,6},{5,7},{12,14},{13,15},{20,22},{21,23},{28,30},{29,31}} | collective-permute-start | bytes 3538952 | tf_op jit(solution)/shard_map/ppermute | solution.py:620
  73.0 23.6 %collective-permute-start.18 = (f32[9,2,128,128]{3,2,1,0:T(8,128)S(1)}, f32[9,2,128,128]{3,2,1,0:T(8,128)S(1)}, u32[]{:S(2)}, u32[]{:S(2)}) collective-permute-start(f32[9,2,128,128]{3,2,1,0:T(8,128)S(1)} %collective-permute-done.13.rest_refs_5_), channel_id=1, source_target_pairs={{2,0},{3,1},{10,8},{11,9},{18,16},{19,17},{26,24},{27,25}} | collective-permute-start | bytes 3538952 | tf_op jit(solution)/shard_map/ppermute | solution.py:620
  73.7 23.8 %collective-permute-start.19 = (f32[9,2,128,128]{3,2,1,0:T(8,128)}, f32[9,2,128,128]{3,2,1,0:T(8,128)S(1)}, u32[]{:S(2)}, u32[]{:S(2)}) collective-permute-start(f32[9,2,128,128]{3,2,1,0:T(8,128)} %select_select_fusion.1), channel_id=1, source_target_pairs={{0,1},{1,0},{2,3},{3,2},{4,5},{5,4},{6,7},{7,6},{8,9},{9,8},{10,11... | collective-permute-start | bytes 3538952 | tf_op jit(solution)/shard_map/ppermute | solution.py:620
  74.1 22.9 %collective-permute-start.20 = (f32[4,2,128,128]{3,2,1,0:T(8,128)}, f32[4,2,128,128]{3,2,1,0:T(8,128)S(1)}, u32[]{:S(2)}, u32[]{:S(2)}) collective-permute-start(f32[4,2,128,128]{3,2,1,0:T(8,128)} %get-tuple-element.85), channel_id=1, source_target_pairs={{2,4},{3,5},{4,2},{5,3},{10,12},{11,13},{12,10},{13,11},{18,20},{1... | collective-permute-start | bytes 1572872 | tf_op jit(solution)/shard_map/ppermute | solution.py:620
  74.8 22.3 %collective-permute-start.21 = (f32[4,2,128,128]{3,2,1,0:T(8,128)}, f32[4,2,128,128]{3,2,1,0:T(8,128)S(1)}, u32[]{:S(2)}, u32[]{:S(2)}) collective-permute-start(f32[4,2,128,128]{3,2,1,0:T(8,128)} %get-tuple-element.93), channel_id=1, source_target_pairs={{0,4},{1,5},{6,2},{7,3},{8,12},{9,13},{14,10},{15,11},{16,20},{17,... | collective-permute-start | bytes 1572872 | tf_op jit(solution)/shard_map/ppermute | solution.py:620
  97.5 37.6 %collective-permute-start.22 = (f32[9,2,128,128]{3,2,1,0:T(8,128)S(1)}, f32[9,2,128,128]{3,2,1,0:T(8,128)S(1)}, u32[]{:S(2)}, u32[]{:S(2)}) collective-permute-start(f32[9,2,128,128]{3,2,1,0:T(8,128)S(1)} %select_select_fusion), channel_id=1, source_target_pairs={{0,1},{1,0},{2,3},{3,2},{4,5},{5,4},{6,7},{7,6},{8,9},{9,8},{10,11... | collective-permute-start | bytes 3538952 | tf_op jit(solution)/shard_map/ppermute | solution.py:620
  97.8 47.2 %collective-permute-start.24 = (f32[4,2,128,128]{3,2,1,0:T(8,128)}, f32[4,2,128,128]{3,2,1,0:T(8,128)}, u32[]{:S(2)}, u32[]{:S(2)}) collective-permute-start(f32[4,2,128,128]{3,2,1,0:T(8,128)} %get-tuple-element.84), channel_id=1, source_target_pairs={{0,7},{1,6},{2,5},{3,4},{4,3},{5,2},{8,15},{9,14},{10,13},{11,12},... | collective-permute-start | bytes 1572872 | tf_op jit(solution)/shard_map/ppermute | solution.py:620
  99.1 45.9 %collective-permute-start.25 = (f32[4,2,128,128]{3,2,1,0:T(8,128)}, f32[4,2,128,128]{3,2,1,0:T(8,128)}, u32[]{:S(2)}, u32[]{:S(2)}) collective-permute-start(f32[4,2,128,128]{3,2,1,0:T(8,128)} %get-tuple-element.85), channel_id=1, source_target_pairs={{0,6},{1,7},{8,14},{9,15},{16,22},{17,23},{24,30},{25,31}} | collective-permute-start | bytes 1572872 | tf_op jit(solution)/shard_map/ppermute | solution.py:620
  100.4 44.6 %collective-permute-start.26 = (f32[4,2,128,128]{3,2,1,0:T(8,128)}, f32[4,2,128,128]{3,2,1,0:T(8,128)}, u32[]{:S(2)}, u32[]{:S(2)}) collective-permute-start(f32[4,2,128,128]{3,2,1,0:T(8,128)} %get-tuple-element.86), channel_id=1, source_target_pairs={{0,2},{1,3},{4,6},{5,7},{6,4},{7,5},{8,10},{9,11},{12,14},{13,15},... | collective-permute-start | bytes 1572872 | tf_op jit(solution)/shard_map/ppermute | solution.py:620
  141.2 15.9 %collective-permute-start.23 = (f32[4,128,128]{2,1,0:T(8,128)S(1)}, f32[4,128,128]{2,1,0:T(8,128)S(1)}, u32[]{:S(2)}, u32[]{:S(2)}) collective-permute-start(f32[4,128,128]{2,1,0:T(8,128)S(1)} %get-tuple-element.83), channel_id=1, source_target_pairs={{0,8},{8,0},{16,24},{24,16},{1,9},{9,1},{17,25},{25,17},{2,10},{10... | collective-permute-start | bytes 786440 | tf_op jit(solution)/shard_map/ppermute | solution.py:262
  145.0 28.7 %collective-permute-start.28 = (f32[4,2,128,128]{3,2,1,0:T(8,128)}, f32[4,2,128,128]{3,2,1,0:T(8,128)S(1)}, u32[]{:S(2)}, u32[]{:S(2)}) collective-permute-start(f32[4,2,128,128]{3,2,1,0:T(8,128)} %get-tuple-element.92), channel_id=1, source_target_pairs={{0,5},{1,4},{2,7},{3,6},{6,3},{7,2},{8,13},{9,12},{10,15},{11,14},... | collective-permute-start | bytes 1572872 | tf_op jit(solution)/shard_map/ppermute | solution.py:620
  150.0 35.0 %collective-permute-start.29 = (f32[4,2,128,128]{3,2,1,0:T(8,128)}, f32[4,2,128,128]{3,2,1,0:T(8,128)S(1)}, u32[]{:S(2)}, u32[]{:S(2)}) collective-permute-start(f32[4,2,128,128]{3,2,1,0:T(8,128)} %get-tuple-element.93), channel_id=1, source_target_pairs={{2,6},{3,7},{10,14},{11,15},{18,22},{19,23},{26,30},{27,31}} | collective-permute-start | bytes 1572872 | tf_op jit(solution)/shard_map/ppermute | solution.py:620
  151.3 36.7 %collective-permute-start.30 = (f32[4,2,128,128]{3,2,1,0:T(8,128)}, f32[4,2,128,128]{3,2,1,0:T(8,128)S(1)}, u32[]{:S(2)}, u32[]{:S(2)}) collective-permute-start(f32[4,2,128,128]{3,2,1,0:T(8,128)} %get-tuple-element.94), channel_id=1, source_target_pairs={{0,3},{1,2},{4,7},{5,6},{6,5},{7,4},{8,11},{9,10},{12,15},{13,14},... | collective-permute-start | bytes 1572872 | tf_op jit(solution)/shard_map/ppermute | solution.py:620
  153.2 34.7 %collective-permute-start.31 = (f32[4,2,128,128]{3,2,1,0:T(8,128)}, f32[4,2,128,128]{3,2,1,0:T(8,128)S(1)}, u32[]{:S(2)}, u32[]{:S(2)}) collective-permute-start(f32[4,2,128,128]{3,2,1,0:T(8,128)} %get-tuple-element.95), channel_id=1, source_target_pairs={{2,3},{3,2},{4,5},{5,4},{6,7},{7,6},{10,11},{11,10},{12,13},{13,12... | collective-permute-start | bytes 1572872 | tf_op jit(solution)/shard_map/ppermute | solution.py:620
  157.1 7.3 %collective-permute-start.27 = (f32[4,128,128]{2,1,0:T(8,128)S(1)}, f32[4,128,128]{2,1,0:T(8,128)S(1)}, u32[]{:S(2)}, u32[]{:S(2)}) collective-permute-start(f32[4,128,128]{2,1,0:T(8,128)S(1)} %get-tuple-element.87), channel_id=1, source_target_pairs={{0,16},{8,24},{16,0},{24,8},{1,17},{9,25},{17,1},{25,9},{2,18},{10... | collective-permute-start | bytes 786440 | tf_op jit(solution)/shard_map/ppermute | solution.py:262
  194.8 2.4 %collective-permute-start.32 = (f32[4,128,128]{2,1,0:T(8,128)S(1)}, f32[4,128,128]{2,1,0:T(8,128)S(1)}, u32[]{:S(2)}, u32[]{:S(2)}) collective-permute-start(f32[4,128,128]{2,1,0:T(8,128)S(1)} %get-tuple-element.98), channel_id=1, source_target_pairs={{0,8},{8,0},{16,24},{24,16},{1,9},{9,1},{17,25},{25,17},{2,10},{10... | collective-permute-start | bytes 786440 | tf_op jit(solution)/shard_map/ppermute | solution.py:262
  196.1 1.6 collective-permute-start.34
  196.2 1.9 collective-permute-start.35
  197.2 9.0 %collective-permute-start.33 = (f32[4,128,128]{2,1,0:T(8,128)S(1)}, f32[4,128,128]{2,1,0:T(8,128)S(1)}, u32[]{:S(2)}, u32[]{:S(2)}) collective-permute-start(f32[4,128,128]{2,1,0:T(8,128)S(1)} %get-tuple-element.109), channel_id=1, source_target_pairs={{0,16},{8,24},{16,0},{24,8},{1,17},{9,25},{17,1},{25,9},{2,18},{10... | collective-permute-start | bytes 786440 | tf_op jit(solution)/shard_map/ppermute | solution.py:262
  206.3 1.6 collective-permute-start.36
  206.6 1.7 collective-permute-start.37
  (18 other events, 447.9 us)
